TPU v7x, 256 devices: a whole 4x4x8 slice. The times are simulated.
256 devices in a mesh: ctx: 32 (over z, y_lo, core), tr: 2 (over y_hi), tc: 4 (over x).
Axes of the slice: x: 4, y: 4 (y_hi: 2, y_lo: 2; y = y_hi * 2 + y_lo), z: 8, core: 2. Of those that a mesh axis runs over, the one named last changes fastest.
Arguments:
- hidden: bfloat16 [16384, 4096], P(('ctx', 'tc'), 'tr'), may hold values from -6 to 6
- norm_gain: float32 [4096], P('tr'), may hold values from 0.25 to 1.75
- seg_lengths: int32 [64], replicated, may hold values from 1 to 512, 16384 in all
- q_weight: bfloat16 [4096, 2048], P('tr', 'tc'), may hold values from -3 to 3
- key_matrix: bfloat16 [4096, 512], P('tr', 'tc'), may hold values from -3 to 3
- value_matrix: bfloat16 [4096, 512], P('tr', 'tc'), may hold values from -0.09375 to 0.09375
- o_weight: bfloat16 [2048, 4096], P('tc', 'tr'), may hold values from -0.125 to 0.125
Outputs:
- layer_out: bfloat16 [16384, 4096], P(('ctx', 'tc'), 'tr')
Inputs may be any that keep to these rules, and one draw needn't show every extreme that they name: `seg_lengths`: entry 0 is the length of the shared prefix, the other entries the candidates' lengths in list order; all sum to 16384, and the longest is exactly 512.
All inputs are finite; a program needn't handle non-finite values.
Results may differ from a plain program's by a relative error of at most 0.01.
Values may be sent and summed in bfloat16 or wider, within the bound.
No kernel may reach another device: no remote copies, remote signals or barrier semaphores. Data moves between devices by JAX's collectives and lax.ppermute only.
A program may use at most 64 MiB of HBM per device.

v0:
```python
import jax
import jax.numpy as jnp
from jax import lax
from jax.sharding import PartitionSpec as P

D = 4096
HEAD_SIZE = 128


epsilon = 1e-05
rope_base = 500000.0
masked_score = -1e30


def from_behind(block, axis, distance):
    devices = range(lax.axis_size(axis))
    route = [(i - distance, i) for i in devices if i - distance in devices]
    return lax.ppermute(block, axis, route)


def rotate(heads_data, positions):
    half_dim = heads_data.shape[-1] // 2
    frequency = rope_base ** (
        -(jnp.arange(half_dim, dtype=jnp.float32) * 2.0 / heads_data.shape[-1])
    )
    angles = positions.astype(jnp.float32)[:, None] * frequency[None, :]
    cosine = jnp.cos(angles)[:, None, :]
    sine_part = jnp.sin(angles)[:, None, :]
    first = heads_data[..., :half_dim]
    second = heads_data[..., half_dim:]
    return jnp.concatenate(
        [first * cosine - second * sine_part, second * cosine + first * sine_part], axis=-1
    )


def segment_of(positions, seg_lengths):
    bounds = jnp.cumsum(seg_lengths)[:-1]
    return jnp.sum((positions[:, None] >= bounds[None, :]).astype(jnp.int32), axis=1)


def per_device(hidden, norm_gain, seg_lengths, q_weight, key_matrix, value_matrix, o_weight):
    wide_hidden = hidden.astype(jnp.float32)
    squares = lax.psum(jnp.sum(wide_hidden * wide_hidden, axis=1), "tr")
    normed_local = (wide_hidden * lax.rsqrt(squares[:, None] / D + epsilon) * norm_gain).astype(
        jnp.bfloat16
    )
    normalized_rows = lax.all_gather(normed_local, "tc", axis=0, tiled=True)
    rows_per_block = normalized_rows.shape[0]
    query_rows = rows_per_block // lax.axis_size("tr")
    query_width = q_weight.shape[1]
    key_width = key_matrix.shape[1]
    summed = lax.psum_scatter(
        jnp.concatenate(
            [
                jnp.dot(normalized_rows, q_weight, preferred_element_type=jnp.float32),
                jnp.dot(normalized_rows, key_matrix, preferred_element_type=jnp.float32),
                jnp.dot(normalized_rows, value_matrix, preferred_element_type=jnp.float32),
            ],
            axis=1,
        ),
        "tr",
        scatter_dimension=0,
        tiled=True,
    )
    cycle_index = lax.axis_index("ctx")
    cycle_size = lax.axis_size("ctx")
    query_pos = (
        cycle_index * rows_per_block
        + lax.axis_index("tr") * query_rows
        + jnp.arange(query_rows, dtype=jnp.int32)
    )
    head_local = query_width // HEAD_SIZE
    key_heads = key_width // HEAD_SIZE
    head_groups = head_local // key_heads
    queries = rotate(summed[:, :query_width].reshape(query_rows, head_local, HEAD_SIZE), query_pos)
    queries = queries.astype(jnp.bfloat16).reshape(query_rows, key_heads, head_groups, HEAD_SIZE)
    key_block_list = rotate(
        summed[:, query_width : query_width + key_width].reshape(query_rows, key_heads, HEAD_SIZE),
        query_pos,
    )
    key_block_list = key_block_list.astype(jnp.bfloat16)
    value_block_list = summed[:, query_width + key_width :].astype(jnp.bfloat16)
    local_pairs = jnp.concatenate(
        [key_block_list.reshape(query_rows, key_width), value_block_list], axis=1
    )
    query_seg = segment_of(query_pos, seg_lengths)
    score_scale = HEAD_SIZE ** (-0.5)

    def attend(softmax_state, key_block, source):
        running_max, weight_sum, accumulated = softmax_state
        key_pos = source * rows_per_block + jnp.arange(rows_per_block, dtype=jnp.int32)
        key_seg = segment_of(key_pos, seg_lengths)
        visible = (key_pos[None, :] <= query_pos[:, None]) & (
            (key_seg[None, :] == 0) | (key_seg[None, :] == query_seg[:, None])
        )
        block_keys = key_block[:, :key_width].reshape(rows_per_block, key_heads, HEAD_SIZE)
        block_values = key_block[:, key_width:].reshape(rows_per_block, key_heads, HEAD_SIZE)
        scores = (
            jnp.einsum("qhgd,khd->hgqk", queries, block_keys, preferred_element_type=jnp.float32)
            * score_scale
        )
        scores = jnp.where(visible, scores, masked_score)
        new_max = jnp.maximum(running_max, jnp.max(scores, axis=-1))
        factor = jnp.exp(running_max - new_max)
        weights = jnp.where(visible, jnp.exp(scores - new_max[..., None]), 0.0)
        weight_sum = weight_sum * factor + jnp.sum(weights, axis=-1)
        accumulated = accumulated * factor[..., None] + jnp.einsum(
            "hgqk,khd->hgqd",
            weights.astype(jnp.bfloat16),
            block_values,
            preferred_element_type=jnp.float32,
        )
        return (new_max, weight_sum, accumulated)

    def maybe_attend(softmax_state, key_block, step_number):
        source = (cycle_index - step_number) % cycle_size
        needed = step_number <= cycle_index
        return lax.cond(
            needed,
            lambda current: attend(current, key_block, source),
            lambda current: current,
            softmax_state,
        )

    state_shape = (key_heads, head_groups, query_rows)
    softmax_state = (
        jnp.full(state_shape, masked_score, jnp.float32),
        jnp.zeros(state_shape, jnp.float32),
        jnp.zeros(state_shape + (HEAD_SIZE,), jnp.float32),
    )
    key_block = lax.all_gather(local_pairs, "tr", axis=0, tiled=True)
    softmax_state = maybe_attend(softmax_state, key_block, 0)

    def advance(step_number, loop_carry):
        moving, current = loop_carry
        moving = from_behind(moving, "ctx", 1)
        return (moving, maybe_attend(current, moving, step_number))

    key_block, softmax_state = lax.fori_loop(1, cycle_size, advance, (key_block, softmax_state))
    running_max, weight_sum, accumulated = softmax_state
    mixed = accumulated / weight_sum[..., None]
    attended = (
        jnp.transpose(mixed, (2, 0, 1, 3)).reshape(query_rows, query_width).astype(jnp.bfloat16)
    )
    partial_terms = jnp.dot(
        lax.all_gather(attended, "tr", axis=0, tiled=True),
        o_weight,
        preferred_element_type=jnp.float32,
    )
    summed_out = lax.psum_scatter(
        partial_terms.astype(jnp.bfloat16), "tc", scatter_dimension=0, tiled=True
    ).astype(jnp.float32)
    return (wide_hidden + summed_out).astype(jnp.bfloat16)


def solution(mesh):
    in_specs = (
        P(("ctx", "tc"), "tr"),
        P("tr"),
        P(),
        P("tr", "tc"),
        P("tr", "tc"),
        P("tr", "tc"),
        P("tc", "tr"),
    )
    out_specs = P(("ctx", "tc"), "tr")
    return jax.shard_map(
        per_device, mesh=mesh, in_specs=in_specs, out_specs=out_specs, check_vma=False
    )
```

profile of v0, /device:TPU:1, one launch (start us, length us, event | category | flops | bytes accessed | tf_op | source)
XLA Modules:
  0.0 513.1 jit_solution(15915280285968883886)
XLA Ops:
  7.9 6.0 %psum.7 = f32[128]{0:T(128)S(1)} all-reduce(f32[128]{0:T(128)S(1)} %fusion.40), channel_id=1, replica_groups=mesh['ctx'=32,'tr'=2,'tc'=4] {'tr'}, use_global_device_ids=true, to_apply=%region_1.0 | all-reduce | flops 128 | bytes 1024 | tf_op jit(solution)/shard_map/psum | solution.py:43
  16.1 37.7 %all-gather.2.cloned.1.call-done = bf16[512,2048]{1,0:T(8,128)(2,1)} async-done(((bf16[128,2048]{1,0:T(8,128)(2,1)}), bf16[512,2048]{1,0:T(8,128)(2,1)}) %all-gather.2.cloned.1.call-update) | async-done | bytes 2097168 | tf_op jit(solution)/shard_map/all_gather | solution.py:47
  62.3 31.2 %reduce-scatter.3.cloned.1.call-done = f32[256,768]{0,1:T(8,128)} async-done(((f32[512,768]{0,1:T(8,128)}), f32[256,768]{0,1:T(8,128)}) %reduce-scatter.3.cloned.1.call-update) | async-done | bytes 786448 | tf_op jit(solution)/shard_map/reduce_scatter | solution.py:52
  100.3 6.5 %all_gather.10 = bf16[512,256]{0,1:T(8,128)(2,1)S(1)} all-gather(bf16[256,256]{0,1:T(8,128)(2,1)S(1)} %pad_maximum_fusion.2), channel_id=1, replica_groups=mesh['ctx'=32,'tr'=2,'tc'=4] {'tr'}, dimensions={0}, use_global_device_ids=true | all-gather | bytes 393216 | tf_op jit(solution)/shard_map/all_gather | solution.py:131
  113.1 279.2 %while.22 = (s32[]{:T(128)}, bf16[512,256]{1,0:T(8,128)(2,1)S(1)}, f32[1,4,256]{2,1,0:T(4,128)S(1)}, f32[1,4,256]{2,1,0:T(4,128)S(1)}, f32[1,4,256,128]{3,2,1,0:...) while((s32[]{:T(128)}, bf16[512,256]{1,0:T(8,128)(2,1)S(1)}, ...), condition=%wide.region_18.19_spmd.clone, body=%wide.region_11.18_spmd.clone.sunk | while | flops 276142272 | bytes 10047672 | solution.py:139
  130.5 7.1 %collective-permute-start = (bf16[512,256]{1,0:T(8,128)(2,1)S(1)}, bf16[512,256]{1,0:T(8,128)(2,1)S(1)}, u32[]{:S(2)}, u32[]{:S(2)}) collective-permute-start(bf16[512,256]{1,0:T(8,128)(2,1)S(1)} %get-tuple-element.707), channel_id=1, source_target_pairs={{0,8},{8,16},{16,24},{24,32},{32,40},{40,48},{48,56},{56,64},{64,7... | collective-permute-start | bytes 786440 | tf_op jit(solution)/shard_map/while/body/eval_jaxpr/ppermute | solution.py:18
  164.9 8.0 %collective-permute-start = (bf16[512,256]{1,0:T(8,128)(2,1)S(1)}, bf16[512,256]{1,0:T(8,128)(2,1)S(1)}, u32[]{:S(2)}, u32[]{:S(2)}) collective-permute-start(bf16[512,256]{1,0:T(8,128)(2,1)S(1)} %get-tuple-element.707), channel_id=1, source_target_pairs={{0,8},{8,16},{16,24},{24,32},{32,40},{40,48},{48,56},{56,64},{64,7... | collective-permute-start | bytes 786440 | tf_op jit(solution)/shard_map/while/body/eval_jaxpr/ppermute | solution.py:18
  184.8 5.3 %collective-permute-start = (bf16[512,256]{1,0:T(8,128)(2,1)S(1)}, bf16[512,256]{1,0:T(8,128)(2,1)S(1)}, u32[]{:S(2)}, u32[]{:S(2)}) collective-permute-start(bf16[512,256]{1,0:T(8,128)(2,1)S(1)} %get-tuple-element.707), channel_id=1, source_target_pairs={{0,8},{8,16},{16,24},{24,32},{32,40},{40,48},{48,56},{56,64},{64,7... | collective-permute-start | bytes 786440 | tf_op jit(solution)/shard_map/while/body/eval_jaxpr/ppermute | solution.py:18
  193.4 5.3 %collective-permute-start = (bf16[512,256]{1,0:T(8,128)(2,1)S(1)}, bf16[512,256]{1,0:T(8,128)(2,1)S(1)}, u32[]{:S(2)}, u32[]{:S(2)}) collective-permute-start(bf16[512,256]{1,0:T(8,128)(2,1)S(1)} %get-tuple-element.707), channel_id=1, source_target_pairs={{0,8},{8,16},{16,24},{24,32},{32,40},{40,48},{48,56},{56,64},{64,7... | collective-permute-start | bytes 786440 | tf_op jit(solution)/shard_map/while/body/eval_jaxpr/ppermute | solution.py:18
  202.1 5.3 %collective-permute-start = (bf16[512,256]{1,0:T(8,128)(2,1)S(1)}, bf16[512,256]{1,0:T(8,128)(2,1)S(1)}, u32[]{:S(2)}, u32[]{:S(2)}) collective-permute-start(bf16[512,256]{1,0:T(8,128)(2,1)S(1)} %get-tuple-element.707), channel_id=1, source_target_pairs={{0,8},{8,16},{16,24},{24,32},{32,40},{40,48},{48,56},{56,64},{64,7... | collective-permute-start | bytes 786440 | tf_op jit(solution)/shard_map/while/body/eval_jaxpr/ppermute | solution.py:18
  210.7 5.3 %collective-permute-start = (bf16[512,256]{1,0:T(8,128)(2,1)S(1)}, bf16[512,256]{1,0:T(8,128)(2,1)S(1)}, u32[]{:S(2)}, u32[]{:S(2)}) collective-permute-start(bf16[512,256]{1,0:T(8,128)(2,1)S(1)} %get-tuple-element.707), channel_id=1, source_target_pairs={{0,8},{8,16},{16,24},{24,32},{32,40},{40,48},{48,56},{56,64},{64,7... | collective-permute-start | bytes 786440 | tf_op jit(solution)/shard_map/while/body/eval_jaxpr/ppermute | solution.py:18
  228.0 5.3 %collective-permute-start = (bf16[512,256]{1,0:T(8,128)(2,1)S(1)}, bf16[512,256]{1,0:T(8,128)(2,1)S(1)}, u32[]{:S(2)}, u32[]{:S(2)}) collective-permute-start(bf16[512,256]{1,0:T(8,128)(2,1)S(1)} %get-tuple-element.707), channel_id=1, source_target_pairs={{0,8},{8,16},{16,24},{24,32},{32,40},{40,48},{48,56},{56,64},{64,7... | collective-permute-start | bytes 786440 | tf_op jit(solution)/shard_map/while/body/eval_jaxpr/ppermute | solution.py:18
  236.6 5.3 %collective-permute-start = (bf16[512,256]{1,0:T(8,128)(2,1)S(1)}, bf16[512,256]{1,0:T(8,128)(2,1)S(1)}, u32[]{:S(2)}, u32[]{:S(2)}) collective-permute-start(bf16[512,256]{1,0:T(8,128)(2,1)S(1)} %get-tuple-element.707), channel_id=1, source_target_pairs={{0,8},{8,16},{16,24},{24,32},{32,40},{40,48},{48,56},{56,64},{64,7... | collective-permute-start | bytes 786440 | tf_op jit(solution)/shard_map/while/body/eval_jaxpr/ppermute | solution.py:18
  253.8 5.3 %collective-permute-start = (bf16[512,256]{1,0:T(8,128)(2,1)S(1)}, bf16[512,256]{1,0:T(8,128)(2,1)S(1)}, u32[]{:S(2)}, u32[]{:S(2)}) collective-permute-start(bf16[512,256]{1,0:T(8,128)(2,1)S(1)} %get-tuple-element.707), channel_id=1, source_target_pairs={{0,8},{8,16},{16,24},{24,32},{32,40},{40,48},{48,56},{56,64},{64,7... | collective-permute-start | bytes 786440 | tf_op jit(solution)/shard_map/while/body/eval_jaxpr/ppermute | solution.py:18
  262.5 5.3 %collective-permute-start = (bf16[512,256]{1,0:T(8,128)(2,1)S(1)}, bf16[512,256]{1,0:T(8,128)(2,1)S(1)}, u32[]{:S(2)}, u32[]{:S(2)}) collective-permute-start(bf16[512,256]{1,0:T(8,128)(2,1)S(1)} %get-tuple-element.707), channel_id=1, source_target_pairs={{0,8},{8,16},{16,24},{24,32},{32,40},{40,48},{48,56},{56,64},{64,7... | collective-permute-start | bytes 786440 | tf_op jit(solution)/shard_map/while/body/eval_jaxpr/ppermute | solution.py:18
  271.1 5.3 %collective-permute-start = (bf16[512,256]{1,0:T(8,128)(2,1)S(1)}, bf16[512,256]{1,0:T(8,128)(2,1)S(1)}, u32[]{:S(2)}, u32[]{:S(2)}) collective-permute-start(bf16[512,256]{1,0:T(8,128)(2,1)S(1)} %get-tuple-element.707), channel_id=1, source_target_pairs={{0,8},{8,16},{16,24},{24,32},{32,40},{40,48},{48,56},{56,64},{64,7... | collective-permute-start | bytes 786440 | tf_op jit(solution)/shard_map/while/body/eval_jaxpr/ppermute | solution.py:18
  279.7 5.3 %collective-permute-start = (bf16[512,256]{1,0:T(8,128)(2,1)S(1)}, bf16[512,256]{1,0:T(8,128)(2,1)S(1)}, u32[]{:S(2)}, u32[]{:S(2)}) collective-permute-start(bf16[512,256]{1,0:T(8,128)(2,1)S(1)} %get-tuple-element.707), channel_id=1, source_target_pairs={{0,8},{8,16},{16,24},{24,32},{32,40},{40,48},{48,56},{56,64},{64,7... | collective-permute-start | bytes 786440 | tf_op jit(solution)/shard_map/while/body/eval_jaxpr/ppermute | solution.py:18
  297.0 5.3 %collective-permute-start = (bf16[512,256]{1,0:T(8,128)(2,1)S(1)}, bf16[512,256]{1,0:T(8,128)(2,1)S(1)}, u32[]{:S(2)}, u32[]{:S(2)}) collective-permute-start(bf16[512,256]{1,0:T(8,128)(2,1)S(1)} %get-tuple-element.707), channel_id=1, source_target_pairs={{0,8},{8,16},{16,24},{24,32},{32,40},{40,48},{48,56},{56,64},{64,7... | collective-permute-start | bytes 786440 | tf_op jit(solution)/shard_map/while/body/eval_jaxpr/ppermute | solution.py:18
  305.6 5.3 %collective-permute-start = (bf16[512,256]{1,0:T(8,128)(2,1)S(1)}, bf16[512,256]{1,0:T(8,128)(2,1)S(1)}, u32[]{:S(2)}, u32[]{:S(2)}) collective-permute-start(bf16[512,256]{1,0:T(8,128)(2,1)S(1)} %get-tuple-element.707), channel_id=1, source_target_pairs={{0,8},{8,16},{16,24},{24,32},{32,40},{40,48},{48,56},{56,64},{64,7... | collective-permute-start | bytes 786440 | tf_op jit(solution)/shard_map/while/body/eval_jaxpr/ppermute | solution.py:18
  357.4 9.1 %collective-permute-start = (bf16[512,256]{1,0:T(8,128)(2,1)S(1)}, bf16[512,256]{1,0:T(8,128)(2,1)S(1)}, u32[]{:S(2)}, u32[]{:S(2)}) collective-permute-start(bf16[512,256]{1,0:T(8,128)(2,1)S(1)} %get-tuple-element.707), channel_id=1, source_target_pairs={{0,8},{8,16},{16,24},{24,32},{32,40},{40,48},{48,56},{56,64},{64,7... | collective-permute-start | bytes 786440 | tf_op jit(solution)/shard_map/while/body/eval_jaxpr/ppermute | solution.py:18
  369.9 6.5 %collective-permute-start = (bf16[512,256]{1,0:T(8,128)(2,1)S(1)}, bf16[512,256]{1,0:T(8,128)(2,1)S(1)}, u32[]{:S(2)}, u32[]{:S(2)}) collective-permute-start(bf16[512,256]{1,0:T(8,128)(2,1)S(1)} %get-tuple-element.707), channel_id=1, source_target_pairs={{0,8},{8,16},{16,24},{24,32},{32,40},{40,48},{48,56},{56,64},{64,7... | collective-permute-start | bytes 786440 | tf_op jit(solution)/shard_map/while/body/eval_jaxpr/ppermute | solution.py:18
  379.7 9.2 %collective-permute-start = (bf16[512,256]{1,0:T(8,128)(2,1)S(1)}, bf16[512,256]{1,0:T(8,128)(2,1)S(1)}, u32[]{:S(2)}, u32[]{:S(2)}) collective-permute-start(bf16[512,256]{1,0:T(8,128)(2,1)S(1)} %get-tuple-element.707), channel_id=1, source_target_pairs={{0,8},{8,16},{16,24},{24,32},{32,40},{40,48},{48,56},{56,64},{64,7... | collective-permute-start | bytes 786440 | tf_op jit(solution)/shard_map/while/body/eval_jaxpr/ppermute | solution.py:18
  392.5 7.4 %all_gather.11 = bf16[512,512]{0,1:T(8,128)(2,1)S(1)} all-gather(bf16[256,512]{0,1:T(8,128)(2,1)S(1)} %bitcast.110), channel_id=1, replica_groups=mesh['ctx'=32,'tr'=2,'tc'=4] {'tr'}, dimensions={0}, use_global_device_ids=true | all-gather | bytes 786432 | tf_op jit(solution)/shard_map/all_gather | solution.py:146
  402.5 102.1 %reduce-scatter.5.cloned.1.call-done = bf16[128,2048]{1,0:T(8,128)(2,1)} async-done(((bf16[512,2048]{1,0:T(8,128)(2,1)}), bf16[128,2048]{1,0:T(8,128)(2,1)}) %reduce-scatter.5.cloned.1.call-update) | async-done | bytes 524304 | tf_op jit(solution)/shard_map/reduce_scatter | solution.py:150
  (220 shorter events, 211.0 us)
Async XLA Ops:
  6.5 47.2 %all-gather.2.cloned.1.call-start = ((), (), s32[]{:S(2)}) async-start(), calls=%async_computation.2 | async-start | bytes 2621440 | tf_op jit(solution)/shard_map/all_gather | solution.py:47
  16.0 77.5 %reduce-scatter.3.cloned.1.call-start = ((), (), s32[]{:S(2)}) async-start(), calls=%async_computation.3 | async-start | bytes 2359296 | tf_op jit(solution)/shard_map/reduce_scatter | solution.py:52
  60.6 444.0 %reduce-scatter.5.cloned.1.call-start = ((), (), s32[]{:S(2)}) async-start(), calls=%async_computation.4 | async-start | bytes 2621440 | tf_op jit(solution)/shard_map/reduce_scatter | solution.py:150
  130.5 10.4 %collective-permute-start = (bf16[512,256]{1,0:T(8,128)(2,1)S(1)}, bf16[512,256]{1,0:T(8,128)(2,1)S(1)}, u32[]{:S(2)}, u32[]{:S(2)}) collective-permute-start(bf16[512,256]{1,0:T(8,128)(2,1)S(1)} %get-tuple-element.707), channel_id=1, source_target_pairs={{0,8},{8,16},{16,24},{24,32},{32,40},{40,48},{48,56},{56,64},{64,7... | collective-permute-start | bytes 786440 | tf_op jit(solution)/shard_map/while/body/eval_jaxpr/ppermute | solution.py:18
  164.9 11.3 %collective-permute-start = (bf16[512,256]{1,0:T(8,128)(2,1)S(1)}, bf16[512,256]{1,0:T(8,128)(2,1)S(1)}, u32[]{:S(2)}, u32[]{:S(2)}) collective-permute-start(bf16[512,256]{1,0:T(8,128)(2,1)S(1)} %get-tuple-element.707), channel_id=1, source_target_pairs={{0,8},{8,16},{16,24},{24,32},{32,40},{40,48},{48,56},{56,64},{64,7... | collective-permute-start | bytes 786440 | tf_op jit(solution)/shard_map/while/body/eval_jaxpr/ppermute | solution.py:18
  176.2 8.6 %collective-permute-start = (bf16[512,256]{1,0:T(8,128)(2,1)S(1)}, bf16[512,256]{1,0:T(8,128)(2,1)S(1)}, u32[]{:S(2)}, u32[]{:S(2)}) collective-permute-start(bf16[512,256]{1,0:T(8,128)(2,1)S(1)} %get-tuple-element.707), channel_id=1, source_target_pairs={{0,8},{8,16},{16,24},{24,32},{32,40},{40,48},{48,56},{56,64},{64,7... | collective-permute-start | bytes 786440 | tf_op jit(solution)/shard_map/while/body/eval_jaxpr/ppermute | solution.py:18
  184.8 8.6 %collective-permute-start = (bf16[512,256]{1,0:T(8,128)(2,1)S(1)}, bf16[512,256]{1,0:T(8,128)(2,1)S(1)}, u32[]{:S(2)}, u32[]{:S(2)}) collective-permute-start(bf16[512,256]{1,0:T(8,128)(2,1)S(1)} %get-tuple-element.707), channel_id=1, source_target_pairs={{0,8},{8,16},{16,24},{24,32},{32,40},{40,48},{48,56},{56,64},{64,7... | collective-permute-start | bytes 786440 | tf_op jit(solution)/shard_map/while/body/eval_jaxpr/ppermute | solution.py:18
  193.4 8.6 %collective-permute-start = (bf16[512,256]{1,0:T(8,128)(2,1)S(1)}, bf16[512,256]{1,0:T(8,128)(2,1)S(1)}, u32[]{:S(2)}, u32[]{:S(2)}) collective-permute-start(bf16[512,256]{1,0:T(8,128)(2,1)S(1)} %get-tuple-element.707), channel_id=1, source_target_pairs={{0,8},{8,16},{16,24},{24,32},{32,40},{40,48},{48,56},{56,64},{64,7... | collective-permute-start | bytes 786440 | tf_op jit(solution)/shard_map/while/body/eval_jaxpr/ppermute | solution.py:18
  202.1 8.6 %collective-permute-start = (bf16[512,256]{1,0:T(8,128)(2,1)S(1)}, bf16[512,256]{1,0:T(8,128)(2,1)S(1)}, u32[]{:S(2)}, u32[]{:S(2)}) collective-permute-start(bf16[512,256]{1,0:T(8,128)(2,1)S(1)} %get-tuple-element.707), channel_id=1, source_target_pairs={{0,8},{8,16},{16,24},{24,32},{32,40},{40,48},{48,56},{56,64},{64,7... | collective-permute-start | bytes 786440 | tf_op jit(solution)/shard_map/while/body/eval_jaxpr/ppermute | solution.py:18
  210.7 8.6 %collective-permute-start = (bf16[512,256]{1,0:T(8,128)(2,1)S(1)}, bf16[512,256]{1,0:T(8,128)(2,1)S(1)}, u32[]{:S(2)}, u32[]{:S(2)}) collective-permute-start(bf16[512,256]{1,0:T(8,128)(2,1)S(1)} %get-tuple-element.707), channel_id=1, source_target_pairs={{0,8},{8,16},{16,24},{24,32},{32,40},{40,48},{48,56},{56,64},{64,7... | collective-permute-start | bytes 786440 | tf_op jit(solution)/shard_map/while/body/eval_jaxpr/ppermute | solution.py:18
  219.3 8.6 %collective-permute-start = (bf16[512,256]{1,0:T(8,128)(2,1)S(1)}, bf16[512,256]{1,0:T(8,128)(2,1)S(1)}, u32[]{:S(2)}, u32[]{:S(2)}) collective-permute-start(bf16[512,256]{1,0:T(8,128)(2,1)S(1)} %get-tuple-element.707), channel_id=1, source_target_pairs={{0,8},{8,16},{16,24},{24,32},{32,40},{40,48},{48,56},{56,64},{64,7... | collective-permute-start | bytes 786440 | tf_op jit(solution)/shard_map/while/body/eval_jaxpr/ppermute | solution.py:18
  228.0 8.6 %collective-permute-start = (bf16[512,256]{1,0:T(8,128)(2,1)S(1)}, bf16[512,256]{1,0:T(8,128)(2,1)S(1)}, u32[]{:S(2)}, u32[]{:S(2)}) collective-permute-start(bf16[512,256]{1,0:T(8,128)(2,1)S(1)} %get-tuple-element.707), channel_id=1, source_target_pairs={{0,8},{8,16},{16,24},{24,32},{32,40},{40,48},{48,56},{56,64},{64,7... | collective-permute-start | bytes 786440 | tf_op jit(solution)/shard_map/while/body/eval_jaxpr/ppermute | solution.py:18
  236.6 8.6 %collective-permute-start = (bf16[512,256]{1,0:T(8,128)(2,1)S(1)}, bf16[512,256]{1,0:T(8,128)(2,1)S(1)}, u32[]{:S(2)}, u32[]{:S(2)}) collective-permute-start(bf16[512,256]{1,0:T(8,128)(2,1)S(1)} %get-tuple-element.707), channel_id=1, source_target_pairs={{0,8},{8,16},{16,24},{24,32},{32,40},{40,48},{48,56},{56,64},{64,7... | collective-permute-start | bytes 786440 | tf_op jit(solution)/shard_map/while/body/eval_jaxpr/ppermute | solution.py:18
  245.2 8.6 %collective-permute-start = (bf16[512,256]{1,0:T(8,128)(2,1)S(1)}, bf16[512,256]{1,0:T(8,128)(2,1)S(1)}, u32[]{:S(2)}, u32[]{:S(2)}) collective-permute-start(bf16[512,256]{1,0:T(8,128)(2,1)S(1)} %get-tuple-element.707), channel_id=1, source_target_pairs={{0,8},{8,16},{16,24},{24,32},{32,40},{40,48},{48,56},{56,64},{64,7... | collective-permute-start | bytes 786440 | tf_op jit(solution)/shard_map/while/body/eval_jaxpr/ppermute | solution.py:18
  253.8 8.6 %collective-permute-start = (bf16[512,256]{1,0:T(8,128)(2,1)S(1)}, bf16[512,256]{1,0:T(8,128)(2,1)S(1)}, u32[]{:S(2)}, u32[]{:S(2)}) collective-permute-start(bf16[512,256]{1,0:T(8,128)(2,1)S(1)} %get-tuple-element.707), channel_id=1, source_target_pairs={{0,8},{8,16},{16,24},{24,32},{32,40},{40,48},{48,56},{56,64},{64,7... | collective-permute-start | bytes 786440 | tf_op jit(solution)/shard_map/while/body/eval_jaxpr/ppermute | solution.py:18
  262.5 8.6 %collective-permute-start = (bf16[512,256]{1,0:T(8,128)(2,1)S(1)}, bf16[512,256]{1,0:T(8,128)(2,1)S(1)}, u32[]{:S(2)}, u32[]{:S(2)}) collective-permute-start(bf16[512,256]{1,0:T(8,128)(2,1)S(1)} %get-tuple-element.707), channel_id=1, source_target_pairs={{0,8},{8,16},{16,24},{24,32},{32,40},{40,48},{48,56},{56,64},{64,7... | collective-permute-start | bytes 786440 | tf_op jit(solution)/shard_map/while/body/eval_jaxpr/ppermute | solution.py:18
  271.1 8.6 %collective-permute-start = (bf16[512,256]{1,0:T(8,128)(2,1)S(1)}, bf16[512,256]{1,0:T(8,128)(2,1)S(1)}, u32[]{:S(2)}, u32[]{:S(2)}) collective-permute-start(bf16[512,256]{1,0:T(8,128)(2,1)S(1)} %get-tuple-element.707), channel_id=1, source_target_pairs={{0,8},{8,16},{16,24},{24,32},{32,40},{40,48},{48,56},{56,64},{64,7... | collective-permute-start | bytes 786440 | tf_op jit(solution)/shard_map/while/body/eval_jaxpr/ppermute | solution.py:18
  279.7 8.6 %collective-permute-start = (bf16[512,256]{1,0:T(8,128)(2,1)S(1)}, bf16[512,256]{1,0:T(8,128)(2,1)S(1)}, u32[]{:S(2)}, u32[]{:S(2)}) collective-permute-start(bf16[512,256]{1,0:T(8,128)(2,1)S(1)} %get-tuple-element.707), channel_id=1, source_target_pairs={{0,8},{8,16},{16,24},{24,32},{32,40},{40,48},{48,56},{56,64},{64,7... | collective-permute-start | bytes 786440 | tf_op jit(solution)/shard_map/while/body/eval_jaxpr/ppermute | solution.py:18
  288.4 8.6 %collective-permute-start = (bf16[512,256]{1,0:T(8,128)(2,1)S(1)}, bf16[512,256]{1,0:T(8,128)(2,1)S(1)}, u32[]{:S(2)}, u32[]{:S(2)}) collective-permute-start(bf16[512,256]{1,0:T(8,128)(2,1)S(1)} %get-tuple-element.707), channel_id=1, source_target_pairs={{0,8},{8,16},{16,24},{24,32},{32,40},{40,48},{48,56},{56,64},{64,7... | collective-permute-start | bytes 786440 | tf_op jit(solution)/shard_map/while/body/eval_jaxpr/ppermute | solution.py:18
  297.0 8.6 %collective-permute-start = (bf16[512,256]{1,0:T(8,128)(2,1)S(1)}, bf16[512,256]{1,0:T(8,128)(2,1)S(1)}, u32[]{:S(2)}, u32[]{:S(2)}) collective-permute-start(bf16[512,256]{1,0:T(8,128)(2,1)S(1)} %get-tuple-element.707), channel_id=1, source_target_pairs={{0,8},{8,16},{16,24},{24,32},{32,40},{40,48},{48,56},{56,64},{64,7... | collective-permute-start | bytes 786440 | tf_op jit(solution)/shard_map/while/body/eval_jaxpr/ppermute | solution.py:18
  322.9 8.6 %collective-permute-start = (bf16[512,256]{1,0:T(8,128)(2,1)S(1)}, bf16[512,256]{1,0:T(8,128)(2,1)S(1)}, u32[]{:S(2)}, u32[]{:S(2)}) collective-permute-start(bf16[512,256]{1,0:T(8,128)(2,1)S(1)} %get-tuple-element.707), channel_id=1, source_target_pairs={{0,8},{8,16},{16,24},{24,32},{32,40},{40,48},{48,56},{56,64},{64,7... | collective-permute-start | bytes 786440 | tf_op jit(solution)/shard_map/while/body/eval_jaxpr/ppermute | solution.py:18
  357.4 12.4 %collective-permute-start = (bf16[512,256]{1,0:T(8,128)(2,1)S(1)}, bf16[512,256]{1,0:T(8,128)(2,1)S(1)}, u32[]{:S(2)}, u32[]{:S(2)}) collective-permute-start(bf16[512,256]{1,0:T(8,128)(2,1)S(1)} %get-tuple-element.707), channel_id=1, source_target_pairs={{0,8},{8,16},{16,24},{24,32},{32,40},{40,48},{48,56},{56,64},{64,7... | collective-permute-start | bytes 786440 | tf_op jit(solution)/shard_map/while/body/eval_jaxpr/ppermute | solution.py:18
  369.9 9.8 %collective-permute-start = (bf16[512,256]{1,0:T(8,128)(2,1)S(1)}, bf16[512,256]{1,0:T(8,128)(2,1)S(1)}, u32[]{:S(2)}, u32[]{:S(2)}) collective-permute-start(bf16[512,256]{1,0:T(8,128)(2,1)S(1)} %get-tuple-element.707), channel_id=1, source_target_pairs={{0,8},{8,16},{16,24},{24,32},{32,40},{40,48},{48,56},{56,64},{64,7... | collective-permute-start | bytes 786440 | tf_op jit(solution)/shard_map/while/body/eval_jaxpr/ppermute | solution.py:18
  379.7 12.5 %collective-permute-start = (bf16[512,256]{1,0:T(8,128)(2,1)S(1)}, bf16[512,256]{1,0:T(8,128)(2,1)S(1)}, u32[]{:S(2)}, u32[]{:S(2)}) collective-permute-start(bf16[512,256]{1,0:T(8,128)(2,1)S(1)} %get-tuple-element.707), channel_id=1, source_target_pairs={{0,8},{8,16},{16,24},{24,32},{32,40},{40,48},{48,56},{56,64},{64,7... | collective-permute-start | bytes 786440 | tf_op jit(solution)/shard_map/while/body/eval_jaxpr/ppermute | solution.py:18
  (19 other events, 662.7 us)
Sparse Core Ops, SparseCore 0:
  16.1 37.5 all-gather.1
  60.8 32.7 reduce-scatter.2
  402.6 101.9 reduce-scatter.4
where the time goes:
time: 514 us; the launch traced here: 513 us
  waiting for transfers between devices  273 us (53%)
  starting transfers between devices  173 us (34%)
  blocking collectives  20 us (4%)
  between operations  13.3 us (3%)
  other arithmetic  13.2 us (3%)
  matrix products  10.6 us (2%)
  local copies, waits for them, and re-layouts  8.94 us (2%)
    ppermute x31, starting transfers between devices, from_behind(): return lax.ppermute(block, axis, route)  173 us
    reduce_scatter x1, waiting for transfers between devices, per_device(): lax.psum_scatter(partial_terms.astype(jnp.bfloat16), 'tc', scatter_dimens...  102 us
    ppermute x31, waiting for transfers between devices, from_behind(): return lax.ppermute(block, axis, route)  102 us
    all_gather x1, waiting for transfers between devices, per_device(): normalized_rows = lax.all_gather(normed_local, 'tc', axis=0, tiled=True)  37.7 us
    reduce_scatter x1, waiting for transfers between devices, per_device(): lax.psum_scatter(jnp.concatenate([jnp.dot(normalized_rows, q_weight, pref...  31.2 us
  transfers between devices with their start and end apart: 34, of which 34 were waited for; matrix products, arithmetic and copies ran while one was open for 0% of the time, Pallas kernels for 0%

commit v1 on v0

v1 whole, which is shorter than its diff:
```python
import functools

import jax
import jax.numpy as jnp
from jax import lax
from jax.experimental import pallas as pl
from jax.experimental.pallas import tpu as pltpu
from jax.sharding import PartitionSpec as P

D = 4096
HEAD = 128
HALF = HEAD // 2
EPS = 1e-05
ROPE_BASE = 500000.0
MASKED = -1e30
ROWS = 128
HEADS = 4
QW = HEADS * HEAD
BLOCK = 512
SCALE = HEAD ** (-0.5)
LOG2E = 1.4426950408889634

f32 = jnp.float32
bf16 = jnp.bfloat16


def spec(memory=pltpu.VMEM):
    return pl.BlockSpec(memory_space=memory)


def rel(x, axis, n, distance):
    return lax.ppermute(x, axis, [((i + distance) % n, i) for i in range(n)])


def qkv_kernel(first, count, *refs):
    idx_ref, power_ref, gain_ref, wq_ref, wk_ref, wv_ref = refs[:6]
    h_refs = refs[6 : 6 + count]
    keep_refs = refs[6 + count : 6 + 2 * count]
    send_refs = refs[6 + 2 * count :]
    tc = idx_ref[0]
    row = lax.broadcasted_iota(jnp.int32, (ROWS, ROWS), 0)
    col = lax.broadcasted_iota(jnp.int32, (ROWS, ROWS), 1)
    gain = gain_ref[...]
    parts = []
    for n in range(count):
        rows = power_ref[pl.ds((tc + first[n]) % 4, 1), :]
        column = jnp.sum(jnp.where(row == col, rows, 0.0), axis=1, keepdims=True)
        scale = lax.rsqrt(column / D + EPS)
        parts.append((h_refs[n][...].astype(f32) * scale * gain).astype(bf16))
    x = parts[0] if count == 1 else jnp.concatenate(parts, axis=0)
    q = jnp.dot(x, wq_ref[...], preferred_element_type=f32)
    k = jnp.dot(x, wk_ref[...], preferred_element_type=f32)
    v = jnp.dot(x, wv_ref[...], preferred_element_type=f32)
    high = k.astype(bf16)
    low = (k - high.astype(f32)).astype(bf16)
    for n in range(count):
        s = slice(n * ROWS, (n + 1) * ROWS)
        keep_refs[n][:, :QW] = q[s]
        keep_refs[n][:, QW : QW + HEAD] = k[s]
        keep_refs[n][:, QW + HEAD :] = v[s]
        send_refs[n][:, :QW] = q[s].astype(bf16)
        send_refs[n][:, QW : QW + HEAD] = v[s].astype(bf16)
        send_refs[n][:, QW + HEAD : QW + 2 * HEAD] = high[s]
        send_refs[n][:, QW + 2 * HEAD :] = low[s]


def qkv(chunks, idx, power, gain, wq, wk, wv, hs):
    n = len(chunks)
    keep = jax.ShapeDtypeStruct((ROWS, QW + 2 * HEAD), f32)
    send = jax.ShapeDtypeStruct((ROWS, QW + 3 * HEAD), bf16)
    out = pl.pallas_call(
        functools.partial(qkv_kernel, chunks, n),
        out_shape=[keep] * n + [send] * n,
        in_specs=[spec(pltpu.SMEM)] + [spec()] * (5 + n),
        out_specs=[spec()] * (2 * n),
        compiler_params=pltpu.CompilerParams(vmem_limit_bytes=24 << 20),
        cost_estimate=pl.CostEstimate(
            flops=2 * n * ROWS * 2048 * 768, bytes_accessed=4 << 20, transcendentals=0
        ),
        name="qkv",
    )(idx, power, gain, wq, wk, wv, *hs)
    return out[:n], out[n:]


def rotated(u, cosine, sine):
    first, second = u[:, :HALF], u[:, HALF:]
    return jnp.concatenate(
        [first * cosine - second * sine, second * cosine + first * sine], axis=1
    )


def rotary_kernel(*refs):
    keep_refs, got_refs = refs[:4], refs[4:8]
    cos_ref, sin_ref, q_ref, kv_ref = refs[8:]
    for r in range(4):
        s = slice(r * ROWS, (r + 1) * ROWS)
        cosine, sine = cos_ref[s, :], sin_ref[s, :]
        keep, got = keep_refs[r], got_refs[r]
        for h in range(HEADS):
            c = slice(h * HEAD, (h + 1) * HEAD)
            u = keep[:, c] + got[:, c].astype(f32)
            q_ref[s, c] = rotated(u, cosine, sine).astype(bf16)
        k = keep[:, QW : QW + HEAD] + (
            got[:, QW + HEAD : QW + 2 * HEAD].astype(f32) + got[:, QW + 2 * HEAD :].astype(f32)
        )
        kv_ref[s, :HEAD] = rotated(k, cosine, sine).astype(bf16)
        v = keep[:, QW + HEAD :] + got[:, QW : QW + HEAD].astype(f32)
        kv_ref[s, HEAD:] = v.astype(bf16)


def rotary(keeps, gots, cosine, sine):
    return pl.pallas_call(
        rotary_kernel,
        out_shape=[
            jax.ShapeDtypeStruct((BLOCK, QW), bf16),
            jax.ShapeDtypeStruct((BLOCK, 2 * HEAD), bf16),
        ],
        in_specs=[spec()] * 10,
        out_specs=[spec()] * 2,
        compiler_params=pltpu.CompilerParams(vmem_limit_bytes=16 << 20),
        cost_estimate=pl.CostEstimate(flops=8 << 20, bytes_accessed=4 << 20, transcendentals=0),
        name="rotary",
    )(*keeps, *gots, cosine, sine)


def attend_kernel(r, idx_ref, len_ref, q_ref, own_ref, prev_ref, pre_a_ref, pre_b_ref, wo_ref, out_ref, bias_ref):
    tc, ctx = idx_ref[0], idx_ref[1]
    a = (tc + r) % 4
    base = ctx * BLOCK + a * ROWS
    lengths = len_ref[...]
    i = lax.broadcasted_iota(jnp.int32, (64, 64), 0)
    j = lax.broadcasted_iota(jnp.int32, (64, 64), 1)
    starts = jnp.sum(jnp.where(i < j, lengths.astype(f32), 0.0), axis=0, keepdims=True)
    pos = base + lax.broadcasted_iota(jnp.int32, (ROWS, 64), 0)
    begun = jnp.where(starts <= pos.astype(f32), starts, 0.0)
    start = jnp.max(begun, axis=1, keepdims=True).astype(jnp.int32)
    prefix = jnp.sum(jnp.where(i[:, :1] < 1, lengths, 0).astype(f32), axis=0, keepdims=True).astype(jnp.int32)
    t = base + lax.broadcasted_iota(jnp.int32, (ROWS, 1), 0)
    low = jnp.where(start >= prefix, start, jnp.int32(1 << 30))
    high = jnp.minimum(prefix, t + 1)
    lane = lax.broadcasted_iota(jnp.int32, (ROWS, ROWS), 1)
    keys, values = [], []
    for n in range(5):
        c = (r + n) % 4
        s = slice(c * ROWS, (c + 1) * ROWS)
        if n == 0:
            chunk = prev_ref[s, :]
        elif n == 4:
            chunk = own_ref[s, :]
        else:
            chunk = jnp.where(a + n < 4, prev_ref[s, :], own_ref[s, :])
        keys.append(chunk[:, :HEAD])
        values.append(chunk[:, HEAD:])
        u = base + (n - 4) * ROWS + lane
        seen = (u >= low) & (u <= t)
        bias_ref[:, n * ROWS : (n + 1) * ROWS] = jnp.where(seen, 0.0, MASKED)
    for c in range(4):
        s = slice(c * ROWS, (c + 1) * ROWS)
        chunk = pre_a_ref[s, :] + pre_b_ref[s, :]
        keys.append(chunk[:, :HEAD])
        values.append(chunk[:, HEAD:])
        u = ((tc + c) % 4) * ROWS + lane
        n = 5 + c
        bias_ref[:, n * ROWS : (n + 1) * ROWS] = jnp.where(u < high, 0.0, MASKED)
    keys = jnp.concatenate(keys, axis=0)
    values = jnp.concatenate(values, axis=0)
    outs = []
    for h in range(HEADS):
        q = q_ref[r * ROWS : (r + 1) * ROWS, h * HEAD : (h + 1) * HEAD]
        s = lax.dot_general(q, keys, (((1,), (1,)), ((), ())), preferred_element_type=f32)
        s = s + bias_ref[...]
        largest = jnp.max(s, axis=1, keepdims=True)
        p = jnp.exp2((s - largest) * (SCALE * LOG2E))
        total = jnp.sum(p, axis=1, keepdims=True)
        mixed = jnp.dot(p.astype(bf16), values, preferred_element_type=f32)
        outs.append((mixed / total).astype(bf16))
    attended = jnp.concatenate(outs, axis=1)
    out_ref[...] = jnp.dot(attended, wo_ref[...], preferred_element_type=f32).astype(out_ref.dtype)


def attend(r, idx, lengths, q, own, prev, pre_a, pre_b, wo, dtype):
    return pl.pallas_call(
        functools.partial(attend_kernel, r),
        out_shape=jax.ShapeDtypeStruct((ROWS, 2048), dtype),
        in_specs=[spec(pltpu.SMEM)] + [spec()] * 7,
        out_specs=spec(),
        scratch_shapes=[pltpu.VMEM((ROWS, 9 * ROWS), f32)],
        compiler_params=pltpu.CompilerParams(vmem_limit_bytes=24 << 20),
        cost_estimate=pl.CostEstimate(
            flops=4 * ROWS * QW * 1152 + 2 * ROWS * QW * 2048,
            bytes_accessed=4 << 20,
            transcendentals=4 * ROWS * 1152,
        ),
        name="attend",
    )(idx, lengths, q, own, prev, pre_a, pre_b, wo)


def ctx_send(x, pairs):
    return lax.ppermute(x, "ctx", pairs)


def per_device(hidden, norm_gain, seg_lengths, wq, wk, wv, wo):
    tc = lax.axis_index("tc")
    ctx = lax.axis_index("ctx")
    idx = jnp.stack([tc, ctx]).astype(jnp.int32)
    h2 = rel(hidden, "tc", 4, 2)
    h1 = rel(hidden, "tc", 4, 1)
    h3 = rel(hidden, "tc", 4, 3)
    wide = hidden.astype(f32)
    mine = jnp.sum(wide * wide, axis=1)
    placed = jnp.where(jnp.arange(4)[:, None] == tc, mine[None, :], 0.0)
    power = lax.psum(placed, ("tr", "tc"))
    gain = norm_gain.reshape(1, -1)
    offset = (jnp.arange(4, dtype=jnp.int32) + tc) % 4 * ROWS
    positions = (ctx * BLOCK + offset[:, None] + jnp.arange(ROWS, dtype=jnp.int32)[None, :]).reshape(-1)
    frequency = ROPE_BASE ** (-(jnp.arange(HALF, dtype=f32) * 2.0 / HEAD))
    angles = positions.astype(f32)[:, None] * frequency[None, :]
    cosine, sine = jnp.cos(angles), jnp.sin(angles)
    lengths = seg_lengths.reshape(-1, 1)

    keeps, gots = [None] * 4, [None] * 4
    for chunks, hs in (((0,), (hidden,)), ((1, 3), (h1, h3)), ((2,), (h2,))):
        kept, sent = qkv(chunks, idx, power, gain, wq, wk, wv, hs)
        for c, k, s in zip(chunks, kept, sent):
            keeps[c] = k
            gots[c] = rel(s, "tr", 2, 1)
    q, kv = rotary(keeps, gots, cosine, sine)
    prev = ctx_send(kv, [(i, i + 1) for i in range(31)])
    at = jnp.where(ctx == 0, kv, jnp.zeros_like(kv))
    got = [ctx_send(kv, [(0, 4 * z)]) for z in (2, 4, 6)]
    at = at + got[0] + got[1] + got[2]
    even = [0, 8, 16, 24]
    got = [ctx_send(at, [(e, e + d) for e in even]) for d in (4, 6, 2)]
    at = at + got[0] + got[1] + got[2]
    other = ctx_send(at, [(2 * i, 2 * i + 1) for i in range(16)])
    parts = {}
    for r in (2, 1, 3, 0):
        parts[r] = attend(r, idx, lengths, q, kv, prev, at, other, wo, f32 if r == 0 else bf16)
    total = parts[0]
    for r in (1, 3, 2):
        total = total + rel(parts[r], "tc", 4, -r).astype(f32)
    return (hidden.astype(f32) + total).astype(bf16)


def solution(mesh):
    in_specs = (
        P(("ctx", "tc"), "tr"),
        P("tr"),
        P(),
        P("tr", "tc"),
        P("tr", "tc"),
        P("tr", "tc"),
        P("tc", "tr"),
    )
    out_specs = P(("ctx", "tc"), "tr")
    return jax.shard_map(
        per_device, mesh=mesh, in_specs=in_specs, out_specs=out_specs, check_vma=False
    )
```

time: 514 us -> 139 us (0.27)
  the two profiles are of different devices: /device:TPU:1 before, /device:TPU:102 now
where the time goes in v1:
time: 139 us
  waiting for transfers between devices  47 us (34%)
  blocking collectives  33.7 us (24%)
  starting transfers between devices  26.6 us (19%)
  Pallas kernels  20.9 us (15%)
  local copies, waits for them, and re-layouts  5.53 us (4%)
  other arithmetic  4.76 us (3%)
    psum x1, blocking collectives, per_device(): power = lax.psum(placed, ('tr', 'tc'))  33.7 us
    ppermute x10, waiting for transfers between devices, rel(): return lax.ppermute(x, axis, [((i + distance) % n, i) for i in range(n)])  27.3 us
    ppermute x8, waiting for transfers between devices, ctx_send(): return lax.ppermute(x, 'ctx', pairs)  19.7 us
    ppermute x10, starting transfers between devices, rel(): return lax.ppermute(x, axis, [((i + distance) % n, i) for i in range(n)])  17.3 us
    pallas_call x4, Pallas kernels, attend(): pl.pallas_call(functools.partial(attend_kernel, r), out_shape=jax.ShapeDt...  12.4 us
    ppermute x8, starting transfers between devices, ctx_send(): return lax.ppermute(x, 'ctx', pairs)  9.29 us
    pallas_call x3, Pallas kernels, qkv(): pl.pallas_call(functools.partial(qkv_kernel, chunks, n), out_shape=[keep]...  6.39 us
    unnamed x24, local copies, waits for them, and re-layouts  5.44 us
  transfers between devices with their start and end apart: 18, of which 7 were waited for; matrix products, arithmetic and copies ran while one was open for 2% of the time, Pallas kernels for 11%

profile of v1, /device:TPU:102, one launch (start us, length us, event | category | flops | bytes accessed | tf_op | source)
XLA Modules:
  0.0 138.7 jit_solution(6069302238380153771)
XLA Ops:
  1.9 2.1 %collective-permute-start.1 = (bf16[128,2048]{1,0:T(8,128)(2,1)}, bf16[128,2048]{1,0:T(8,128)(2,1)}, u32[]{:S(2)}, u32[]{:S(2)}) collective-permute-start(bf16[128,2048]{1,0:T(8,128)(2,1)} %refs_6_.1), channel_id=1, source_target_pairs={{3,0},{0,1},{1,2},{2,3},{7,4},{4,5},{5,6},{6,7},{11,8},{8,9},{9,10... | collective-permute-start | bytes 1572872 | tf_op jit(solution)/shard_map/ppermute | solution.py:32
  5.5 33.7 %psum.7.refs_1_ = f32[4,128]{1,0:T(4,128)S(1)} all-reduce(f32[4,128]{1,0:T(4,128)S(1)} %broadcast_select_fusion), channel_id=1, replica_groups=mesh['ctx'=32,'tr'=2,'tc'=4] {'tr','tc'}, use_global_device_ids=true, to_apply=%region_1.2 | all-reduce | flops 512 | bytes 4096 | tf_op jit(solution)/shard_map/psum | solution.py:212
  39.2 1.6 %copy-done.1 = bf16[2048,512]{1,0:T(8,128)(2,1)S(1)} copy-done((bf16[2048,512]{1,0:T(8,128)(2,1)S(1)}, bf16[2048,512]{1,0:T(8,128)(2,1)}, u32[]{:S(2)}) %copy-start.1) | copy-done | bytes 2097176
  44.6 2.0 %qkv.3 = (f32[128,768]{1,0:T(8,128)S(1)}, bf16[128,896]{1,0:T(8,128)(2,1)}) custom-call(s32[2]{0:T(128)S(1)} %pad_add_fusion.refs_0_.idx_ref, f32[4,128]{1,0:T(4,128)S(1)} %psum.7.refs_1_, f32[1,2048]{1,0:T(1,128)S(1)} %bitcast.6, bf16[2048,512]{1,0:T(8,128)(2,1)S(1)} %copy-done.1, bf16[2048,128]{1,0:T(8,128)(2,1)S(1)} %copy-done.5, ...), custom_call_target="tpu_custom_call" | custom-call | flops 402653184 | bytes 4194304 | tf_op jit(solution)/shard_map/qkv/pallas_call | solution.py:71
  46.7 2.9 %collective-permute-start.3 = (bf16[128,896]{1,0:T(8,128)(2,1)}, bf16[128,896]{1,0:T(8,128)(2,1)}, u32[]{:S(2)}, u32[]{:S(2)}) collective-permute-start(bf16[128,896]{1,0:T(8,128)(2,1)} %get-tuple-element.19), channel_id=1, source_target_pairs={{4,0},{0,4},{5,1},{1,5},{6,2},{2,6},{7,3},{3,7},{12,8},{8,12},{13,... | collective-permute-start | bytes 688136 | tf_op jit(solution)/shard_map/ppermute | solution.py:32
  49.7 1.8 %qkv.5 = (f32[128,768]{1,0:T(8,128)S(1)}, bf16[128,896]{1,0:T(8,128)(2,1)S(1)}) custom-call(s32[2]{0:T(128)S(1)} %pad_add_fusion.refs_0_.idx_ref, f32[4,128]{1,0:T(4,128)S(1)} %psum.7.refs_1_, f32[1,2048]{1,0:T(1,128)S(1)} %bitcast.7, bf16[2048,512]{1,0:T(8,128)(2,1)S(1)} %copy-done.2, bf16[2048,128]{1,0:T(8,128)(2,1)S(1)} %copy-done.6, ...), custom_call_target="tpu_custom_call" | custom-call | flops 402653184 | bytes 4194304 | tf_op jit(solution)/shard_map/qkv/pallas_call | solution.py:71
  52.3 2.5 %qkv.4 = (f32[128,768]{1,0:T(8,128)S(1)}, f32[128,768]{1,0:T(8,128)S(1)}, bf16[128,896]{1,0:T(8,128)(2,1)S(1)}, bf16[128,896]{1,0:T(8,128)(2,1)S(1)}) custom-call(s32[2]{0:T(128)S(1)} %pad_add_fusion.refs_0_.idx_ref, f32[4,128]{1,0:T(4,128)S(1)} %psum.7.refs_1_, f32[1,2048]{1,0:T(1,128)S(1)} %bitcast.8, bf16[2048,512]{1,0:T(8,128)(2,1)S(1)} %copy-done.2, ...), custom_call_target="tpu_custom_call" | custom-call | flops 805306368 | bytes 4194304 | tf_op jit(solution)/shard_map/qkv/pallas_call | solution.py:71
  54.8 2.9 %collective-permute-start.4 = (bf16[128,896]{1,0:T(8,128)(2,1)S(1)}, bf16[128,896]{1,0:T(8,128)(2,1)S(1)}, u32[]{:S(2)}, u32[]{:S(2)}) collective-permute-start(bf16[128,896]{1,0:T(8,128)(2,1)S(1)} %get-tuple-element.20), channel_id=1, source_target_pairs={{4,0},{0,4},{5,1},{1,5},{6,2},{2,6},{7,3},{3,7},{12,8},{8,12},{13,... | collective-permute-start | bytes 688136 | tf_op jit(solution)/shard_map/ppermute | solution.py:32
  59.4 2.2 %collective-permute-done.5.refs_6_ = bf16[128,896]{1,0:T(8,128)(2,1)S(1)} collective-permute-done((bf16[128,896]{1,0:T(8,128)(2,1)S(1)}, bf16[128,896]{1,0:T(8,128)(2,1)S(1)}, u32[]{:S(2)}, u32[]{:S(2)}) %collective-permute-start.5) | collective-permute-done | bytes 229408 | tf_op jit(solution)/shard_map/ppermute | solution.py:32
  61.6 4.9 %collective-permute-done.4.refs_5_ = bf16[128,896]{1,0:T(8,128)(2,1)S(1)} collective-permute-done((bf16[128,896]{1,0:T(8,128)(2,1)S(1)}, bf16[128,896]{1,0:T(8,128)(2,1)S(1)}, u32[]{:S(2)}, u32[]{:S(2)}) %collective-permute-start.4) | collective-permute-done | bytes 229408 | tf_op jit(solution)/shard_map/ppermute | solution.py:32
  66.5 2.6 %collective-permute-done.6.refs_7_ = bf16[128,896]{1,0:T(8,128)(2,1)S(1)} collective-permute-done((bf16[128,896]{1,0:T(8,128)(2,1)S(1)}, bf16[128,896]{1,0:T(8,128)(2,1)S(1)}, u32[]{:S(2)}, u32[]{:S(2)}) %collective-permute-start.6) | collective-permute-done | bytes 229408 | tf_op jit(solution)/shard_map/ppermute | solution.py:32
  69.1 2.2 %rotary.1 = (bf16[512,512]{1,0:T(8,128)(2,1)S(1)}, bf16[512,256]{1,0:T(8,128)(2,1)S(1)}) custom-call(f32[128,768]{1,0:T(8,128)S(1)} %get-tuple-element.15.refs_0_, f32[128,768]{1,0:T(8,128)S(1)} %get-tuple-element.16.refs_1_, f32[128,768]{1,0:T(8,128)S(1)} %get-tuple-element.17.refs_2_, f32[128,768]{1,0:T(8,128)S(1)} %get-tuple-element.18.refs_3_, ...), custom_call_target="tpu_custom_call" | custom-call | flops 8388608 | bytes 4194304 | tf_op jit(solution)/shard_map/rotary/pallas_call | solution.py:112
  72.7 1.4 collective-permute-start.8
  77.7 1.9 %collective-permute-start.7 = (bf16[512,256]{1,0:T(8,128)(2,1)S(1)}, bf16[512,256]{1,0:T(8,128)(2,1)S(1)}, u32[]{:S(2)}, u32[]{:S(2)}) collective-permute-start(bf16[512,256]{1,0:T(8,128)(2,1)S(1)} %get-tuple-element.24.own_ref), channel_id=1, source_target_pairs={{0,8},{8,16},{16,24},{24,32},{32,40},{40,48},{48,56},{56,64},{64,7... | collective-permute-start | bytes 786440 | tf_op jit(solution)/shard_map/ppermute | solution.py:199
  79.7 19.2 %collective-permute-done.11 = bf16[512,256]{1,0:T(8,128)(2,1)S(1)} collective-permute-done((bf16[512,256]{1,0:T(8,128)(2,1)S(1)}, bf16[512,256]{1,0:T(8,128)(2,1)S(1)}, u32[]{:S(2)}, u32[]{:S(2)}) %collective-permute-start.11) | collective-permute-done | bytes 262176 | tf_op jit(solution)/shard_map/ppermute | solution.py:199
  98.9 2.0 %collective-permute-start.14 = (bf16[512,256]{1,0:T(8,128)(2,1)S(1)}, bf16[512,256]{1,0:T(8,128)(2,1)}, u32[]{:S(2)}, u32[]{:S(2)}) collective-permute-start(bf16[512,256]{1,0:T(8,128)(2,1)S(1)} %add_add_fusion.pre_a_ref), channel_id=1, source_target_pairs={{0,8},{16,24},{32,40},{48,56},{64,72},{80,88},{96,104},{112,120},{... | collective-permute-start | bytes 786440 | tf_op jit(solution)/shard_map/ppermute | solution.py:199
  101.5 3.1 %attend.5 = bf16[128,2048]{1,0:T(8,128)(2,1)S(1)} custom-call(s32[2]{0:T(128)S(1)} %pad_add_fusion.refs_0_.idx_ref, s32[64,1]{1,0:T(8,128)S(1)} %copy.8.len_ref, bf16[512,512]{1,0:T(8,128)(2,1)S(1)} %get-tuple-element.23.q_ref, bf16[512,256]{1,0:T(8,128)(2,1)S(1)} %get-tuple-element.24.own_ref, bf16[512,256]{1,0:T(8,128)(2,1)S(1)} %collective-permute-done.7.prev_ref, ...), custom_call_target="tpu_custom_call" | custom-call | flops 570425344 | bytes 4194304 | tf_op jit(solution)/shard_map/attend/pallas_call | solution.py:182
  104.6 3.4 %collective-permute-start.15 = (bf16[128,2048]{1,0:T(8,128)(2,1)S(1)}, bf16[128,2048]{1,0:T(8,128)(2,1)S(1)}, u32[]{:S(2)}, u32[]{:S(2)}) collective-permute-start(bf16[128,2048]{1,0:T(8,128)(2,1)S(1)} %attend.5), channel_id=1, source_target_pairs={{3,0},{0,1},{1,2},{2,3},{7,4},{4,5},{5,6},{6,7},{11,8},{8,9},{9,10... | collective-permute-start | bytes 1572872 | tf_op jit(solution)/shard_map/ppermute | solution.py:32
  108.0 3.1 %attend.6 = bf16[128,2048]{1,0:T(8,128)(2,1)S(1)} custom-call(s32[2]{0:T(128)S(1)} %pad_add_fusion.refs_0_.idx_ref, s32[64,1]{1,0:T(8,128)S(1)} %copy.8.len_ref, bf16[512,512]{1,0:T(8,128)(2,1)S(1)} %get-tuple-element.23.q_ref, bf16[512,256]{1,0:T(8,128)(2,1)S(1)} %get-tuple-element.24.own_ref, bf16[512,256]{1,0:T(8,128)(2,1)S(1)} %collective-permute-done.7.prev_ref, ...), custom_call_target="tpu_custom_call" | custom-call | flops 570425344 | bytes 4194304 | tf_op jit(solution)/shard_map/attend/pallas_call | solution.py:182
  111.2 3.1 %attend.7 = bf16[128,2048]{1,0:T(8,128)(2,1)S(1)} custom-call(s32[2]{0:T(128)S(1)} %pad_add_fusion.refs_0_.idx_ref, s32[64,1]{1,0:T(8,128)S(1)} %copy.8.len_ref, bf16[512,512]{1,0:T(8,128)(2,1)S(1)} %get-tuple-element.23.q_ref, bf16[512,256]{1,0:T(8,128)(2,1)S(1)} %get-tuple-element.24.own_ref, bf16[512,256]{1,0:T(8,128)(2,1)S(1)} %collective-permute-done.7.prev_ref, ...), custom_call_target="tpu_custom_call" | custom-call | flops 570425344 | bytes 4194304 | tf_op jit(solution)/shard_map/attend/pallas_call | solution.py:182
  114.3 2.5 %collective-permute-start.17 = (bf16[128,2048]{1,0:T(8,128)(2,1)S(1)}, bf16[128,2048]{1,0:T(8,128)(2,1)S(1)}, u32[]{:S(2)}, u32[]{:S(2)}) collective-permute-start(bf16[128,2048]{1,0:T(8,128)(2,1)S(1)} %attend.7), channel_id=1, source_target_pairs={{2,0},{3,1},{0,2},{1,3},{6,4},{7,5},{4,6},{5,7},{10,8},{11,9},{8,1... | collective-permute-start | bytes 1572872 | tf_op jit(solution)/shard_map/ppermute | solution.py:32
  116.8 3.1 %attend.4 = f32[128,2048]{1,0:T(8,128)S(1)} custom-call(s32[2]{0:T(128)S(1)} %pad_add_fusion.refs_0_.idx_ref, s32[64,1]{1,0:T(8,128)S(1)} %copy.8.len_ref, bf16[512,512]{1,0:T(8,128)(2,1)S(1)} %get-tuple-element.23.q_ref, bf16[512,256]{1,0:T(8,128)(2,1)S(1)} %get-tuple-element.24.own_ref, bf16[512,256]{1,0:T(8,128)(2,1)S(1)} %collective-permute-done.7.prev_ref, ...), custom_call_target="tpu_custom_call" | custom-call | flops 570425344 | bytes 4194304 | tf_op jit(solution)/shard_map/attend/pallas_call | solution.py:182
  119.9 11.0 %collective-permute-done.15 = bf16[128,2048]{1,0:T(8,128)(2,1)S(1)} collective-permute-done((bf16[128,2048]{1,0:T(8,128)(2,1)S(1)}, bf16[128,2048]{1,0:T(8,128)(2,1)S(1)}, u32[]{:S(2)}, u32[]{:S(2)}) %collective-permute-start.15) | collective-permute-done | bytes 524320 | tf_op jit(solution)/shard_map/ppermute | solution.py:32
  130.9 6.6 %collective-permute-done.16 = bf16[128,2048]{1,0:T(8,128)(2,1)S(1)} collective-permute-done((bf16[128,2048]{1,0:T(8,128)(2,1)S(1)}, bf16[128,2048]{1,0:T(8,128)(2,1)S(1)}, u32[]{:S(2)}, u32[]{:S(2)}) %collective-permute-start.16) | collective-permute-done | bytes 524320 | tf_op jit(solution)/shard_map/ppermute | solution.py:32
  (57 shorter events, 16.7 us)
Async XLA Ops:
  0.0 52.3 %collective-permute-start = (bf16[128,2048]{1,0:T(8,128)(2,1)}, bf16[128,2048]{1,0:T(8,128)(2,1)}, u32[]{:S(2)}, u32[]{:S(2)}) collective-permute-start(bf16[128,2048]{1,0:T(8,128)(2,1)} %refs_6_.1), channel_id=1, source_target_pairs={{1,0},{2,1},{3,2},{0,3},{5,4},{6,5},{7,6},{4,7},{9,8},{10,9},{11,1... | collective-permute-start | bytes 1572872 | tf_op jit(solution)/shard_map/ppermute | solution.py:32
  0.8 48.8 %collective-permute-start.2 = (bf16[128,2048]{1,0:T(8,128)(2,1)}, bf16[128,2048]{1,0:T(8,128)(2,1)}, u32[]{:S(2)}, u32[]{:S(2)}) collective-permute-start(bf16[128,2048]{1,0:T(8,128)(2,1)} %refs_6_.1), channel_id=1, source_target_pairs={{2,0},{3,1},{0,2},{1,3},{6,4},{7,5},{4,6},{5,7},{10,8},{11,9},{8,1... | collective-permute-start | bytes 1572872 | tf_op jit(solution)/shard_map/ppermute | solution.py:32
  1.9 50.3 %collective-permute-start.1 = (bf16[128,2048]{1,0:T(8,128)(2,1)}, bf16[128,2048]{1,0:T(8,128)(2,1)}, u32[]{:S(2)}, u32[]{:S(2)}) collective-permute-start(bf16[128,2048]{1,0:T(8,128)(2,1)} %refs_6_.1), channel_id=1, source_target_pairs={{3,0},{0,1},{1,2},{2,3},{7,4},{4,5},{5,6},{6,7},{11,8},{8,9},{9,10... | collective-permute-start | bytes 1572872 | tf_op jit(solution)/shard_map/ppermute | solution.py:32
  4.0 45.6 %copy-start.6 = (bf16[2048,128]{1,0:T(8,128)(2,1)S(1)}, bf16[2048,128]{1,0:T(8,128)(2,1)}, u32[]{:S(2)}) copy-start(bf16[2048,128]{1,0:T(8,128)(2,1)} %refs_4_.5) | copy-start | bytes 1572868
  4.0 45.6 %copy-start.10 = (f32[2048]{0:T(1024)S(1)}, f32[2048]{0:T(1024)}, u32[]{:S(2)}) copy-start(f32[2048]{0:T(1024)} %param.8) | copy-start | bytes 24580
  44.6 5.0 %copy-start.8 = (bf16[2048,128]{1,0:T(8,128)(2,1)S(1)}, bf16[2048,128]{1,0:T(8,128)(2,1)}, u32[]{:S(2)}) copy-start(bf16[2048,128]{1,0:T(8,128)(2,1)} %refs_5_.5) | copy-start | bytes 1572868
  46.7 12.8 %collective-permute-start.3 = (bf16[128,896]{1,0:T(8,128)(2,1)}, bf16[128,896]{1,0:T(8,128)(2,1)}, u32[]{:S(2)}, u32[]{:S(2)}) collective-permute-start(bf16[128,896]{1,0:T(8,128)(2,1)} %get-tuple-element.19), channel_id=1, source_target_pairs={{4,0},{0,4},{5,1},{1,5},{6,2},{2,6},{7,3},{3,7},{12,8},{8,12},{13,... | collective-permute-start | bytes 688136 | tf_op jit(solution)/shard_map/ppermute | solution.py:32
  51.5 10.1 %collective-permute-start.5 = (bf16[128,896]{1,0:T(8,128)(2,1)S(1)}, bf16[128,896]{1,0:T(8,128)(2,1)S(1)}, u32[]{:S(2)}, u32[]{:S(2)}) collective-permute-start(bf16[128,896]{1,0:T(8,128)(2,1)S(1)} %get-tuple-element.21), channel_id=1, source_target_pairs={{4,0},{0,4},{5,1},{1,5},{6,2},{2,6},{7,3},{3,7},{12,8},{8,12},{13,... | collective-permute-start | bytes 688136 | tf_op jit(solution)/shard_map/ppermute | solution.py:32
  54.8 11.7 %collective-permute-start.4 = (bf16[128,896]{1,0:T(8,128)(2,1)S(1)}, bf16[128,896]{1,0:T(8,128)(2,1)S(1)}, u32[]{:S(2)}, u32[]{:S(2)}) collective-permute-start(bf16[128,896]{1,0:T(8,128)(2,1)S(1)} %get-tuple-element.20), channel_id=1, source_target_pairs={{4,0},{0,4},{5,1},{1,5},{6,2},{2,6},{7,3},{3,7},{12,8},{8,12},{13,... | collective-permute-start | bytes 688136 | tf_op jit(solution)/shard_map/ppermute | solution.py:32
  57.8 11.4 %collective-permute-start.6 = (bf16[128,896]{1,0:T(8,128)(2,1)S(1)}, bf16[128,896]{1,0:T(8,128)(2,1)S(1)}, u32[]{:S(2)}, u32[]{:S(2)}) collective-permute-start(bf16[128,896]{1,0:T(8,128)(2,1)S(1)} %get-tuple-element.22), channel_id=1, source_target_pairs={{4,0},{0,4},{5,1},{1,5},{6,2},{2,6},{7,3},{3,7},{12,8},{8,12},{13,... | collective-permute-start | bytes 688136 | tf_op jit(solution)/shard_map/ppermute | solution.py:32
  69.1 31.8 %copy-start.11 = (s32[64]{0:T(128)S(1)}, s32[64]{0:T(128)}, u32[]{:S(2)}) copy-start(s32[64]{0:T(128)} %param.9) | copy-start | bytes 772
  69.1 32.3 %copy-start = (bf16[512,2048]{1,0:T(8,128)(2,1)S(1)}, bf16[512,2048]{1,0:T(8,128)(2,1)}, u32[]{:S(2)}) copy-start(bf16[512,2048]{1,0:T(8,128)(2,1)} %wo_ref.7) | copy-start | bytes 6291460
  71.3 2.7 %collective-permute-start.10 = (bf16[512,256]{1,0:T(8,128)(2,1)S(1)}, bf16[512,256]{1,0:T(8,128)(2,1)S(1)}, u32[]{:S(2)}, u32[]{:S(2)}) collective-permute-start(bf16[512,256]{1,0:T(8,128)(2,1)S(1)} %get-tuple-element.24.own_ref), channel_id=1, source_target_pairs={{0,192},{1,193},{2,194},{3,195},{4,196},{5,197},{6,198},{7,199}} | collective-permute-start | bytes 786440 | tf_op jit(solution)/shard_map/ppermute | solution.py:199
  72.0 2.1 %collective-permute-start.9 = (bf16[512,256]{1,0:T(8,128)(2,1)S(1)}, bf16[512,256]{1,0:T(8,128)(2,1)S(1)}, u32[]{:S(2)}, u32[]{:S(2)}) collective-permute-start(bf16[512,256]{1,0:T(8,128)(2,1)S(1)} %get-tuple-element.24.own_ref), channel_id=1, source_target_pairs={{0,128},{1,129},{2,130},{3,131},{4,132},{5,133},{6,134},{7,135}} | collective-permute-start | bytes 786440 | tf_op jit(solution)/shard_map/ppermute | solution.py:199
  72.7 1.4 collective-permute-start.8
  75.1 4.6 %collective-permute-start.13 = (bf16[512,256]{1,0:T(8,128)(2,1)S(1)}, bf16[512,256]{1,0:T(8,128)(2,1)S(1)}, u32[]{:S(2)}, u32[]{:S(2)}) collective-permute-start(bf16[512,256]{1,0:T(8,128)(2,1)S(1)} %add_add_fusion.1), channel_id=1, source_target_pairs={{0,16},{64,80},{128,144},{192,208},{1,17},{65,81},{129,145},{193,2... | collective-permute-start | bytes 786440 | tf_op jit(solution)/shard_map/ppermute | solution.py:199
  75.8 3.9 %collective-permute-start.12 = (bf16[512,256]{1,0:T(8,128)(2,1)S(1)}, bf16[512,256]{1,0:T(8,128)(2,1)S(1)}, u32[]{:S(2)}, u32[]{:S(2)}) collective-permute-start(bf16[512,256]{1,0:T(8,128)(2,1)S(1)} %add_add_fusion.1), channel_id=1, source_target_pairs={{0,48},{64,112},{128,176},{192,240},{1,49},{65,113},{129,177},{193... | collective-permute-start | bytes 786440 | tf_op jit(solution)/shard_map/ppermute | solution.py:199
  76.4 22.4 %collective-permute-start.11 = (bf16[512,256]{1,0:T(8,128)(2,1)S(1)}, bf16[512,256]{1,0:T(8,128)(2,1)S(1)}, u32[]{:S(2)}, u32[]{:S(2)}) collective-permute-start(bf16[512,256]{1,0:T(8,128)(2,1)S(1)} %add_add_fusion.1), channel_id=1, source_target_pairs={{0,32},{64,96},{128,160},{192,224},{1,33},{65,97},{129,161},{193,2... | collective-permute-start | bytes 786440 | tf_op jit(solution)/shard_map/ppermute | solution.py:199
  77.7 23.3 %collective-permute-start.7 = (bf16[512,256]{1,0:T(8,128)(2,1)S(1)}, bf16[512,256]{1,0:T(8,128)(2,1)S(1)}, u32[]{:S(2)}, u32[]{:S(2)}) collective-permute-start(bf16[512,256]{1,0:T(8,128)(2,1)S(1)} %get-tuple-element.24.own_ref), channel_id=1, source_target_pairs={{0,8},{8,16},{16,24},{24,32},{32,40},{40,48},{48,56},{56,64},{64,7... | collective-permute-start | bytes 786440 | tf_op jit(solution)/shard_map/ppermute | solution.py:199
  98.9 2.6 %collective-permute-start.14 = (bf16[512,256]{1,0:T(8,128)(2,1)S(1)}, bf16[512,256]{1,0:T(8,128)(2,1)}, u32[]{:S(2)}, u32[]{:S(2)}) collective-permute-start(bf16[512,256]{1,0:T(8,128)(2,1)S(1)} %add_add_fusion.pre_a_ref), channel_id=1, source_target_pairs={{0,8},{16,24},{32,40},{48,56},{64,72},{80,88},{96,104},{112,120},{... | collective-permute-start | bytes 786440 | tf_op jit(solution)/shard_map/ppermute | solution.py:199
  104.6 26.3 %collective-permute-start.15 = (bf16[128,2048]{1,0:T(8,128)(2,1)S(1)}, bf16[128,2048]{1,0:T(8,128)(2,1)S(1)}, u32[]{:S(2)}, u32[]{:S(2)}) collective-permute-start(bf16[128,2048]{1,0:T(8,128)(2,1)S(1)} %attend.5), channel_id=1, source_target_pairs={{3,0},{0,1},{1,2},{2,3},{7,4},{4,5},{5,6},{6,7},{11,8},{8,9},{9,10... | collective-permute-start | bytes 1572872 | tf_op jit(solution)/shard_map/ppermute | solution.py:32
  111.1 26.4 %collective-permute-start.16 = (bf16[128,2048]{1,0:T(8,128)(2,1)S(1)}, bf16[128,2048]{1,0:T(8,128)(2,1)S(1)}, u32[]{:S(2)}, u32[]{:S(2)}) collective-permute-start(bf16[128,2048]{1,0:T(8,128)(2,1)S(1)} %attend.6), channel_id=1, source_target_pairs={{1,0},{2,1},{3,2},{0,3},{5,4},{6,5},{7,6},{4,7},{9,8},{10,9},{11,1... | collective-permute-start | bytes 1572872 | tf_op jit(solution)/shard_map/ppermute | solution.py:32
  114.3 23.2 %copy-start.4 = (bf16[128,2048]{1,0:T(8,128)(2,1)S(1)}, bf16[128,2048]{1,0:T(8,128)(2,1)}, u32[]{:S(2)}) copy-start(bf16[128,2048]{1,0:T(8,128)(2,1)} %refs_6_.1) | copy-start | bytes 1572868
  114.3 23.2 %collective-permute-start.17 = (bf16[128,2048]{1,0:T(8,128)(2,1)S(1)}, bf16[128,2048]{1,0:T(8,128)(2,1)S(1)}, u32[]{:S(2)}, u32[]{:S(2)}) collective-permute-start(bf16[128,2048]{1,0:T(8,128)(2,1)S(1)} %attend.7), channel_id=1, source_target_pairs={{2,0},{3,1},{0,2},{1,3},{6,4},{7,5},{4,6},{5,7},{10,8},{11,9},{8,1... | collective-permute-start | bytes 1572872 | tf_op jit(solution)/shard_map/ppermute | solution.py:32
  (6 other events, 10.4 us)

commit v2 on v1

v2 whole, which is shorter than its diff:
```python
import functools

import jax
import jax.numpy as jnp
from jax import lax
from jax.experimental import pallas as pl
from jax.experimental.pallas import tpu as pltpu
from jax.sharding import PartitionSpec as P

D = 4096
HEAD = 128
HALF = HEAD // 2
EPS = 1e-05
ROPE_BASE = 500000.0
MASKED = -1e30
ROWS = 128
HEADS = 4
QW = HEADS * HEAD
BLOCK = 512
SCALE = HEAD ** (-0.5)
EXPONENT = SCALE * 1.4426950408889634

f32 = jnp.float32
bf16 = jnp.bfloat16


def spec(memory=pltpu.VMEM):
    return pl.BlockSpec(memory_space=memory)


def rel(x, axis, n, distance):
    return lax.ppermute(x, axis, [((i + distance) % n, i) for i in range(n)])


def call(kernel, name, out_shape, ins, smem=0, stay=(), scratch=(), vmem=24, flops=0, exps=0):
    many = isinstance(out_shape, list)
    where = [pltpu.SMEM] * smem + [pltpu.HBM if n in stay else pltpu.VMEM for n in range(smem, len(ins))]
    return pl.pallas_call(
        kernel,
        out_shape=out_shape,
        in_specs=[spec(w) for w in where],
        out_specs=[spec()] * len(out_shape) if many else spec(),
        scratch_shapes=list(scratch),
        compiler_params=pltpu.CompilerParams(vmem_limit_bytes=vmem << 20),
        cost_estimate=pl.CostEstimate(flops=flops, bytes_accessed=4 << 20, transcendentals=exps),
        name=name,
    )(*ins)


def square_column(n):
    return lax.broadcasted_iota(jnp.int32, (n, n), 0) == lax.broadcasted_iota(jnp.int32, (n, n), 1)


def fetch(sems, *pairs):
    copies = [pltpu.make_async_copy(src, dst, sems.at[n]) for n, (src, dst) in enumerate(pairs)]
    for copy in copies:
        copy.start()
    return copies


def squares_kernel(h_ref, out_ref, held, sems):
    fetch(sems, (h_ref, held))[0].wait()
    h = held[...].astype(f32)
    column = jnp.sum(h * h, axis=1, keepdims=True)
    row = jnp.sum(jnp.where(square_column(ROWS), column, 0.0), axis=0, keepdims=True)
    out_ref[...] = jnp.broadcast_to(row, (8, ROWS))


def normed(h, power, gain):
    column = jnp.sum(jnp.where(square_column(ROWS), power, 0.0), axis=1, keepdims=True)
    return (h.astype(f32) * lax.rsqrt(column / D + EPS) * gain).astype(bf16)


def put_kv(x, wk_ref, wv_ref, keep_ref, send_ref):
    k = jnp.dot(x, wk_ref[...], preferred_element_type=f32)
    v = jnp.dot(x, wv_ref[...], preferred_element_type=f32)
    high = k.astype(bf16)
    keep_ref[:, :HEAD] = v
    keep_ref[:, HEAD:] = k
    send_ref[:, :HEAD] = v.astype(bf16)
    send_ref[:, HEAD : 2 * HEAD] = high
    send_ref[:, 2 * HEAD : 3 * HEAD] = (k - high.astype(f32)).astype(bf16)


def put_q(x, wq_ref, keep_ref, send_ref, at):
    q = jnp.dot(x, wq_ref[...], preferred_element_type=f32)
    keep_ref[...] = q
    send_ref[:, at : at + QW] = q.astype(bf16)


def own_kernel(gain_ref, wq_ref, wk_ref, wv_ref, mine_ref, theirs_ref, h_ref, kv_ref, q_ref, send_ref, h, wq, wk, wv, sems):
    pending = fetch(sems, (h_ref, h), (wk_ref, wk), (wv_ref, wv), (wq_ref, wq))
    pending[0].wait()
    x = normed(h[...], mine_ref[:1, :] + theirs_ref[:1, :], gain_ref[...])
    pending[1].wait()
    pending[2].wait()
    put_kv(x, wk, wv, kv_ref, send_ref)
    pending[3].wait()
    put_q(x, wq, q_ref, send_ref, 3 * HEAD)


def others_kernel(n, gain_ref, wk_ref, wv_ref, *refs):
    powers, halves = refs[:n], refs[n : 3 * n]
    x_ref, kv_ref, send_ref, wk, wv, sems = refs[3 * n :]
    pending = fetch(sems, (wk_ref, wk), (wv_ref, wv))
    for c in range(n):
        h = jnp.concatenate([halves[2 * c][...], halves[2 * c + 1][...]], axis=0)
        x_ref[c * ROWS : (c + 1) * ROWS, :] = normed(h, powers[c][:1, :], gain_ref[...])
    for copy in pending:
        copy.wait()
    put_kv(x_ref[...], wk, wv, kv_ref, send_ref)


def q_kernel(xa_ref, xb_ref, wq_ref, keep_ref, send_ref, wq, sems):
    for copy in fetch(sems, (wq_ref, wq)):
        copy.wait()
    q = jnp.dot(jnp.concatenate([xa_ref[...], xb_ref[...]], axis=0), wq[...], preferred_element_type=f32)
    keep_ref[...] = q
    send_ref[...] = q.astype(bf16)


def rotated(u, cosine, sine):
    return (u * cosine + pltpu.roll(u, HALF, 1) * sine).astype(bf16)


def rotary_kv_kernel(keep0_ref, got0_ref, keepa_ref, gota_ref, keepb_ref, gotb_ref, cos_ref, sin_ref, kv_ref):
    for keep, got, s in (
        (keep0_ref, got0_ref, slice(0, ROWS)),
        (keepa_ref, gota_ref, slice(ROWS, 3 * ROWS)),
        (keepb_ref, gotb_ref, slice(3 * ROWS, BLOCK)),
    ):
        k = keep[:, HEAD:] + (
            got[:, HEAD : 2 * HEAD].astype(f32) + got[:, 2 * HEAD : 3 * HEAD].astype(f32)
        )
        kv_ref[s, :HEAD] = rotated(k, cos_ref[s, :], sin_ref[s, :])
        kv_ref[s, HEAD:] = (keep[:, :HEAD] + got[:, :HEAD].astype(f32)).astype(bf16)


def rotary_q_kernel(keep0_ref, got0_ref, keep_ref, got_ref, cos_ref, sin_ref, q_ref):
    for keep, got, s, at in (
        (keep0_ref, got0_ref, slice(0, ROWS), 3 * HEAD),
        (keep_ref, got_ref, slice(ROWS, BLOCK), 0),
    ):
        for h in range(HEADS):
            w = slice(h * HEAD, (h + 1) * HEAD)
            u = keep[:, w] + got[:, at + h * HEAD : at + (h + 1) * HEAD].astype(f32)
            q_ref[s, w] = rotated(u, cos_ref[s, :], sin_ref[s, :])


def chunk_of(ref, c):
    at = (0, 1, 3, 2)[c] * ROWS
    return ref[at : at + ROWS, :]


def stacked(q):
    return jnp.concatenate([q[:, h * HEAD : (h + 1) * HEAD] for h in range(HEADS)], axis=0)


def local_kernel(idx_ref, len_ref, q_ref, own_ref, prev_ref, acc_ref, max_ref, sum_ref, bias_ref):
    tc, ctx = idx_ref[0], idx_ref[1]
    lengths = len_ref[...].astype(f32)
    i = lax.broadcasted_iota(jnp.int32, (64, 64), 0)
    j = lax.broadcasted_iota(jnp.int32, (64, 64), 1)
    starts = jnp.sum(jnp.where(i < j, lengths, 0.0), axis=0, keepdims=True)
    prefix = jnp.sum(jnp.where(i[:, :1] < 1, lengths, 0.0), axis=0, keepdims=True).astype(jnp.int32)
    lane = lax.broadcasted_iota(jnp.int32, (ROWS, ROWS), 1)
    for r in range(4):
        a = (tc + r) % 4
        base = ctx * BLOCK + a * ROWS
        pos = base + lax.broadcasted_iota(jnp.int32, (ROWS, 64), 0)
        begun = jnp.where(starts <= pos.astype(f32), starts, 0.0)
        start = jnp.max(begun, axis=1, keepdims=True).astype(jnp.int32)
        t = base + lax.broadcasted_iota(jnp.int32, (ROWS, 1), 0)
        low = jnp.where(start >= prefix, start, jnp.int32(1 << 30))
        keys, values = [], []
        for n in range(5):
            c = (r + n) % 4
            if n == 0:
                chunk = chunk_of(prev_ref, c)
            elif n == 4:
                chunk = chunk_of(own_ref, c)
            else:
                chunk = jnp.where(a + n < 4, chunk_of(prev_ref, c), chunk_of(own_ref, c))
            keys.append(chunk[:, :HEAD])
            values.append(chunk[:, HEAD:])
            u = base + (n - 4) * ROWS + lane
            bias_ref[:, n * ROWS : (n + 1) * ROWS] = jnp.where((u >= low) & (u <= t), 0.0, MASKED)
        keys = jnp.concatenate(keys, axis=0)
        values = jnp.concatenate(values, axis=0)
        q = stacked(chunk_of(q_ref, r))
        s = lax.dot_general(q, keys, (((1,), (1,)), ((), ())), preferred_element_type=f32)
        s = (s.reshape(HEADS, ROWS, 5 * ROWS) + bias_ref[...][None]).reshape(BLOCK, 5 * ROWS)
        largest = jnp.max(s, axis=1, keepdims=True)
        p = jnp.exp2((s - largest) * EXPONENT)
        total = jnp.sum(p, axis=1, keepdims=True)
        acc_ref[r] = jnp.dot(p.astype(bf16), values, preferred_element_type=f32)
        max_ref[r] = jnp.broadcast_to(largest, (BLOCK, HEAD))
        sum_ref[r] = jnp.broadcast_to(total, (BLOCK, HEAD))


def local(idx, lengths, q, own, prev):
    shape = jax.ShapeDtypeStruct((4, BLOCK, HEAD), f32)
    return call(
        local_kernel, "local", [shape] * 3, (idx, lengths, q, own, prev), smem=1,
        scratch=[pltpu.VMEM((ROWS, 5 * ROWS), f32)], vmem=32,
        flops=4 * BLOCK * QW * 640, exps=4 * BLOCK * 640,
    )


def prefix_kernel(r, idx_ref, len_ref, acc_ref, max_ref, sum_ref, q_ref, pre_ref, other_ref, wo_ref, out_ref, bias_ref):
    tc, ctx = idx_ref[0], idx_ref[1]
    base = ctx * BLOCK + (tc + r) % 4 * ROWS
    lengths = len_ref[...].astype(f32)
    i = lax.broadcasted_iota(jnp.int32, (64, 1), 0)
    prefix = jnp.sum(jnp.where(i < 1, lengths, 0.0), axis=0, keepdims=True).astype(jnp.int32)
    high = jnp.minimum(prefix, base + 1 + lax.broadcasted_iota(jnp.int32, (ROWS, 1), 0))
    lane = lax.broadcasted_iota(jnp.int32, (ROWS, ROWS), 1)
    keys, values = [], []
    for c in range(4):
        chunk = chunk_of(pre_ref, c) + chunk_of(other_ref, c)
        keys.append(chunk[:, :HEAD])
        values.append(chunk[:, HEAD:])
        u = ((tc + c) % 4) * ROWS + lane
        bias_ref[:, c * ROWS : (c + 1) * ROWS] = jnp.where(u < high, 0.0, MASKED)
    keys = jnp.concatenate(keys, axis=0)
    values = jnp.concatenate(values, axis=0)
    q = stacked(chunk_of(q_ref, r))
    s = lax.dot_general(q, keys, (((1,), (1,)), ((), ())), preferred_element_type=f32)
    s = (s.reshape(HEADS, ROWS, BLOCK) + bias_ref[...][None]).reshape(BLOCK, BLOCK)
    before = max_ref[r][:, :1]
    largest = jnp.maximum(jnp.max(s, axis=1, keepdims=True), before)
    p = jnp.exp2((s - largest) * EXPONENT)
    factor = jnp.exp2((before - largest) * EXPONENT)
    total = jnp.sum(p, axis=1, keepdims=True) + factor * sum_ref[r][:, :1]
    mixed = jnp.dot(p.astype(bf16), values, preferred_element_type=f32) + factor * acc_ref[r]
    mixed = (mixed / total).astype(bf16)
    attended = jnp.concatenate([mixed[h * ROWS : (h + 1) * ROWS] for h in range(HEADS)], axis=1)
    out_ref[...] = jnp.dot(attended, wo_ref[...], preferred_element_type=f32).astype(out_ref.dtype)


def finish(r, idx, lengths, state, q, pre, wo, dtype):
    return call(
        functools.partial(prefix_kernel, r), "prefix", jax.ShapeDtypeStruct((ROWS, 2048), dtype),
        (idx, lengths, *state, q, *pre, wo), smem=1,
        scratch=[pltpu.VMEM((ROWS, BLOCK), f32)],
        flops=4 * ROWS * QW * 512 + 2 * ROWS * QW * 2048, exps=4 * ROWS * 512,
    )


def spread_far(x, ctx):
    at = jnp.where(ctx == 0, x, jnp.zeros_like(x))
    got = [lax.ppermute(x, "ctx", [(0, 4 * z)]) for z in (2, 4, 6)]
    at = at + got[0] + got[1] + got[2]
    return at, [lax.ppermute(at, "ctx", [(e, e + d) for e in (0, 8, 16, 24)]) for d in (4, 6, 2)]


def held(*arrays):
    return [pltpu.VMEM(a.shape, a.dtype) for a in arrays] + [pltpu.SemaphoreType.DMA((len(arrays),))]


def per_device(hidden, norm_gain, seg_lengths, wq, wk, wv, wo):
    tc = lax.axis_index("tc")
    ctx = lax.axis_index("ctx")
    idx = jnp.stack([tc, ctx]).astype(jnp.int32)
    upper, lower = hidden[:HALF], hidden[HALF:]
    h1u = rel(upper, "tc", 4, 1)
    h3l = rel(lower, "tc", 4, 3)
    h1l = rel(lower, "tc", 4, 1)
    h3u = rel(upper, "tc", 4, 3)
    h2u = rel(h1u, "tc", 4, 1)
    h2l = rel(h3l, "tc", 4, 3)
    mine = call(
        squares_kernel, "squares", jax.ShapeDtypeStruct((8, ROWS), f32), (hidden,), stay=(0,),
        scratch=held(hidden),
    )
    theirs = rel(mine, "tr", 2, 1)
    theirs, _, _ = lax.optimization_barrier((theirs, h1u, h3l))
    gain = norm_gain.reshape(1, -1)
    offset = (jnp.array([0, 1, 3, 2], jnp.int32) + tc) % 4 * ROWS
    positions = (ctx * BLOCK + offset[:, None] + jnp.arange(ROWS, dtype=jnp.int32)[None, :]).reshape(-1)
    frequency = ROPE_BASE ** (-(jnp.arange(HALF, dtype=f32) * 2.0 / HEAD))
    angles = positions.astype(f32)[:, None] * jnp.concatenate([frequency, frequency])[None, :]
    cosine = jnp.cos(angles)
    sine = jnp.sin(angles) * jnp.where(jnp.arange(HEAD) < HALF, -1.0, 1.0)[None, :]
    lengths = seg_lengths.reshape(-1, 1)

    def shape(rows, columns, dtype):
        return jax.ShapeDtypeStruct((rows, columns), dtype)

    kv0, q0, send0 = call(
        own_kernel, "own", [shape(ROWS, 2 * HEAD, f32), shape(ROWS, QW, f32), shape(ROWS, 7 * HEAD, bf16)],
        (gain, wq, wk, wv, mine, theirs, hidden), stay=(1, 2, 3, 6),
        scratch=held(hidden, wq, wk, wv), flops=2 * ROWS * 2048 * 768,
    )
    got0 = rel(send0, "tr", 2, 1)
    power, send0 = lax.optimization_barrier((mine + theirs, send0))
    p1, p3, p2 = [rel(power, "tc", 4, d) for d in (1, 3, 2)]

    def others(powers, hs):
        rows = ROWS * len(powers)
        return call(
            functools.partial(others_kernel, len(powers)), "others",
            [shape(rows, 2048, bf16), shape(rows, 2 * HEAD, f32), shape(rows, 3 * HEAD, bf16)],
            (gain, wk, wv, *powers, *hs), stay=(1, 2), scratch=held(wk, wv), flops=2 * rows * 2048 * 256,
        )

    x13, kv13, send13 = others((p1, p3), (h1u, h1l, h3u, h3l))
    got13 = rel(send13, "tr", 2, 1)
    x2, kv2, send2 = others((p2,), (h2u, h2l))
    got2 = rel(send2, "tr", 2, 1)
    q1, send_q = call(
        q_kernel, "q", [shape(3 * ROWS, QW, f32), shape(3 * ROWS, QW, bf16)], (x13, x2, wq),
        stay=(2,), scratch=held(wq), flops=6 * ROWS * 2048 * QW,
    )
    got_q = rel(send_q, "tr", 2, 1)
    got2, send_q = lax.optimization_barrier((got2, send_q))
    kv = call(
        rotary_kv_kernel, "rotary_kv", shape(BLOCK, 2 * HEAD, bf16), (kv0, got0, kv13, got13, kv2, got2, cosine, sine),
        flops=BLOCK * 256 * 8,
    )
    prev = lax.ppermute(kv, "ctx", [(i, i + 1) for i in range(lax.axis_size("ctx") - 1)])
    at, got = spread_far(kv, ctx)
    q = call(
        rotary_q_kernel, "rotary_q", shape(BLOCK, QW, bf16), (q0, got0, q1, got_q, cosine, sine),
        flops=BLOCK * 512 * 8,
    )
    got, q, prev = lax.optimization_barrier((got, q, prev))
    at = at + got[0] + got[1] + got[2]
    pre = (at, lax.ppermute(at, "ctx", [(2 * i, 2 * i + 1) for i in range(lax.axis_size("ctx") // 2)]))
    state = local(idx, lengths, q, kv, prev)
    parts = {}
    for r in (2, 1, 3, 0):
        parts[r] = finish(r, idx, lengths, state, q, pre, wo, f32 if r == 0 else bf16)
    total = parts[0]
    for r in (1, 3, 2):
        total = total + rel(parts[r], "tc", 4, -r).astype(f32)
    return (hidden.astype(f32) + total).astype(bf16)


def solution(mesh):
    in_specs = (
        P(("ctx", "tc"), "tr"),
        P("tr"),
        P(),
        P("tr", "tc"),
        P("tr", "tc"),
        P("tr", "tc"),
        P("tc", "tr"),
    )
    out_specs = P(("ctx", "tc"), "tr")
    return jax.shard_map(
        per_device, mesh=mesh, in_specs=in_specs, out_specs=out_specs, check_vma=False
    )
```

time: 139 us -> 107 us (0.77)
  blocking collectives: 33.7 us -> 0 us
  starting transfers between devices: 26.6 us -> 39.2 us
  waiting for transfers between devices: 47 us -> 37.6 us
  Pallas kernels: 20.9 us -> 16 us
  local copies, waits for them, and re-layouts: 5.53 us -> 9.35 us
    psum x1 -> x0, blocking collectives: 33.7 us -> none  [per_device(): power = lax.psum(placed, ('tr', 'tc'))]
    ppermute x10 -> x17, starting transfers between devices: 17.3 us -> 29.9 us  [rel(): return lax.ppermute(x, axis, [((i + distance) % n, i) for i in range(n)])]
    ppermute x8, waiting for transfers between devices: 19.7 us -> 11.5 us  [the longest x3 11.4 us: spread_far(): lax.ppermute(at, 'ctx', [(e, e + d) for e in (0, 8, 16, 24)])]
    pallas_call x8 -> x12, Pallas kernels: 20.9 us -> 16 us  [call(): pl.pallas_call(kernel, out_shape=out_shape, in_specs=[spec(w) for w in wh...]
    unnamed x24 -> x30, local copies, waits for them, and re-layouts: 5.44 us -> 8.13 us
    ppermute x10 -> x17, waiting for transfers between devices: 27.3 us -> 26.1 us  [rel(): return lax.ppermute(x, axis, [((i + distance) % n, i) for i in range(n)])]
  transfers between devices with their start and end apart: 18 -> 25, of which waited for: 7 -> 6; matrix products, arithmetic and copies ran while one was open for 2% -> 3% of each run, Pallas kernels for 11% -> 13%
where the time goes in v2:
time: 107 us
  starting transfers between devices  39.2 us (37%)
  waiting for transfers between devices  37.6 us (35%)
  Pallas kernels  16 us (15%)
  local copies, waits for them, and re-layouts  9.35 us (9%)
  other arithmetic  4.22 us (4%)
    ppermute x17, starting transfers between devices, rel(): return lax.ppermute(x, axis, [((i + distance) % n, i) for i in range(n)])  29.9 us
    ppermute x17, waiting for transfers between devices, rel(): return lax.ppermute(x, axis, [((i + distance) % n, i) for i in range(n)])  26.1 us
    pallas_call x12, Pallas kernels, call(): pl.pallas_call(kernel, out_shape=out_shape, in_specs=[spec(w) for w in wh...  16 us
    ppermute x3, waiting for transfers between devices, spread_far(): lax.ppermute(at, 'ctx', [(e, e + d) for e in (0, 8, 16, 24)])  11.4 us
    unnamed x30, local copies, waits for them, and re-layouts  8.13 us
    ppermute x3, starting transfers between devices, spread_far(): got = [lax.ppermute(x, 'ctx', [(0, 4 * z)]) for z in (2, 4, 6)]  3.43 us
    ppermute x3, starting transfers between devices, spread_far(): lax.ppermute(at, 'ctx', [(e, e + d) for e in (0, 8, 16, 24)])  2.65 us
  transfers between devices with their start and end apart: 25, of which 6 were waited for; matrix products, arithmetic and copies ran while one was open for 3% of the time, Pallas kernels for 13%

profile of v2, /device:TPU:102, one launch (start us, length us, event | category | flops | bytes accessed | tf_op | source)
XLA Modules:
  0.0 106.7 jit_solution(13188826980452006866)
XLA Ops:
  2.0 2.4 %collective-permute-start.2 = (bf16[64,2048]{1,0:T(8,128)(2,1)S(1)}, bf16[64,2048]{1,0:T(8,128)(2,1)S(1)}, u32[]{:S(2)}, u32[]{:S(2)}) collective-permute-start(bf16[64,2048]{1,0:T(8,128)(2,1)S(1)} %get-tuple-element.49), channel_id=1, source_target_pairs={{3,0},{0,1},{1,2},{2,3},{7,4},{4,5},{5,6},{6,7},{11,8},{8,9},{9,10... | collective-permute-start | bytes 786440 | tf_op jit(solution)/shard_map/ppermute | solution.py:32
  4.5 2.0 %collective-permute-start.1 = (bf16[64,2048]{1,0:T(8,128)(2,1)S(1)}, bf16[64,2048]{1,0:T(8,128)(2,1)S(1)}, u32[]{:S(2)}, u32[]{:S(2)}) collective-permute-start(bf16[64,2048]{1,0:T(8,128)(2,1)S(1)} %get-tuple-element.50), channel_id=1, source_target_pairs={{1,0},{2,1},{3,2},{0,3},{5,4},{6,5},{7,6},{4,7},{9,8},{10,9},{11,1... | collective-permute-start | bytes 786440 | tf_op jit(solution)/shard_map/ppermute | solution.py:32
  7.8 3.3 %collective-permute-start = (f32[8,128]{1,0:T(8,128)S(1)}, f32[8,128]{1,0:T(8,128)S(1)}, u32[]{:S(2)}, u32[]{:S(2)}) collective-permute-start(f32[8,128]{1,0:T(8,128)S(1)} %squares.1.mine_ref), channel_id=1, source_target_pairs={{4,0},{0,4},{5,1},{1,5},{6,2},{2,6},{7,3},{3,7},{12,8},{8,12},{13,... | collective-permute-start | bytes 12296 | tf_op jit(solution)/shard_map/ppermute | solution.py:32
  11.8 3.1 %collective-permute-start.11 = (bf16[64,2048]{1,0:T(8,128)(2,1)S(1)}, bf16[64,2048]{1,0:T(8,128)(2,1)S(1)}, u32[]{:S(2)}, u32[]{:S(2)}) collective-permute-start(bf16[64,2048]{1,0:T(8,128)(2,1)S(1)} %collective-permute-done.2.refs_5_), channel_id=1, source_target_pairs={{3,0},{0,1},{1,2},{2,3},{7,4},{4,5},{5,6},{6,7},{11,8},{8,9},{9,10... | collective-permute-start | bytes 786440 | tf_op jit(solution)/shard_map/ppermute | solution.py:32
  16.1 1.6 %copy-done.1 = bf16[2048,512]{1,0:T(8,128)(2,1)S(1)} copy-done((bf16[2048,512]{1,0:T(8,128)(2,1)S(1)}, bf16[2048,512]{1,0:T(8,128)(2,1)}, u32[]{:S(2)}) %copy-start.1) | copy-done | bytes 2097176
  22.9 3.3 %collective-permute-start.5 = (f32[8,128]{1,0:T(8,128)S(1)}, f32[8,128]{1,0:T(8,128)S(1)}, u32[]{:S(2)}, u32[]{:S(2)}) collective-permute-start(f32[8,128]{1,0:T(8,128)S(1)} %add.71), channel_id=1, source_target_pairs={{3,0},{0,1},{1,2},{2,3},{7,4},{4,5},{5,6},{6,7},{11,8},{8,9},{9,10... | collective-permute-start | bytes 12296 | tf_op jit(solution)/shard_map/ppermute | solution.py:32
  26.3 1.6 %collective-permute-start.9 = (f32[8,128]{1,0:T(8,128)S(1)}, f32[8,128]{1,0:T(8,128)S(1)}, u32[]{:S(2)}, u32[]{:S(2)}) collective-permute-start(f32[8,128]{1,0:T(8,128)S(1)} %add.71), channel_id=1, source_target_pairs={{2,0},{3,1},{0,2},{1,3},{6,4},{7,5},{4,6},{5,7},{10,8},{11,9},{8,1... | collective-permute-start | bytes 12296 | tf_op jit(solution)/shard_map/ppermute | solution.py:32
  27.9 3.2 %collective-permute-start.3 = (bf16[128,896]{1,0:T(8,128)(2,1)S(1)}, bf16[128,896]{1,0:T(8,128)(2,1)S(1)}, u32[]{:S(2)}, u32[]{:S(2)}) collective-permute-start(bf16[128,896]{1,0:T(8,128)(2,1)S(1)} %get-tuple-element.29), channel_id=1, source_target_pairs={{4,0},{0,4},{5,1},{1,5},{6,2},{2,6},{7,3},{3,7},{12,8},{8,12},{13,... | collective-permute-start | bytes 688136 | tf_op jit(solution)/shard_map/ppermute | solution.py:32
  32.3 3.2 %collective-permute-start.8 = (bf16[256,384]{1,0:T(8,128)(2,1)S(1)}, bf16[256,384]{1,0:T(8,128)(2,1)S(1)}, u32[]{:S(2)}, u32[]{:S(2)}) collective-permute-start(bf16[256,384]{1,0:T(8,128)(2,1)S(1)} %get-tuple-element.32), channel_id=1, source_target_pairs={{4,0},{0,4},{5,1},{1,5},{6,2},{2,6},{7,3},{3,7},{12,8},{8,12},{13,... | collective-permute-start | bytes 589832 | tf_op jit(solution)/shard_map/ppermute | solution.py:32
  39.1 3.6 %collective-permute-done.12.gotb_ref = bf16[128,384]{1,0:T(8,128)(2,1)S(1)} collective-permute-done((bf16[128,384]{1,0:T(8,128)(2,1)S(1)}, bf16[128,384]{1,0:T(8,128)(2,1)S(1)}, u32[]{:S(2)}, u32[]{:S(2)}) %collective-permute-start.12) | collective-permute-done | bytes 98336 | tf_op jit(solution)/shard_map/ppermute | solution.py:32
  43.5 1.4 %collective-permute-start.14 = (bf16[512,256]{1,0:T(8,128)(2,1)S(1)}, bf16[512,256]{1,0:T(8,128)(2,1)}, u32[]{:S(2)}, u32[]{:S(2)}) collective-permute-start(bf16[512,256]{1,0:T(8,128)(2,1)S(1)} %rotary_kv.1.own_ref), channel_id=1, source_target_pairs={{0,128},{1,129},{2,130},{3,131},{4,132},{5,133},{6,134},{7,135}} | collective-permute-start | bytes 786440 | tf_op jit(solution)/shard_map/ppermute | solution.py:252
  46.3 2.3 %collective-permute-start.19 = (bf16[384,512]{1,0:T(8,128)(2,1)S(1)}, bf16[384,512]{1,0:T(8,128)(2,1)S(1)}, u32[]{:S(2)}, u32[]{:S(2)}) collective-permute-start(bf16[384,512]{1,0:T(8,128)(2,1)S(1)} %get-tuple-element.37), channel_id=1, source_target_pairs={{4,0},{0,4},{5,1},{1,5},{6,2},{2,6},{7,3},{3,7},{12,8},{8,12},{13,... | collective-permute-start | bytes 1179656 | tf_op jit(solution)/shard_map/ppermute | solution.py:32
  48.5 1.9 %collective-permute-start.20 = (bf16[512,256]{1,0:T(8,128)(2,1)S(1)}, bf16[512,256]{1,0:T(8,128)(2,1)S(1)}, u32[]{:S(2)}, u32[]{:S(2)}) collective-permute-start(bf16[512,256]{1,0:T(8,128)(2,1)S(1)} %rotary_kv.1.own_ref), channel_id=1, source_target_pairs={{0,8},{8,16},{16,24},{24,32},{32,40},{40,48},{48,56},{56,64},{64,7... | collective-permute-start | bytes 786440 | tf_op jit(solution)/shard_map/ppermute | solution.py:321
  54.3 3.7 %collective-permute-done.19.got_ref = bf16[384,512]{1,0:T(8,128)(2,1)S(1)} collective-permute-done((bf16[384,512]{1,0:T(8,128)(2,1)S(1)}, bf16[384,512]{1,0:T(8,128)(2,1)S(1)}, u32[]{:S(2)}, u32[]{:S(2)}) %collective-permute-start.19) | collective-permute-done | bytes 393248 | tf_op jit(solution)/shard_map/ppermute | solution.py:32
  59.0 11.4 %collective-permute-done.16 = bf16[512,256]{1,0:T(8,128)(2,1)S(1)} collective-permute-done((bf16[512,256]{1,0:T(8,128)(2,1)S(1)}, bf16[512,256]{1,0:T(8,128)(2,1)S(1)}, u32[]{:S(2)}, u32[]{:S(2)}) %collective-permute-start.16) | collective-permute-done | bytes 262176 | tf_op jit(solution)/shard_map/ppermute | solution.py:254
  73.0 3.3 %local.1 = (f32[4,512,128]{2,1,0:T(8,128)S(1)}, f32[4,512,128]{2,1,0:T(8,128)S(1)}, f32[4,512,128]{2,1,0:T(8,128)S(1)}) custom-call(s32[2]{0:T(128)S(1)} %pad_add_fusion.idx_ref, s32[64,1]{1,0:T(8,128)S(1)} %copy.10.len_ref, bf16[512,512]{1,0:T(8,128)(2,1)S(1)} %rotary_q.1.q_ref, bf16[512,256]{1,0:T(8,128)(2,1)S(1)} %rotary_kv.1.own_ref, ...), custom_call_target="tpu_custom_call" | custom-call | flops 671088640 | bytes 4194304 | tf_op jit(solution)/shard_map/local/pallas_call | solution.py:38
  76.3 1.9 %prefix.5 = bf16[128,2048]{1,0:T(8,128)(2,1)S(1)} custom-call(s32[2]{0:T(128)S(1)} %pad_add_fusion.idx_ref, s32[64,1]{1,0:T(8,128)S(1)} %copy.10.len_ref, f32[4,512,128]{2,1,0:T(8,128)S(1)} %get-tuple-element.43.acc_ref, f32[4,512,128]{2,1,0:T(8,128)S(1)} %get-tuple-element.44.max_ref, f32[4,512,128]{2,1,0:T(8,128)S(1)} %get-tuple-element.45.sum_ref, ...), custom_call_target="tpu_custom_call" | custom-call | flops 402653184 | bytes 4194304 | tf_op jit(solution)/shard_map/prefix/pallas_call | solution.py:38
  78.2 2.3 %collective-permute-start.22 = (bf16[128,2048]{1,0:T(8,128)(2,1)S(1)}, bf16[128,2048]{1,0:T(8,128)(2,1)S(1)}, u32[]{:S(2)}, u32[]{:S(2)}) collective-permute-start(bf16[128,2048]{1,0:T(8,128)(2,1)S(1)} %prefix.5), channel_id=1, source_target_pairs={{3,0},{0,1},{1,2},{2,3},{7,4},{4,5},{5,6},{6,7},{11,8},{8,9},{9,10... | collective-permute-start | bytes 1572872 | tf_op jit(solution)/shard_map/ppermute | solution.py:32
  80.5 1.9 %prefix.6 = bf16[128,2048]{1,0:T(8,128)(2,1)S(1)} custom-call(s32[2]{0:T(128)S(1)} %pad_add_fusion.idx_ref, s32[64,1]{1,0:T(8,128)S(1)} %copy.10.len_ref, f32[4,512,128]{2,1,0:T(8,128)S(1)} %get-tuple-element.43.acc_ref, f32[4,512,128]{2,1,0:T(8,128)S(1)} %get-tuple-element.44.max_ref, f32[4,512,128]{2,1,0:T(8,128)S(1)} %get-tuple-element.45.sum_ref, ...), custom_call_target="tpu_custom_call" | custom-call | flops 402653184 | bytes 4194304 | tf_op jit(solution)/shard_map/prefix/pallas_call | solution.py:38
  82.5 1.9 %prefix.7 = bf16[128,2048]{1,0:T(8,128)(2,1)S(1)} custom-call(s32[2]{0:T(128)S(1)} %pad_add_fusion.idx_ref, s32[64,1]{1,0:T(8,128)S(1)} %copy.10.len_ref, f32[4,512,128]{2,1,0:T(8,128)S(1)} %get-tuple-element.43.acc_ref, f32[4,512,128]{2,1,0:T(8,128)S(1)} %get-tuple-element.44.max_ref, f32[4,512,128]{2,1,0:T(8,128)S(1)} %get-tuple-element.45.sum_ref, ...), custom_call_target="tpu_custom_call" | custom-call | flops 402653184 | bytes 4194304 | tf_op jit(solution)/shard_map/prefix/pallas_call | solution.py:38
  84.4 1.6 %collective-permute-start.24 = (bf16[128,2048]{1,0:T(8,128)(2,1)S(1)}, bf16[128,2048]{1,0:T(8,128)(2,1)S(1)}, u32[]{:S(2)}, u32[]{:S(2)}) collective-permute-start(bf16[128,2048]{1,0:T(8,128)(2,1)S(1)} %prefix.7), channel_id=1, source_target_pairs={{2,0},{3,1},{0,2},{1,3},{6,4},{7,5},{4,6},{5,7},{10,8},{11,9},{8,1... | collective-permute-start | bytes 1572872 | tf_op jit(solution)/shard_map/ppermute | solution.py:32
  86.0 1.9 %prefix.4 = f32[128,2048]{1,0:T(8,128)S(1)} custom-call(s32[2]{0:T(128)S(1)} %pad_add_fusion.idx_ref, s32[64,1]{1,0:T(8,128)S(1)} %copy.10.len_ref, f32[4,512,128]{2,1,0:T(8,128)S(1)} %get-tuple-element.43.acc_ref, f32[4,512,128]{2,1,0:T(8,128)S(1)} %get-tuple-element.44.max_ref, f32[4,512,128]{2,1,0:T(8,128)S(1)} %get-tuple-element.45.sum_ref, ...), custom_call_target="tpu_custom_call" | custom-call | flops 402653184 | bytes 4194304 | tf_op jit(solution)/shard_map/prefix/pallas_call | solution.py:38
  87.8 12.3 %collective-permute-done.22 = bf16[128,2048]{1,0:T(8,128)(2,1)S(1)} collective-permute-done((bf16[128,2048]{1,0:T(8,128)(2,1)S(1)}, bf16[128,2048]{1,0:T(8,128)(2,1)S(1)}, u32[]{:S(2)}, u32[]{:S(2)}) %collective-permute-start.22) | collective-permute-done | bytes 524320 | tf_op jit(solution)/shard_map/ppermute | solution.py:32
  100.1 5.3 %collective-permute-done.23 = bf16[128,2048]{1,0:T(8,128)(2,1)S(1)} collective-permute-done((bf16[128,2048]{1,0:T(8,128)(2,1)S(1)}, bf16[128,2048]{1,0:T(8,128)(2,1)S(1)}, u32[]{:S(2)}, u32[]{:S(2)}) %collective-permute-start.23) | collective-permute-done | bytes 524320 | tf_op jit(solution)/shard_map/ppermute | solution.py:32
  (80 shorter events, 26.1 us)
Async XLA Ops:
  1.1 25.1 %collective-permute-start.6 = (bf16[64,2048]{1,0:T(8,128)(2,1)S(1)}, bf16[64,2048]{1,0:T(8,128)(2,1)S(1)}, u32[]{:S(2)}, u32[]{:S(2)}) collective-permute-start(bf16[64,2048]{1,0:T(8,128)(2,1)S(1)} %get-tuple-element.49), channel_id=1, source_target_pairs={{1,0},{2,1},{3,2},{0,3},{5,4},{6,5},{7,6},{4,7},{9,8},{10,9},{11,1... | collective-permute-start | bytes 786440 | tf_op jit(solution)/shard_map/ppermute | solution.py:32
  2.0 9.8 %collective-permute-start.2 = (bf16[64,2048]{1,0:T(8,128)(2,1)S(1)}, bf16[64,2048]{1,0:T(8,128)(2,1)S(1)}, u32[]{:S(2)}, u32[]{:S(2)}) collective-permute-start(bf16[64,2048]{1,0:T(8,128)(2,1)S(1)} %get-tuple-element.49), channel_id=1, source_target_pairs={{3,0},{0,1},{1,2},{2,3},{7,4},{4,5},{5,6},{6,7},{11,8},{8,9},{9,10... | collective-permute-start | bytes 786440 | tf_op jit(solution)/shard_map/ppermute | solution.py:32
  4.5 21.8 %collective-permute-start.7 = (bf16[64,2048]{1,0:T(8,128)(2,1)S(1)}, bf16[64,2048]{1,0:T(8,128)(2,1)S(1)}, u32[]{:S(2)}, u32[]{:S(2)}) collective-permute-start(bf16[64,2048]{1,0:T(8,128)(2,1)S(1)} %get-tuple-element.50), channel_id=1, source_target_pairs={{3,0},{0,1},{1,2},{2,3},{7,4},{4,5},{5,6},{6,7},{11,8},{8,9},{9,10... | collective-permute-start | bytes 786440 | tf_op jit(solution)/shard_map/ppermute | solution.py:32
  4.5 11.6 %collective-permute-start.1 = (bf16[64,2048]{1,0:T(8,128)(2,1)S(1)}, bf16[64,2048]{1,0:T(8,128)(2,1)S(1)}, u32[]{:S(2)}, u32[]{:S(2)}) collective-permute-start(bf16[64,2048]{1,0:T(8,128)(2,1)S(1)} %get-tuple-element.50), channel_id=1, source_target_pairs={{1,0},{2,1},{3,2},{0,3},{5,4},{6,5},{7,6},{4,7},{9,8},{10,9},{11,1... | collective-permute-start | bytes 786440 | tf_op jit(solution)/shard_map/ppermute | solution.py:32
  7.8 8.3 %collective-permute-start = (f32[8,128]{1,0:T(8,128)S(1)}, f32[8,128]{1,0:T(8,128)S(1)}, u32[]{:S(2)}, u32[]{:S(2)}) collective-permute-start(f32[8,128]{1,0:T(8,128)S(1)} %squares.1.mine_ref), channel_id=1, source_target_pairs={{4,0},{0,4},{5,1},{1,5},{6,2},{2,6},{7,3},{3,7},{12,8},{8,12},{13,... | collective-permute-start | bytes 12296 | tf_op jit(solution)/shard_map/ppermute | solution.py:32
  11.8 23.7 %collective-permute-start.11 = (bf16[64,2048]{1,0:T(8,128)(2,1)S(1)}, bf16[64,2048]{1,0:T(8,128)(2,1)S(1)}, u32[]{:S(2)}, u32[]{:S(2)}) collective-permute-start(bf16[64,2048]{1,0:T(8,128)(2,1)S(1)} %collective-permute-done.2.refs_5_), channel_id=1, source_target_pairs={{3,0},{0,1},{1,2},{2,3},{7,4},{4,5},{5,6},{6,7},{11,8},{8,9},{9,10... | collective-permute-start | bytes 786440 | tf_op jit(solution)/shard_map/ppermute | solution.py:32
  16.1 19.4 %collective-permute-start.10 = (bf16[64,2048]{1,0:T(8,128)(2,1)S(1)}, bf16[64,2048]{1,0:T(8,128)(2,1)S(1)}, u32[]{:S(2)}, u32[]{:S(2)}) collective-permute-start(bf16[64,2048]{1,0:T(8,128)(2,1)S(1)} %collective-permute-done.1.refs_2_), channel_id=1, source_target_pairs={{1,0},{2,1},{3,2},{0,3},{5,4},{6,5},{7,6},{4,7},{9,8},{10,9},{11,1... | collective-permute-start | bytes 786440 | tf_op jit(solution)/shard_map/ppermute | solution.py:32
  22.9 5.0 %collective-permute-start.5 = (f32[8,128]{1,0:T(8,128)S(1)}, f32[8,128]{1,0:T(8,128)S(1)}, u32[]{:S(2)}, u32[]{:S(2)}) collective-permute-start(f32[8,128]{1,0:T(8,128)S(1)} %add.71), channel_id=1, source_target_pairs={{3,0},{0,1},{1,2},{2,3},{7,4},{4,5},{5,6},{6,7},{11,8},{8,9},{9,10... | collective-permute-start | bytes 12296 | tf_op jit(solution)/shard_map/ppermute | solution.py:32
  26.3 9.2 %collective-permute-start.9 = (f32[8,128]{1,0:T(8,128)S(1)}, f32[8,128]{1,0:T(8,128)S(1)}, u32[]{:S(2)}, u32[]{:S(2)}) collective-permute-start(f32[8,128]{1,0:T(8,128)S(1)} %add.71), channel_id=1, source_target_pairs={{2,0},{3,1},{0,2},{1,3},{6,4},{7,5},{4,6},{5,7},{10,8},{11,9},{8,1... | collective-permute-start | bytes 12296 | tf_op jit(solution)/shard_map/ppermute | solution.py:32
  27.9 14.8 %collective-permute-start.3 = (bf16[128,896]{1,0:T(8,128)(2,1)S(1)}, bf16[128,896]{1,0:T(8,128)(2,1)S(1)}, u32[]{:S(2)}, u32[]{:S(2)}) collective-permute-start(bf16[128,896]{1,0:T(8,128)(2,1)S(1)} %get-tuple-element.29), channel_id=1, source_target_pairs={{4,0},{0,4},{5,1},{1,5},{6,2},{2,6},{7,3},{3,7},{12,8},{8,12},{13,... | collective-permute-start | bytes 688136 | tf_op jit(solution)/shard_map/ppermute | solution.py:32
  32.3 10.4 %collective-permute-start.8 = (bf16[256,384]{1,0:T(8,128)(2,1)S(1)}, bf16[256,384]{1,0:T(8,128)(2,1)S(1)}, u32[]{:S(2)}, u32[]{:S(2)}) collective-permute-start(bf16[256,384]{1,0:T(8,128)(2,1)S(1)} %get-tuple-element.32), channel_id=1, source_target_pairs={{4,0},{0,4},{5,1},{1,5},{6,2},{2,6},{7,3},{3,7},{12,8},{8,12},{13,... | collective-permute-start | bytes 589832 | tf_op jit(solution)/shard_map/ppermute | solution.py:32
  36.3 6.4 %collective-permute-start.12 = (bf16[128,384]{1,0:T(8,128)(2,1)S(1)}, bf16[128,384]{1,0:T(8,128)(2,1)S(1)}, u32[]{:S(2)}, u32[]{:S(2)}) collective-permute-start(bf16[128,384]{1,0:T(8,128)(2,1)S(1)} %get-tuple-element.34), channel_id=1, source_target_pairs={{4,0},{0,4},{5,1},{1,5},{6,2},{2,6},{7,3},{3,7},{12,8},{8,12},{13,... | collective-permute-start | bytes 294920 | tf_op jit(solution)/shard_map/ppermute | solution.py:32
  42.8 7.6 %collective-permute-start.15 = (bf16[512,256]{1,0:T(8,128)(2,1)S(1)}, bf16[512,256]{1,0:T(8,128)(2,1)S(1)}, u32[]{:S(2)}, u32[]{:S(2)}) collective-permute-start(bf16[512,256]{1,0:T(8,128)(2,1)S(1)} %rotary_kv.1.own_ref), channel_id=1, source_target_pairs={{0,192},{1,193},{2,194},{3,195},{4,196},{5,197},{6,198},{7,199}} | collective-permute-start | bytes 786440 | tf_op jit(solution)/shard_map/ppermute | solution.py:252
  43.5 6.9 %collective-permute-start.14 = (bf16[512,256]{1,0:T(8,128)(2,1)S(1)}, bf16[512,256]{1,0:T(8,128)(2,1)}, u32[]{:S(2)}, u32[]{:S(2)}) collective-permute-start(bf16[512,256]{1,0:T(8,128)(2,1)S(1)} %rotary_kv.1.own_ref), channel_id=1, source_target_pairs={{0,128},{1,129},{2,130},{3,131},{4,132},{5,133},{6,134},{7,135}} | collective-permute-start | bytes 786440 | tf_op jit(solution)/shard_map/ppermute | solution.py:252
  44.9 5.6 %collective-permute-start.13 = (bf16[512,256]{1,0:T(8,128)(2,1)S(1)}, bf16[512,256]{1,0:T(8,128)(2,1)}, u32[]{:S(2)}, u32[]{:S(2)}) collective-permute-start(bf16[512,256]{1,0:T(8,128)(2,1)S(1)} %rotary_kv.1.own_ref), channel_id=1, source_target_pairs={{0,64},{1,65},{2,66},{3,67},{4,68},{5,69},{6,70},{7,71}} | collective-permute-start | bytes 786440 | tf_op jit(solution)/shard_map/ppermute | solution.py:252
  46.3 11.7 %collective-permute-start.19 = (bf16[384,512]{1,0:T(8,128)(2,1)S(1)}, bf16[384,512]{1,0:T(8,128)(2,1)S(1)}, u32[]{:S(2)}, u32[]{:S(2)}) collective-permute-start(bf16[384,512]{1,0:T(8,128)(2,1)S(1)} %get-tuple-element.37), channel_id=1, source_target_pairs={{4,0},{0,4},{5,1},{1,5},{6,2},{2,6},{7,3},{3,7},{12,8},{8,12},{13,... | collective-permute-start | bytes 1179656 | tf_op jit(solution)/shard_map/ppermute | solution.py:32
  48.5 9.8 %collective-permute-start.20 = (bf16[512,256]{1,0:T(8,128)(2,1)S(1)}, bf16[512,256]{1,0:T(8,128)(2,1)S(1)}, u32[]{:S(2)}, u32[]{:S(2)}) collective-permute-start(bf16[512,256]{1,0:T(8,128)(2,1)S(1)} %rotary_kv.1.own_ref), channel_id=1, source_target_pairs={{0,8},{8,16},{16,24},{24,32},{32,40},{40,48},{48,56},{56,64},{64,7... | collective-permute-start | bytes 786440 | tf_op jit(solution)/shard_map/ppermute | solution.py:321
  51.6 7.5 %collective-permute-start.18 = (bf16[512,256]{1,0:T(8,128)(2,1)S(1)}, bf16[512,256]{1,0:T(8,128)(2,1)S(1)}, u32[]{:S(2)}, u32[]{:S(2)}) collective-permute-start(bf16[512,256]{1,0:T(8,128)(2,1)S(1)} %add_add_fusion.1), channel_id=1, source_target_pairs={{0,16},{64,80},{128,144},{192,208},{1,17},{65,81},{129,145},{193,2... | collective-permute-start | bytes 786440 | tf_op jit(solution)/shard_map/ppermute | solution.py:254
  52.3 6.8 %collective-permute-start.17 = (bf16[512,256]{1,0:T(8,128)(2,1)S(1)}, bf16[512,256]{1,0:T(8,128)(2,1)S(1)}, u32[]{:S(2)}, u32[]{:S(2)}) collective-permute-start(bf16[512,256]{1,0:T(8,128)(2,1)S(1)} %add_add_fusion.1), channel_id=1, source_target_pairs={{0,48},{64,112},{128,176},{192,240},{1,49},{65,113},{129,177},{193... | collective-permute-start | bytes 786440 | tf_op jit(solution)/shard_map/ppermute | solution.py:254
  53.0 17.5 %collective-permute-start.16 = (bf16[512,256]{1,0:T(8,128)(2,1)S(1)}, bf16[512,256]{1,0:T(8,128)(2,1)S(1)}, u32[]{:S(2)}, u32[]{:S(2)}) collective-permute-start(bf16[512,256]{1,0:T(8,128)(2,1)S(1)} %add_add_fusion.1), channel_id=1, source_target_pairs={{0,32},{64,96},{128,160},{192,224},{1,33},{65,97},{129,161},{193,2... | collective-permute-start | bytes 786440 | tf_op jit(solution)/shard_map/ppermute | solution.py:254
  70.5 5.8 %collective-permute-start.21 = (bf16[512,256]{1,0:T(8,128)(2,1)S(1)}, bf16[512,256]{1,0:T(8,128)(2,1)S(1)}, u32[]{:S(2)}, u32[]{:S(2)}) collective-permute-start(bf16[512,256]{1,0:T(8,128)(2,1)S(1)} %add_add_fusion.pre_ref), channel_id=1, source_target_pairs={{0,8},{16,24},{32,40},{48,56},{64,72},{80,88},{96,104},{112,120},{... | collective-permute-start | bytes 786440 | tf_op jit(solution)/shard_map/ppermute | solution.py:329
  78.2 21.9 %collective-permute-start.22 = (bf16[128,2048]{1,0:T(8,128)(2,1)S(1)}, bf16[128,2048]{1,0:T(8,128)(2,1)S(1)}, u32[]{:S(2)}, u32[]{:S(2)}) collective-permute-start(bf16[128,2048]{1,0:T(8,128)(2,1)S(1)} %prefix.5), channel_id=1, source_target_pairs={{3,0},{0,1},{1,2},{2,3},{7,4},{4,5},{5,6},{6,7},{11,8},{8,9},{9,10... | collective-permute-start | bytes 1572872 | tf_op jit(solution)/shard_map/ppermute | solution.py:32
  82.4 23.1 %collective-permute-start.23 = (bf16[128,2048]{1,0:T(8,128)(2,1)S(1)}, bf16[128,2048]{1,0:T(8,128)(2,1)S(1)}, u32[]{:S(2)}, u32[]{:S(2)}) collective-permute-start(bf16[128,2048]{1,0:T(8,128)(2,1)S(1)} %prefix.6), channel_id=1, source_target_pairs={{1,0},{2,1},{3,2},{0,3},{5,4},{6,5},{7,6},{4,7},{9,8},{10,9},{11,1... | collective-permute-start | bytes 1572872 | tf_op jit(solution)/shard_map/ppermute | solution.py:32
  84.4 21.1 %collective-permute-start.24 = (bf16[128,2048]{1,0:T(8,128)(2,1)S(1)}, bf16[128,2048]{1,0:T(8,128)(2,1)S(1)}, u32[]{:S(2)}, u32[]{:S(2)}) collective-permute-start(bf16[128,2048]{1,0:T(8,128)(2,1)S(1)} %prefix.7), channel_id=1, source_target_pairs={{2,0},{3,1},{0,2},{1,3},{6,4},{7,5},{4,6},{5,7},{10,8},{11,9},{8,1... | collective-permute-start | bytes 1572872 | tf_op jit(solution)/shard_map/ppermute | solution.py:32
  (16 other events, 162.2 us)

commit v3 on v2

--- a/solution.py
+++ b/solution.py
@@ -17,6 +17,8 @@
 HEADS = 4
 QW = HEADS * HEAD
 BLOCK = 512
+SIDE = 1024
+TAILED = HALF + 16
 SCALE = HEAD ** (-0.5)
 EXPONENT = SCALE * 1.4426950408889634
 
@@ -34,6 +36,7 @@
 
 def call(kernel, name, out_shape, ins, smem=0, stay=(), scratch=(), vmem=24, flops=0, exps=0):
     many = isinstance(out_shape, list)
+    ins = [pltpu.with_memory_space_constraint(x, pltpu.HBM) if n in stay else x for n, x in enumerate(ins)]
     where = [pltpu.SMEM] * smem + [pltpu.HBM if n in stay else pltpu.VMEM for n in range(smem, len(ins))]
     return pl.pallas_call(
         kernel,
@@ -58,8 +61,10 @@
     return copies
 
 
-def squares_kernel(h_ref, out_ref, held, sems):
+def squares_kernel(h_ref, upper_ref, lower_ref, out_ref, held, sems):
     fetch(sems, (h_ref, held))[0].wait()
+    upper_ref[...] = held[:HALF, :]
+    lower_ref[...] = held[HALF:, :]
     h = held[...].astype(f32)
     column = jnp.sum(h * h, axis=1, keepdims=True)
     row = jnp.sum(jnp.where(square_column(ROWS), column, 0.0), axis=0, keepdims=True)
@@ -67,8 +72,7 @@
 
 
 def normed(h, power, gain):
-    column = jnp.sum(jnp.where(square_column(ROWS), power, 0.0), axis=1, keepdims=True)
-    return (h.astype(f32) * lax.rsqrt(column / D + EPS) * gain).astype(bf16)
+    return (h.astype(f32) * lax.rsqrt(power / D + EPS) * gain).astype(bf16)
 
 
 def put_kv(x, wk_ref, wv_ref, keep_ref, send_ref):
@@ -88,24 +92,59 @@
     send_ref[:, at : at + QW] = q.astype(bf16)
 
 
-def own_kernel(gain_ref, wq_ref, wk_ref, wv_ref, mine_ref, theirs_ref, h_ref, kv_ref, q_ref, send_ref, h, wq, wk, wv, sems):
-    pending = fetch(sems, (h_ref, h), (wk_ref, wk), (wv_ref, wv), (wq_ref, wq))
+def tail_of(column):
+    column = jnp.concatenate([column, jnp.zeros_like(column)], axis=0)
+    row = jnp.sum(jnp.where(square_column(ROWS), column, 0.0), axis=0, keepdims=True)
+    high = row.astype(bf16).astype(f32)
+    middle = (row - high).astype(bf16).astype(f32)
+    place = lax.broadcasted_iota(jnp.int32, (16, ROWS), 0)
+    low = row - high - middle
+    rows = jnp.where(place == 0, high, jnp.where(place == 1, middle, jnp.where(place == 2, low, 0.0)))
+    return jnp.concatenate([rows, jnp.zeros((16, 2048 - ROWS), f32)], axis=1).astype(bf16)
+
+
+def power_of(tail):
+    row = jnp.sum(tail[:, :ROWS].astype(f32), axis=0, keepdims=True)
+    return jnp.sum(jnp.where(square_column(ROWS), row, 0.0), axis=1, keepdims=True)[:HALF]
+
+
+def prepare_kernel(mine_ref, theirs_ref, gain_ref, h_ref, upper_ref, lower_ref, h, sems):
+    pending = fetch(sems, (h_ref, h))
+    power = mine_ref[:1, :] + theirs_ref[:1, :]
+    column = jnp.sum(jnp.where(square_column(ROWS), power, 0.0), axis=1, keepdims=True)
+    upper_ref[HALF:, :] = tail_of(column[HALF:])
+    lower_ref[HALF:, :] = tail_of(column[:HALF])
     pending[0].wait()
-    x = normed(h[...], mine_ref[:1, :] + theirs_ref[:1, :], gain_ref[...])
+    x = normed(h[...], column, gain_ref[...])
+    upper_ref[:HALF, :] = x[:HALF]
+    lower_ref[:HALF, :] = x[HALF:]
+
+
+def own_kernel(wq_ref, wk_ref, wv_ref, upper_ref, lower_ref, kv_ref, q_ref, send_ref, wq, wk, wv, sems):
+    pending = fetch(sems, (wk_ref, wk), (wv_ref, wv), (wq_ref, wq))
+    x = jnp.concatenate([upper_ref[:HALF, :], lower_ref[:HALF, :]], axis=0)
+    pending[0].wait()
     pending[1].wait()
+    put_kv(x, wk, wv, kv_ref, send_ref)
     pending[2].wait()
-    put_kv(x, wk, wv, kv_ref, send_ref)
-    pending[3].wait()
     put_q(x, wq, q_ref, send_ref, 3 * HEAD)
 
 
-def others_kernel(n, gain_ref, wk_ref, wv_ref, *refs):
-    powers, halves = refs[:n], refs[n : 3 * n]
-    x_ref, kv_ref, send_ref, wk, wv, sems = refs[3 * n :]
+def near_kernel(wk_ref, wv_ref, gain_ref, h1u_ref, x1l_ref, x3u_ref, h3l_ref, x_ref, kv_ref, send_ref, wk, wv, sems):
     pending = fetch(sems, (wk_ref, wk), (wv_ref, wv))
-    for c in range(n):
-        h = jnp.concatenate([halves[2 * c][...], halves[2 * c + 1][...]], axis=0)
-        x_ref[c * ROWS : (c + 1) * ROWS, :] = normed(h, powers[c][:1, :], gain_ref[...])
+    x_ref[:HALF, :] = normed(h1u_ref[...], power_of(x1l_ref[HALF:, :]), gain_ref[...])
+    x_ref[HALF : 2 * HALF, :] = x1l_ref[:HALF, :]
+    x_ref[2 * HALF : 3 * HALF, :] = x3u_ref[:HALF, :]
+    x_ref[3 * HALF :, :] = normed(h3l_ref[...], power_of(x3u_ref[HALF:, :]), gain_ref[...])
+    for copy in pending:
+        copy.wait()
+    put_kv(x_ref[...], wk, wv, kv_ref, send_ref)
+
+
+def far_kernel(wk_ref, wv_ref, x2u_ref, x2l_ref, x_ref, kv_ref, send_ref, wk, wv, sems):
+    pending = fetch(sems, (wk_ref, wk), (wv_ref, wv))
+    x_ref[:HALF, :] = x2u_ref[:HALF, :]
+    x_ref[HALF:, :] = x2l_ref[:HALF, :]
     for copy in pending:
         copy.wait()
     put_kv(x_ref[...], wk, wv, kv_ref, send_ref)
@@ -207,50 +246,74 @@
     )
 
 
-def prefix_kernel(r, idx_ref, len_ref, acc_ref, max_ref, sum_ref, q_ref, pre_ref, other_ref, wo_ref, out_ref, bias_ref):
+def prefix_kernel(chunks, idx_ref, len_ref, acc_ref, max_ref, sum_ref, q_ref, pre_ref, other_ref, wo_ref, *refs):
+    bias_ref, attended_ref = refs[-2:]
     tc, ctx = idx_ref[0], idx_ref[1]
-    base = ctx * BLOCK + (tc + r) % 4 * ROWS
     lengths = len_ref[...].astype(f32)
     i = lax.broadcasted_iota(jnp.int32, (64, 1), 0)
     prefix = jnp.sum(jnp.where(i < 1, lengths, 0.0), axis=0, keepdims=True).astype(jnp.int32)
-    high = jnp.minimum(prefix, base + 1 + lax.broadcasted_iota(jnp.int32, (ROWS, 1), 0))
     lane = lax.broadcasted_iota(jnp.int32, (ROWS, ROWS), 1)
     keys, values = [], []
     for c in range(4):
         chunk = chunk_of(pre_ref, c) + chunk_of(other_ref, c)
         keys.append(chunk[:, :HEAD])
         values.append(chunk[:, HEAD:])
-        u = ((tc + c) % 4) * ROWS + lane
-        bias_ref[:, c * ROWS : (c + 1) * ROWS] = jnp.where(u < high, 0.0, MASKED)
     keys = jnp.concatenate(keys, axis=0)
     values = jnp.concatenate(values, axis=0)
-    q = stacked(chunk_of(q_ref, r))
-    s = lax.dot_general(q, keys, (((1,), (1,)), ((), ())), preferred_element_type=f32)
-    s = (s.reshape(HEADS, ROWS, BLOCK) + bias_ref[...][None]).reshape(BLOCK, BLOCK)
-    before = max_ref[r][:, :1]
-    largest = jnp.maximum(jnp.max(s, axis=1, keepdims=True), before)
-    p = jnp.exp2((s - largest) * EXPONENT)
-    factor = jnp.exp2((before - largest) * EXPONENT)
-    total = jnp.sum(p, axis=1, keepdims=True) + factor * sum_ref[r][:, :1]
-    mixed = jnp.dot(p.astype(bf16), values, preferred_element_type=f32) + factor * acc_ref[r]
-    mixed = (mixed / total).astype(bf16)
-    attended = jnp.concatenate([mixed[h * ROWS : (h + 1) * ROWS] for h in range(HEADS)], axis=1)
-    out_ref[...] = jnp.dot(attended, wo_ref[...], preferred_element_type=f32).astype(out_ref.dtype)
-
-
-def finish(r, idx, lengths, state, q, pre, wo, dtype):
+    for n, r in enumerate(chunks):
+        base = ctx * BLOCK + (tc + r) % 4 * ROWS
+        high = jnp.minimum(prefix, base + 1 + lax.broadcasted_iota(jnp.int32, (ROWS, 1), 0))
+        for c in range(4):
+            u = ((tc + c) % 4) * ROWS + lane
+            bias_ref[:, c * ROWS : (c + 1) * ROWS] = jnp.where(u < high, 0.0, MASKED)
+        q = stacked(chunk_of(q_ref, r))
+        s = lax.dot_general(q, keys, (((1,), (1,)), ((), ())), preferred_element_type=f32)
+        s = (s.reshape(HEADS, ROWS, BLOCK) + bias_ref[...][None]).reshape(BLOCK, BLOCK)
+        before = max_ref[r][:, :1]
+        largest = jnp.maximum(jnp.max(s, axis=1, keepdims=True), before)
+        p = jnp.exp2((s - largest) * EXPONENT)
+        factor = jnp.exp2((before - largest) * EXPONENT)
+        total = jnp.sum(p, axis=1, keepdims=True) + factor * sum_ref[r][:, :1]
+        mixed = jnp.dot(p.astype(bf16), values, preferred_element_type=f32) + factor * acc_ref[r]
+        mixed = (mixed / total).astype(bf16)
+        for h in range(HEADS):
+            attended_ref[n * ROWS : (n + 1) * ROWS, h * HEAD : (h + 1) * HEAD] = mixed[h * ROWS : (h + 1) * ROWS]
+    for side, columns in ((0, slice(0, SIDE)), (1, slice(SIDE, 2 * SIDE))):
+        out = jnp.dot(attended_ref[...], wo_ref[:, columns], preferred_element_type=f32)
+        for n in range(len(chunks)):
+            ref = refs[2 * n + side]
+            ref[...] = out[n * ROWS : (n + 1) * ROWS].astype(ref.dtype)
+
+
+def output_kernel(h_ref, *refs):
+    for s, (own, one, two) in ((slice(0, SIDE), refs[:3]), (slice(SIDE, 2 * SIDE), refs[3:6])):
+        total = own[...] + one[...].astype(f32) + two[...].astype(f32)
+        refs[6][:, s] = (h_ref[:, s].astype(f32) + total).astype(bf16)
+
+
+def finish(chunks, idx, lengths, state, q, pre, wo, kinds):
+    n = len(chunks)
     return call(
-        functools.partial(prefix_kernel, r), "prefix", jax.ShapeDtypeStruct((ROWS, 2048), dtype),
+        functools.partial(prefix_kernel, chunks), "prefix",
+        [jax.ShapeDtypeStruct((ROWS, SIDE), kind) for kind in kinds],
         (idx, lengths, *state, q, *pre, wo), smem=1,
-        scratch=[pltpu.VMEM((ROWS, BLOCK), f32)],
-        flops=4 * ROWS * QW * 512 + 2 * ROWS * QW * 2048, exps=4 * ROWS * 512,
-    )
-
-
-def spread_far(x, ctx):
-    at = jnp.where(ctx == 0, x, jnp.zeros_like(x))
+        scratch=[pltpu.VMEM((ROWS, BLOCK), f32), pltpu.VMEM((n * ROWS, QW), bf16)],
+        flops=n * (4 * ROWS * QW * 512 + 2 * ROWS * QW * 2048), exps=4 * n * ROWS * 512,
+    )
+
+
+def first_kernel(idx_ref, x_ref, a_ref, b_ref, c_ref, out_ref):
+    x = jnp.where(idx_ref[1] == 0, x_ref[...], jnp.zeros_like(x_ref))
+    out_ref[...] = x + a_ref[...] + b_ref[...] + c_ref[...]
+
+
+def second_kernel(x_ref, a_ref, b_ref, c_ref, out_ref):
+    out_ref[...] = x_ref[...] + a_ref[...] + b_ref[...] + c_ref[...]
+
+
+def spread_far(x, idx):
     got = [lax.ppermute(x, "ctx", [(0, 4 * z)]) for z in (2, 4, 6)]
-    at = at + got[0] + got[1] + got[2]
+    at = call(first_kernel, "first", jax.ShapeDtypeStruct(x.shape, x.dtype), (idx, x, *got), smem=1)
     return at, [lax.ppermute(at, "ctx", [(e, e + d) for e in (0, 8, 16, 24)]) for d in (4, 6, 2)]
 
 
@@ -262,19 +325,16 @@
     tc = lax.axis_index("tc")
     ctx = lax.axis_index("ctx")
     idx = jnp.stack([tc, ctx]).astype(jnp.int32)
-    upper, lower = hidden[:HALF], hidden[HALF:]
+    def shape(rows, columns, dtype):
+        return jax.ShapeDtypeStruct((rows, columns), dtype)
+
+    upper, lower, mine = call(
+        squares_kernel, "squares", [shape(HALF, 2048, bf16)] * 2 + [shape(8, ROWS, f32)], (hidden,), stay=(0,),
+        scratch=held(hidden),
+    )
     h1u = rel(upper, "tc", 4, 1)
     h3l = rel(lower, "tc", 4, 3)
-    h1l = rel(lower, "tc", 4, 1)
-    h3u = rel(upper, "tc", 4, 3)
-    h2u = rel(h1u, "tc", 4, 1)
-    h2l = rel(h3l, "tc", 4, 3)
-    mine = call(
-        squares_kernel, "squares", jax.ShapeDtypeStruct((8, ROWS), f32), (hidden,), stay=(0,),
-        scratch=held(hidden),
-    )
     theirs = rel(mine, "tr", 2, 1)
-    theirs, _, _ = lax.optimization_barrier((theirs, h1u, h3l))
     gain = norm_gain.reshape(1, -1)
     offset = (jnp.array([0, 1, 3, 2], jnp.int32) + tc) % 4 * ROWS
     positions = (ctx * BLOCK + offset[:, None] + jnp.arange(ROWS, dtype=jnp.int32)[None, :]).reshape(-1)
@@ -284,29 +344,31 @@
     sine = jnp.sin(angles) * jnp.where(jnp.arange(HEAD) < HALF, -1.0, 1.0)[None, :]
     lengths = seg_lengths.reshape(-1, 1)
 
-    def shape(rows, columns, dtype):
-        return jax.ShapeDtypeStruct((rows, columns), dtype)
-
+    xu, xl = call(
+        prepare_kernel, "prepare", [shape(TAILED, 2048, bf16)] * 2, (mine, theirs, gain, hidden), stay=(3,),
+        scratch=held(hidden), flops=ROWS * 2048 * 3,
+    )
+    x1l = rel(xl, "tc", 4, 1)
+    x3u = rel(xu, "tc", 4, 3)
     kv0, q0, send0 = call(
         own_kernel, "own", [shape(ROWS, 2 * HEAD, f32), shape(ROWS, QW, f32), shape(ROWS, 7 * HEAD, bf16)],
-        (gain, wq, wk, wv, mine, theirs, hidden), stay=(1, 2, 3, 6),
-        scratch=held(hidden, wq, wk, wv), flops=2 * ROWS * 2048 * 768,
-    )
+        (wq, wk, wv, xu, xl), stay=(0, 1, 2), scratch=held(wq, wk, wv), flops=2 * ROWS * 2048 * 768,
+    )
+    x1l, x3u, send0 = lax.optimization_barrier((x1l, x3u, send0))
+    x2l = rel(x1l, "tc", 4, 1)
+    x2u = rel(x3u, "tc", 4, 3)
     got0 = rel(send0, "tr", 2, 1)
-    power, send0 = lax.optimization_barrier((mine + theirs, send0))
-    p1, p3, p2 = [rel(power, "tc", 4, d) for d in (1, 3, 2)]
-
-    def others(powers, hs):
-        rows = ROWS * len(powers)
-        return call(
-            functools.partial(others_kernel, len(powers)), "others",
-            [shape(rows, 2048, bf16), shape(rows, 2 * HEAD, f32), shape(rows, 3 * HEAD, bf16)],
-            (gain, wk, wv, *powers, *hs), stay=(1, 2), scratch=held(wk, wv), flops=2 * rows * 2048 * 256,
-        )
-
-    x13, kv13, send13 = others((p1, p3), (h1u, h1l, h3u, h3l))
+    x13, kv13, send13 = call(
+        near_kernel, "near",
+        [shape(2 * ROWS, 2048, bf16), shape(2 * ROWS, 2 * HEAD, f32), shape(2 * ROWS, 3 * HEAD, bf16)],
+        (wk, wv, gain, h1u, x1l, x3u, h3l), stay=(0, 1), scratch=held(wk, wv), flops=4 * ROWS * 2048 * 256,
+    )
     got13 = rel(send13, "tr", 2, 1)
-    x2, kv2, send2 = others((p2,), (h2u, h2l))
+    x2, kv2, send2 = call(
+        far_kernel, "far",
+        [shape(ROWS, 2048, bf16), shape(ROWS, 2 * HEAD, f32), shape(ROWS, 3 * HEAD, bf16)],
+        (wk, wv, x2u, x2l), stay=(0, 1), scratch=held(wk, wv), flops=2 * ROWS * 2048 * 256,
+    )
     got2 = rel(send2, "tr", 2, 1)
     q1, send_q = call(
         q_kernel, "q", [shape(3 * ROWS, QW, f32), shape(3 * ROWS, QW, bf16)], (x13, x2, wq),
@@ -319,22 +381,26 @@
         flops=BLOCK * 256 * 8,
     )
     prev = lax.ppermute(kv, "ctx", [(i, i + 1) for i in range(lax.axis_size("ctx") - 1)])
-    at, got = spread_far(kv, ctx)
+    at, got = spread_far(kv, idx)
     q = call(
         rotary_q_kernel, "rotary_q", shape(BLOCK, QW, bf16), (q0, got0, q1, got_q, cosine, sine),
         flops=BLOCK * 512 * 8,
     )
-    got, q, prev = lax.optimization_barrier((got, q, prev))
-    at = at + got[0] + got[1] + got[2]
+    state = local(idx, lengths, q, kv, prev)
+    got, state = lax.optimization_barrier((got, state))
+    at = call(second_kernel, "second", shape(BLOCK, 2 * HEAD, bf16), (at, *got))
     pre = (at, lax.ppermute(at, "ctx", [(2 * i, 2 * i + 1) for i in range(lax.axis_size("ctx") // 2)]))
-    state = local(idx, lengths, q, kv, prev)
-    parts = {}
-    for r in (2, 1, 3, 0):
-        parts[r] = finish(r, idx, lengths, state, q, pre, wo, f32 if r == 0 else bf16)
-    total = parts[0]
-    for r in (1, 3, 2):
-        total = total + rel(parts[r], "tc", 4, -r).astype(f32)
-    return (hidden.astype(f32) + total).astype(bf16)
+    args = (idx, lengths, state, q, pre, wo)
+    left2, right2, left1, right1, left3, right3 = finish((2, 1, 3), *args, (bf16, bf16, f32, bf16, bf16, f32))
+    left2, right2 = rel(left2, "tc", 4, -1), rel(right2, "tc", 4, 1)
+    right1, left3 = rel(right1, "tc", 4, -1), rel(left3, "tc", 4, 1)
+    left1 = rel((left1 + left2.astype(f32)).astype(bf16), "tc", 4, -1)
+    right3 = rel((right3 + right2.astype(f32)).astype(bf16), "tc", 4, 1)
+    left0, right0 = finish((0,), *args, (f32, f32))
+    return call(
+        output_kernel, "output", shape(ROWS, 2048, bf16),
+        (hidden, left0, left1, left3, right0, right1, right3), flops=ROWS * 2048 * 3,
+    )
 
 
 def solution(mesh):

time: 107 us -> 97.3 us (0.909)
  the two profiles are of different devices: /device:TPU:102 before, /device:TPU:1 now
where the time goes in v3:
time: 97.3 us; the launch traced here: 96.8 us
  starting transfers between devices  35.9 us (37%)
  waiting for transfers between devices  34.7 us (36%)
  Pallas kernels  23.2 us (24%)
  other arithmetic  2.01 us (2%)
    ppermute x17, starting transfers between devices, rel(): return lax.ppermute(x, axis, [((i + distance) % n, i) for i in range(n)])  24.9 us
    pallas_call x14, Pallas kernels, call(): pl.pallas_call(kernel, out_shape=out_shape, in_specs=[spec(w) for w in wh...  23.2 us
    ppermute x17, waiting for transfers between devices, rel(): return lax.ppermute(x, axis, [((i + distance) % n, i) for i in range(n)])  21.9 us
    ppermute x1, waiting for transfers between devices, per_device(): lax.ppermute(at, 'ctx', [(2 * i, 2 * i + 1) for i in range(lax.axis_size(...  6.82 us
    ppermute x1, waiting for transfers between devices, per_device(): lax.ppermute(kv, 'ctx', [(i, i + 1) for i in range(lax.axis_size('ctx') -...  5.88 us
    ppermute x1, starting transfers between devices, per_device(): lax.ppermute(kv, 'ctx', [(i, i + 1) for i in range(lax.axis_size('ctx') -...  5.41 us
    ppermute x3, starting transfers between devices, spread_far(): lax.ppermute(at, 'ctx', [(e, e + d) for e in (0, 8, 16, 24)])  2.21 us
    ppermute x3, starting transfers between devices, spread_far(): got = [lax.ppermute(x, 'ctx', [(0, 4 * z)]) for z in (2, 4, 6)]  2.03 us
  transfers between devices with their start and end apart: 25, of which 10 were waited for; matrix products, arithmetic and copies ran while one was open for 2% of the time, Pallas kernels for 18%

profile of v3, /device:TPU:1, one launch (start us, length us, event | category | flops | bytes accessed | tf_op | source)
XLA Modules:
  0.0 96.8 jit_solution(15157240500108798877)
XLA Ops:
  1.3 3.8 %collective-permute-start = (f32[8,128]{1,0:T(8,128)S(1)}, f32[8,128]{1,0:T(8,128)S(1)}, u32[]{:S(2)}, u32[]{:S(2)}) collective-permute-start(f32[8,128]{1,0:T(8,128)S(1)} %get-tuple-element.42.mine_ref), channel_id=1, source_target_pairs={{4,0},{0,4},{5,1},{1,5},{6,2},{2,6},{7,3},{3,7},{12,8},{8,12},{13,... | collective-permute-start | bytes 12296 | tf_op jit(solution)/shard_map/ppermute | solution.py:34
  5.1 2.5 %collective-permute-start.4 = (bf16[64,2048]{1,0:T(8,128)(2,1)S(1)}, bf16[64,2048]{1,0:T(8,128)(2,1)S(1)}, u32[]{:S(2)}, u32[]{:S(2)}) collective-permute-start(bf16[64,2048]{1,0:T(8,128)(2,1)S(1)} %get-tuple-element.48), channel_id=1, source_target_pairs={{1,0},{2,1},{3,2},{0,3},{5,4},{6,5},{7,6},{4,7},{9,8},{10,9},{11,1... | collective-permute-start | bytes 786440 | tf_op jit(solution)/shard_map/ppermute | solution.py:34
  9.5 2.8 %collective-permute-start.1 = (bf16[80,2048]{1,0:T(8,128)(2,1)S(1)}, bf16[80,2048]{1,0:T(8,128)(2,1)S(1)}, u32[]{:S(2)}, u32[]{:S(2)}) collective-permute-start(bf16[80,2048]{1,0:T(8,128)(2,1)S(1)} %get-tuple-element.44.lower_ref), channel_id=1, source_target_pairs={{1,0},{2,1},{3,2},{0,3},{5,4},{6,5},{7,6},{4,7},{9,8},{10,9},{11,1... | collective-permute-start | bytes 983048 | tf_op jit(solution)/shard_map/ppermute | solution.py:34
  12.9 2.4 %own.1 = (f32[128,256]{1,0:T(8,128)S(1)}, f32[128,512]{1,0:T(8,128)S(1)}, bf16[128,896]{1,0:T(8,128)(2,1)S(1)}) custom-call(bf16[2048,512]{1,0:T(8,128)(2,1)} %wq_ref.3, bf16[2048,128]{1,0:T(8,128)(2,1)} %wk_ref.5, bf16[2048,128]{1,0:T(8,128)(2,1)} %wv_ref.5, bf16[80,2048]{1,0:T(8,128)(2,1)S(1)} %get-tuple-element.43.upper_ref, ...), custom_call_target="tpu_custom_call" | custom-call | flops 402653184 | bytes 4194304 | tf_op jit(solution)/shard_map/own/pallas_call | solution.py:41
  15.3 4.3 %collective-permute-done.1.x1l_ref = bf16[80,2048]{1,0:T(8,128)(2,1)S(1)} collective-permute-done((bf16[80,2048]{1,0:T(8,128)(2,1)S(1)}, bf16[80,2048]{1,0:T(8,128)(2,1)S(1)}, u32[]{:S(2)}, u32[]{:S(2)}) %collective-permute-start.1) | collective-permute-done | bytes 327712 | tf_op jit(solution)/shard_map/ppermute | solution.py:34
  19.6 3.1 %collective-permute-done.2.x3u_ref = bf16[80,2048]{1,0:T(8,128)(2,1)S(1)} collective-permute-done((bf16[80,2048]{1,0:T(8,128)(2,1)S(1)}, bf16[80,2048]{1,0:T(8,128)(2,1)S(1)}, u32[]{:S(2)}, u32[]{:S(2)}) %collective-permute-start.2) | collective-permute-done | bytes 327712 | tf_op jit(solution)/shard_map/ppermute | solution.py:34
  22.8 2.7 %collective-permute-start.8 = (bf16[80,2048]{1,0:T(8,128)(2,1)S(1)}, bf16[80,2048]{1,0:T(8,128)(2,1)S(1)}, u32[]{:S(2)}, u32[]{:S(2)}) collective-permute-start(bf16[80,2048]{1,0:T(8,128)(2,1)S(1)} %collective-permute-done.1.x1l_ref), channel_id=1, source_target_pairs={{1,0},{2,1},{3,2},{0,3},{5,4},{6,5},{7,6},{4,7},{9,8},{10,9},{11,1... | collective-permute-start | bytes 983048 | tf_op jit(solution)/shard_map/ppermute | solution.py:34
  25.6 1.9 %near.1 = (bf16[256,2048]{1,0:T(8,128)(2,1)S(1)}, f32[256,256]{1,0:T(8,128)S(1)}, bf16[256,384]{1,0:T(8,128)(2,1)S(1)}) custom-call(bf16[2048,128]{1,0:T(8,128)(2,1)} %wk_ref.5, bf16[2048,128]{1,0:T(8,128)(2,1)} %wv_ref.5, f32[1,2048]{1,0:T(1,128)S(1)} %bitcast.7, bf16[64,2048]{1,0:T(8,128)(2,1)S(1)} %collective-permute-done.4.h1u_ref, ...), custom_call_target="tpu_custom_call" | custom-call | flops 268435456 | bytes 4194304 | tf_op jit(solution)/shard_map/near/pallas_call | solution.py:41
  27.5 3.0 %collective-permute-start.6 = (bf16[256,384]{1,0:T(8,128)(2,1)S(1)}, bf16[256,384]{1,0:T(8,128)(2,1)S(1)}, u32[]{:S(2)}, u32[]{:S(2)}) collective-permute-start(bf16[256,384]{1,0:T(8,128)(2,1)S(1)} %get-tuple-element.53), channel_id=1, source_target_pairs={{4,0},{0,4},{5,1},{1,5},{6,2},{2,6},{7,3},{3,7},{12,8},{8,12},{13,... | collective-permute-start | bytes 589832 | tf_op jit(solution)/shard_map/ppermute | solution.py:34
  34.2 3.3 %q.1 = (f32[384,512]{1,0:T(8,128)S(1)}, bf16[384,512]{1,0:T(8,128)(2,1)}) custom-call(bf16[256,2048]{1,0:T(8,128)(2,1)S(1)} %get-tuple-element.56.xa_ref, bf16[128,2048]{1,0:T(8,128)(2,1)S(1)} %get-tuple-element.57.xb_ref, bf16[2048,512]{1,0:T(8,128)(2,1)} %wq_ref.3), custom_call_target="tpu_custom_call" | custom-call | flops 805306368 | bytes 4194304 | tf_op jit(solution)/shard_map/q/pallas_call | solution.py:41
  37.5 2.0 %collective-permute-done.9.gotb_ref = bf16[128,384]{1,0:T(8,128)(2,1)S(1)} collective-permute-done((bf16[128,384]{1,0:T(8,128)(2,1)S(1)}, bf16[128,384]{1,0:T(8,128)(2,1)S(1)}, u32[]{:S(2)}, u32[]{:S(2)}) %collective-permute-start.9) | collective-permute-done | bytes 98336 | tf_op jit(solution)/shard_map/ppermute | solution.py:34
  42.8 5.4 %collective-permute-start.17 = (bf16[512,256]{1,0:T(8,128)(2,1)S(1)}, bf16[512,256]{1,0:T(8,128)(2,1)}, u32[]{:S(2)}, u32[]{:S(2)}) collective-permute-start(bf16[512,256]{1,0:T(8,128)(2,1)S(1)} %rotary_kv.1.x_ref.own_ref), channel_id=1, source_target_pairs={{0,8},{8,16},{16,24},{24,32},{32,40},{40,48},{48,56},{56,64},{64,7... | collective-permute-start | bytes 786440 | tf_op jit(solution)/shard_map/ppermute | solution.py:383
  51.7 5.9 %collective-permute-done.17.prev_ref = bf16[512,256]{1,0:T(8,128)(2,1)} collective-permute-done((bf16[512,256]{1,0:T(8,128)(2,1)S(1)}, bf16[512,256]{1,0:T(8,128)(2,1)}, u32[]{:S(2)}, u32[]{:S(2)}) %collective-permute-start.17) | collective-permute-done | bytes 262176 | tf_op jit(solution)/shard_map/ppermute | solution.py:383
  57.5 3.8 %local.1 = (f32[4,512,128]{2,1,0:T(8,128)S(1)}, f32[4,512,128]{2,1,0:T(8,128)S(1)}, f32[4,512,128]{2,1,0:T(8,128)S(1)}) custom-call(s32[2]{0:T(128)S(1)} %pad_add_fusion.idx_ref, s32[64,1]{1,0:T(8,128)S(1)} %copy.10.len_ref, bf16[512,512]{1,0:T(8,128)(2,1)S(1)} %rotary_q.1.q_ref, bf16[512,256]{1,0:T(8,128)(2,1)S(1)} %rotary_kv.1.x_ref.own_ref, ...), custom_call_target="tpu_custom_call" | custom-call | flops 671088640 | bytes 4194304 | tf_op jit(solution)/shard_map/local/pallas_call | solution.py:41
  62.7 6.8 %collective-permute-done.18.other_ref = bf16[512,256]{1,0:T(8,128)(2,1)S(1)} collective-permute-done((bf16[512,256]{1,0:T(8,128)(2,1)S(1)}, bf16[512,256]{1,0:T(8,128)(2,1)S(1)}, u32[]{:S(2)}, u32[]{:S(2)}) %collective-permute-start.18) | collective-permute-done | bytes 262176 | tf_op jit(solution)/shard_map/ppermute | solution.py:392
  69.5 3.6 %prefix.3 = (bf16[128,1024]{1,0:T(8,128)(2,1)S(1)}, bf16[128,1024]{1,0:T(8,128)(2,1)S(1)}, f32[128,1024]{1,0:T(8,128)S(1)}, bf16[128,1024]{1,0:T(8,128)(2,1)S(1)...) custom-call(s32[2]{0:T(128)S(1)} %pad_add_fusion.idx_ref, s32[64,1]{1,0:T(8,128)S(1)} %copy.10.len_ref, ...), custom_call_target="tpu_custom_call" | custom-call | flops 1207959552 | bytes 4194304 | tf_op jit(solution)/shard_map/prefix/pallas_call | solution.py:41
  73.1 2.8 %collective-permute-start.23 = (bf16[128,1024]{1,0:T(8,128)(2,1)S(1)}, bf16[128,1024]{1,0:T(8,128)(2,1)S(1)}, u32[]{:S(2)}, u32[]{:S(2)}) collective-permute-start(bf16[128,1024]{1,0:T(8,128)(2,1)S(1)} %get-tuple-element.78), channel_id=1, source_target_pairs={{1,0},{2,1},{3,2},{0,3},{5,4},{6,5},{7,6},{4,7},{9,8},{10,9},{11,1... | collective-permute-start | bytes 786440 | tf_op jit(solution)/shard_map/ppermute | solution.py:34
  75.8 2.7 %collective-permute-start.21 = (bf16[128,1024]{1,0:T(8,128)(2,1)S(1)}, bf16[128,1024]{1,0:T(8,128)(2,1)S(1)}, u32[]{:S(2)}, u32[]{:S(2)}) collective-permute-start(bf16[128,1024]{1,0:T(8,128)(2,1)S(1)} %get-tuple-element.74), channel_id=1, source_target_pairs={{1,0},{2,1},{3,2},{0,3},{5,4},{6,5},{7,6},{4,7},{9,8},{10,9},{11,1... | collective-permute-start | bytes 786440 | tf_op jit(solution)/shard_map/ppermute | solution.py:34
  78.5 2.9 %collective-permute-done.23 = bf16[128,1024]{1,0:T(8,128)(2,1)S(1)} collective-permute-done((bf16[128,1024]{1,0:T(8,128)(2,1)S(1)}, bf16[128,1024]{1,0:T(8,128)(2,1)S(1)}, u32[]{:S(2)}, u32[]{:S(2)}) %collective-permute-start.23) | collective-permute-done | bytes 262176 | tf_op jit(solution)/shard_map/ppermute | solution.py:34
  81.5 3.5 %collective-permute-start.24 = (bf16[128,1024]{1,0:T(8,128)(2,1)S(1)}, bf16[128,1024]{1,0:T(8,128)(2,1)S(1)}, u32[]{:S(2)}, u32[]{:S(2)}) collective-permute-start(bf16[128,1024]{1,0:T(8,128)(2,1)S(1)} %add_convert_fusion), channel_id=1, source_target_pairs={{1,0},{2,1},{3,2},{0,3},{5,4},{6,5},{7,6},{4,7},{9,8},{10,9},{11,1... | collective-permute-start | bytes 786440 | tf_op jit(solution)/shard_map/ppermute | solution.py:34
  85.1 1.9 %prefix.2 = (f32[128,1024]{1,0:T(8,128)S(1)}, f32[128,1024]{1,0:T(8,128)S(1)}) custom-call(s32[2]{0:T(128)S(1)} %pad_add_fusion.idx_ref, s32[64,1]{1,0:T(8,128)S(1)} %copy.10.len_ref, f32[4,512,128]{2,1,0:T(8,128)S(1)} %get-tuple-element.65.acc_ref, f32[4,512,128]{2,1,0:T(8,128)S(1)} %get-tuple-element.66.max_ref, ...), custom_call_target="tpu_custom_call" | custom-call | flops 402653184 | bytes 4194304 | tf_op jit(solution)/shard_map/prefix/pallas_call | solution.py:41
  87.0 3.1 %collective-permute-done.22.refs_4_ = bf16[128,1024]{1,0:T(8,128)(2,1)S(1)} collective-permute-done((bf16[128,1024]{1,0:T(8,128)(2,1)S(1)}, bf16[128,1024]{1,0:T(8,128)(2,1)S(1)}, u32[]{:S(2)}, u32[]{:S(2)}) %collective-permute-start.22) | collective-permute-done | bytes 262176 | tf_op jit(solution)/shard_map/ppermute | solution.py:34
  90.1 2.5 %collective-permute-done.24.refs_5_ = bf16[128,1024]{1,0:T(8,128)(2,1)S(1)} collective-permute-done((bf16[128,1024]{1,0:T(8,128)(2,1)S(1)}, bf16[128,1024]{1,0:T(8,128)(2,1)S(1)}, u32[]{:S(2)}, u32[]{:S(2)}) %collective-permute-start.24) | collective-permute-done | bytes 262176 | tf_op jit(solution)/shard_map/ppermute | solution.py:34
  92.6 3.1 %collective-permute-done.20.refs_1_ = bf16[128,1024]{1,0:T(8,128)(2,1)S(1)} collective-permute-done((bf16[128,1024]{1,0:T(8,128)(2,1)S(1)}, bf16[128,1024]{1,0:T(8,128)(2,1)S(1)}, u32[]{:S(2)}, u32[]{:S(2)}) %collective-permute-start.20) | collective-permute-done | bytes 262176 | tf_op jit(solution)/shard_map/ppermute | solution.py:34
  (57 shorter events, 16.8 us)
Async XLA Ops:
  5.1 20.5 %collective-permute-start.4 = (bf16[64,2048]{1,0:T(8,128)(2,1)S(1)}, bf16[64,2048]{1,0:T(8,128)(2,1)S(1)}, u32[]{:S(2)}, u32[]{:S(2)}) collective-permute-start(bf16[64,2048]{1,0:T(8,128)(2,1)S(1)} %get-tuple-element.48), channel_id=1, source_target_pairs={{1,0},{2,1},{3,2},{0,3},{5,4},{6,5},{7,6},{4,7},{9,8},{10,9},{11,1... | collective-permute-start | bytes 786440 | tf_op jit(solution)/shard_map/ppermute | solution.py:34
  7.6 18.0 %collective-permute-start.5 = (bf16[64,2048]{1,0:T(8,128)(2,1)S(1)}, bf16[64,2048]{1,0:T(8,128)(2,1)S(1)}, u32[]{:S(2)}, u32[]{:S(2)}) collective-permute-start(bf16[64,2048]{1,0:T(8,128)(2,1)S(1)} %get-tuple-element.51), channel_id=1, source_target_pairs={{3,0},{0,1},{1,2},{2,3},{7,4},{4,5},{5,6},{6,7},{11,8},{8,9},{9,10... | collective-permute-start | bytes 786440 | tf_op jit(solution)/shard_map/ppermute | solution.py:34
  9.5 10.2 %collective-permute-start.1 = (bf16[80,2048]{1,0:T(8,128)(2,1)S(1)}, bf16[80,2048]{1,0:T(8,128)(2,1)S(1)}, u32[]{:S(2)}, u32[]{:S(2)}) collective-permute-start(bf16[80,2048]{1,0:T(8,128)(2,1)S(1)} %get-tuple-element.44.lower_ref), channel_id=1, source_target_pairs={{1,0},{2,1},{3,2},{0,3},{5,4},{6,5},{7,6},{4,7},{9,8},{10,9},{11,1... | collective-permute-start | bytes 983048 | tf_op jit(solution)/shard_map/ppermute | solution.py:34
  12.2 10.6 %collective-permute-start.2 = (bf16[80,2048]{1,0:T(8,128)(2,1)S(1)}, bf16[80,2048]{1,0:T(8,128)(2,1)S(1)}, u32[]{:S(2)}, u32[]{:S(2)}) collective-permute-start(bf16[80,2048]{1,0:T(8,128)(2,1)S(1)} %get-tuple-element.43.upper_ref), channel_id=1, source_target_pairs={{3,0},{0,1},{1,2},{2,3},{7,4},{4,5},{5,6},{6,7},{11,8},{8,9},{9,10... | collective-permute-start | bytes 983048 | tf_op jit(solution)/shard_map/ppermute | solution.py:34
  22.8 8.7 %collective-permute-start.7 = (bf16[80,2048]{1,0:T(8,128)(2,1)S(1)}, bf16[80,2048]{1,0:T(8,128)(2,1)S(1)}, u32[]{:S(2)}, u32[]{:S(2)}) collective-permute-start(bf16[80,2048]{1,0:T(8,128)(2,1)S(1)} %collective-permute-done.2.x3u_ref), channel_id=1, source_target_pairs={{3,0},{0,1},{1,2},{2,3},{7,4},{4,5},{5,6},{6,7},{11,8},{8,9},{9,10... | collective-permute-start | bytes 983048 | tf_op jit(solution)/shard_map/ppermute | solution.py:34
  22.8 8.7 %collective-permute-start.8 = (bf16[80,2048]{1,0:T(8,128)(2,1)S(1)}, bf16[80,2048]{1,0:T(8,128)(2,1)S(1)}, u32[]{:S(2)}, u32[]{:S(2)}) collective-permute-start(bf16[80,2048]{1,0:T(8,128)(2,1)S(1)} %collective-permute-done.1.x1l_ref), channel_id=1, source_target_pairs={{1,0},{2,1},{3,2},{0,3},{5,4},{6,5},{7,6},{4,7},{9,8},{10,9},{11,1... | collective-permute-start | bytes 983048 | tf_op jit(solution)/shard_map/ppermute | solution.py:34
  25.6 14.0 %collective-permute-start.3 = (bf16[128,896]{1,0:T(8,128)(2,1)S(1)}, bf16[128,896]{1,0:T(8,128)(2,1)S(1)}, u32[]{:S(2)}, u32[]{:S(2)}) collective-permute-start(bf16[128,896]{1,0:T(8,128)(2,1)S(1)} %get-tuple-element.47), channel_id=1, source_target_pairs={{4,0},{0,4},{5,1},{1,5},{6,2},{2,6},{7,3},{3,7},{12,8},{8,12},{13,... | collective-permute-start | bytes 688136 | tf_op jit(solution)/shard_map/ppermute | solution.py:34
  27.5 12.0 %collective-permute-start.6 = (bf16[256,384]{1,0:T(8,128)(2,1)S(1)}, bf16[256,384]{1,0:T(8,128)(2,1)S(1)}, u32[]{:S(2)}, u32[]{:S(2)}) collective-permute-start(bf16[256,384]{1,0:T(8,128)(2,1)S(1)} %get-tuple-element.53), channel_id=1, source_target_pairs={{4,0},{0,4},{5,1},{1,5},{6,2},{2,6},{7,3},{3,7},{12,8},{8,12},{13,... | collective-permute-start | bytes 589832 | tf_op jit(solution)/shard_map/ppermute | solution.py:34
  33.1 6.5 %collective-permute-start.9 = (bf16[128,384]{1,0:T(8,128)(2,1)S(1)}, bf16[128,384]{1,0:T(8,128)(2,1)S(1)}, u32[]{:S(2)}, u32[]{:S(2)}) collective-permute-start(bf16[128,384]{1,0:T(8,128)(2,1)S(1)} %get-tuple-element.55), channel_id=1, source_target_pairs={{4,0},{0,4},{5,1},{1,5},{6,2},{2,6},{7,3},{3,7},{12,8},{8,12},{13,... | collective-permute-start | bytes 294920 | tf_op jit(solution)/shard_map/ppermute | solution.py:34
  39.7 8.6 %collective-permute-start.10 = (bf16[512,256]{1,0:T(8,128)(2,1)S(1)}, bf16[512,256]{1,0:T(8,128)(2,1)S(1)}, u32[]{:S(2)}, u32[]{:S(2)}) collective-permute-start(bf16[512,256]{1,0:T(8,128)(2,1)S(1)} %rotary_kv.1.x_ref.own_ref), channel_id=1, source_target_pairs={{0,64},{1,65},{2,66},{3,67},{4,68},{5,69},{6,70},{7,71}} | collective-permute-start | bytes 786440 | tf_op jit(solution)/shard_map/ppermute | solution.py:315
  40.4 7.9 %collective-permute-start.11 = (bf16[512,256]{1,0:T(8,128)(2,1)S(1)}, bf16[512,256]{1,0:T(8,128)(2,1)S(1)}, u32[]{:S(2)}, u32[]{:S(2)}) collective-permute-start(bf16[512,256]{1,0:T(8,128)(2,1)S(1)} %rotary_kv.1.x_ref.own_ref), channel_id=1, source_target_pairs={{0,128},{1,129},{2,130},{3,131},{4,132},{5,133},{6,134},{7,135}} | collective-permute-start | bytes 786440 | tf_op jit(solution)/shard_map/ppermute | solution.py:315
  41.1 7.2 %collective-permute-start.12 = (bf16[512,256]{1,0:T(8,128)(2,1)S(1)}, bf16[512,256]{1,0:T(8,128)(2,1)S(1)}, u32[]{:S(2)}, u32[]{:S(2)}) collective-permute-start(bf16[512,256]{1,0:T(8,128)(2,1)S(1)} %rotary_kv.1.x_ref.own_ref), channel_id=1, source_target_pairs={{0,192},{1,193},{2,194},{3,195},{4,196},{5,197},{6,198},{7,199}} | collective-permute-start | bytes 786440 | tf_op jit(solution)/shard_map/ppermute | solution.py:315
  41.8 9.5 %collective-permute-start.16 = (bf16[384,512]{1,0:T(8,128)(2,1)}, bf16[384,512]{1,0:T(8,128)(2,1)S(1)}, u32[]{:S(2)}, u32[]{:S(2)}) collective-permute-start(bf16[384,512]{1,0:T(8,128)(2,1)} %get-tuple-element.58), channel_id=1, source_target_pairs={{4,0},{0,4},{5,1},{1,5},{6,2},{2,6},{7,3},{3,7},{12,8},{8,12},{13,... | collective-permute-start | bytes 1179656 | tf_op jit(solution)/shard_map/ppermute | solution.py:34
  42.8 14.7 %collective-permute-start.17 = (bf16[512,256]{1,0:T(8,128)(2,1)S(1)}, bf16[512,256]{1,0:T(8,128)(2,1)}, u32[]{:S(2)}, u32[]{:S(2)}) collective-permute-start(bf16[512,256]{1,0:T(8,128)(2,1)S(1)} %rotary_kv.1.x_ref.own_ref), channel_id=1, source_target_pairs={{0,8},{8,16},{16,24},{24,32},{32,40},{40,48},{48,56},{56,64},{64,7... | collective-permute-start | bytes 786440 | tf_op jit(solution)/shard_map/ppermute | solution.py:383
  48.9 12.4 %collective-permute-start.13 = (bf16[512,256]{1,0:T(8,128)(2,1)S(1)}, bf16[512,256]{1,0:T(8,128)(2,1)S(1)}, u32[]{:S(2)}, u32[]{:S(2)}) collective-permute-start(bf16[512,256]{1,0:T(8,128)(2,1)S(1)} %first.1.x_ref), channel_id=1, source_target_pairs={{0,32},{64,96},{128,160},{192,224},{1,33},{65,97},{129,161},{193,2... | collective-permute-start | bytes 786440 | tf_op jit(solution)/shard_map/ppermute | solution.py:317
  49.6 11.7 %collective-permute-start.14 = (bf16[512,256]{1,0:T(8,128)(2,1)S(1)}, bf16[512,256]{1,0:T(8,128)(2,1)S(1)}, u32[]{:S(2)}, u32[]{:S(2)}) collective-permute-start(bf16[512,256]{1,0:T(8,128)(2,1)S(1)} %first.1.x_ref), channel_id=1, source_target_pairs={{0,48},{64,112},{128,176},{192,240},{1,49},{65,113},{129,177},{193... | collective-permute-start | bytes 786440 | tf_op jit(solution)/shard_map/ppermute | solution.py:317
  50.3 11.0 %collective-permute-start.15 = (bf16[512,256]{1,0:T(8,128)(2,1)S(1)}, bf16[512,256]{1,0:T(8,128)(2,1)S(1)}, u32[]{:S(2)}, u32[]{:S(2)}) collective-permute-start(bf16[512,256]{1,0:T(8,128)(2,1)S(1)} %first.1.x_ref), channel_id=1, source_target_pairs={{0,16},{64,80},{128,144},{192,208},{1,17},{65,81},{129,145},{193,2... | collective-permute-start | bytes 786440 | tf_op jit(solution)/shard_map/ppermute | solution.py:317
  61.4 8.1 %collective-permute-start.18 = (bf16[512,256]{1,0:T(8,128)(2,1)S(1)}, bf16[512,256]{1,0:T(8,128)(2,1)S(1)}, u32[]{:S(2)}, u32[]{:S(2)}) collective-permute-start(bf16[512,256]{1,0:T(8,128)(2,1)S(1)} %second.1.pre_ref), channel_id=1, source_target_pairs={{0,8},{16,24},{32,40},{48,56},{64,72},{80,88},{96,104},{112,120},{... | collective-permute-start | bytes 786440 | tf_op jit(solution)/shard_map/ppermute | solution.py:392
  73.1 8.3 %collective-permute-start.23 = (bf16[128,1024]{1,0:T(8,128)(2,1)S(1)}, bf16[128,1024]{1,0:T(8,128)(2,1)S(1)}, u32[]{:S(2)}, u32[]{:S(2)}) collective-permute-start(bf16[128,1024]{1,0:T(8,128)(2,1)S(1)} %get-tuple-element.78), channel_id=1, source_target_pairs={{1,0},{2,1},{3,2},{0,3},{5,4},{6,5},{7,6},{4,7},{9,8},{10,9},{11,1... | collective-permute-start | bytes 786440 | tf_op jit(solution)/shard_map/ppermute | solution.py:34
  75.8 9.1 %collective-permute-start.19 = (bf16[128,1024]{1,0:T(8,128)(2,1)S(1)}, bf16[128,1024]{1,0:T(8,128)(2,1)S(1)}, u32[]{:S(2)}, u32[]{:S(2)}) collective-permute-start(bf16[128,1024]{1,0:T(8,128)(2,1)S(1)} %get-tuple-element.73), channel_id=1, source_target_pairs={{3,0},{0,1},{1,2},{2,3},{7,4},{4,5},{5,6},{6,7},{11,8},{8,9},{9,10... | collective-permute-start | bytes 786440 | tf_op jit(solution)/shard_map/ppermute | solution.py:34
  75.8 11.2 %collective-permute-start.21 = (bf16[128,1024]{1,0:T(8,128)(2,1)S(1)}, bf16[128,1024]{1,0:T(8,128)(2,1)S(1)}, u32[]{:S(2)}, u32[]{:S(2)}) collective-permute-start(bf16[128,1024]{1,0:T(8,128)(2,1)S(1)} %get-tuple-element.74), channel_id=1, source_target_pairs={{1,0},{2,1},{3,2},{0,3},{5,4},{6,5},{7,6},{4,7},{9,8},{10,9},{11,1... | collective-permute-start | bytes 786440 | tf_op jit(solution)/shard_map/ppermute | solution.py:34
  78.5 11.6 %collective-permute-start.22 = (bf16[128,1024]{1,0:T(8,128)(2,1)S(1)}, bf16[128,1024]{1,0:T(8,128)(2,1)S(1)}, u32[]{:S(2)}, u32[]{:S(2)}) collective-permute-start(bf16[128,1024]{1,0:T(8,128)(2,1)S(1)} %get-tuple-element.76), channel_id=1, source_target_pairs={{3,0},{0,1},{1,2},{2,3},{7,4},{4,5},{5,6},{6,7},{11,8},{8,9},{9,10... | collective-permute-start | bytes 786440 | tf_op jit(solution)/shard_map/ppermute | solution.py:34
  81.5 11.2 %collective-permute-start.24 = (bf16[128,1024]{1,0:T(8,128)(2,1)S(1)}, bf16[128,1024]{1,0:T(8,128)(2,1)S(1)}, u32[]{:S(2)}, u32[]{:S(2)}) collective-permute-start(bf16[128,1024]{1,0:T(8,128)(2,1)S(1)} %add_convert_fusion), channel_id=1, source_target_pairs={{1,0},{2,1},{3,2},{0,3},{5,4},{6,5},{7,6},{4,7},{9,8},{10,9},{11,1... | collective-permute-start | bytes 786440 | tf_op jit(solution)/shard_map/ppermute | solution.py:34
  85.0 10.7 %collective-permute-start.20 = (bf16[128,1024]{1,0:T(8,128)(2,1)S(1)}, bf16[128,1024]{1,0:T(8,128)(2,1)S(1)}, u32[]{:S(2)}, u32[]{:S(2)}) collective-permute-start(bf16[128,1024]{1,0:T(8,128)(2,1)S(1)} %add_convert_fusion.1), channel_id=1, source_target_pairs={{3,0},{0,1},{1,2},{2,3},{7,4},{4,5},{5,6},{6,7},{11,8},{8,9},{9,10... | collective-permute-start | bytes 786440 | tf_op jit(solution)/shard_map/ppermute | solution.py:34
  (5 other events, 49.3 us)

commit v4 on v3

--- a/solution.py
+++ b/solution.py
@@ -108,9 +108,10 @@
     return jnp.sum(jnp.where(square_column(ROWS), row, 0.0), axis=1, keepdims=True)[:HALF]
 
 
-def prepare_kernel(mine_ref, theirs_ref, gain_ref, h_ref, upper_ref, lower_ref, h, sems):
+def prepare_kernel(mine_ref, theirs_ref, gain_ref, h_ref, upper_ref, lower_ref, power_ref, h, sems):
     pending = fetch(sems, (h_ref, h))
     power = mine_ref[:1, :] + theirs_ref[:1, :]
+    power_ref[...] = jnp.broadcast_to(power, (8, ROWS))
     column = jnp.sum(jnp.where(square_column(ROWS), power, 0.0), axis=1, keepdims=True)
     upper_ref[HALF:, :] = tail_of(column[HALF:])
     lower_ref[HALF:, :] = tail_of(column[:HALF])
@@ -141,21 +142,21 @@
     put_kv(x_ref[...], wk, wv, kv_ref, send_ref)
 
 
-def far_kernel(wk_ref, wv_ref, x2u_ref, x2l_ref, x_ref, kv_ref, send_ref, wk, wv, sems):
+def far_kernel(wk_ref, wv_ref, gain_ref, power_ref, h2u_ref, h2l_ref, x_ref, kv_ref, send_ref, wk, wv, sems):
     pending = fetch(sems, (wk_ref, wk), (wv_ref, wv))
-    x_ref[:HALF, :] = x2u_ref[:HALF, :]
-    x_ref[HALF:, :] = x2l_ref[:HALF, :]
+    column = jnp.sum(jnp.where(square_column(ROWS), power_ref[:1, :], 0.0), axis=1, keepdims=True)
+    h = jnp.concatenate([h2u_ref[...], h2l_ref[...]], axis=0)
+    x_ref[...] = normed(h, column, gain_ref[...])
     for copy in pending:
         copy.wait()
     put_kv(x_ref[...], wk, wv, kv_ref, send_ref)
 
 
-def q_kernel(xa_ref, xb_ref, wq_ref, keep_ref, send_ref, wq, sems):
-    for copy in fetch(sems, (wq_ref, wq)):
-        copy.wait()
-    q = jnp.dot(jnp.concatenate([xa_ref[...], xb_ref[...]], axis=0), wq[...], preferred_element_type=f32)
-    keep_ref[...] = q
-    send_ref[...] = q.astype(bf16)
+def q_kernel(xa_ref, xb_ref, wq_ref, keep_ref, send_ref):
+    for x_ref, s in ((xa_ref, slice(0, 2 * ROWS)), (xb_ref, slice(2 * ROWS, 3 * ROWS))):
+        q = jnp.dot(x_ref[...], wq_ref[...], preferred_element_type=f32)
+        keep_ref[s, :] = q
+        send_ref[s, :] = q.astype(bf16)
 
 
 def rotated(u, cosine, sine):
@@ -311,10 +312,24 @@
     out_ref[...] = x_ref[...] + a_ref[...] + b_ref[...] + c_ref[...]
 
 
+FIRST = ((1, 0), (7, 0), (4, 0))
+SECOND = (
+    {(1, 0): (2, 0), (7, 0): (6, 0), (4, 0): (3, 0), (0, 0): (5, 1)},
+    {(1, 0): (2, 1), (7, 0): (6, 1), (4, 0): (5, 0), (0, 0): (3, 1)},
+    {(1, 0): (1, 1), (7, 0): (7, 1), (4, 0): (4, 1), (0, 0): (0, 1)},
+)
+
+
+def even_index(chip):
+    return 4 * chip[0] + 2 * chip[1]
+
+
 def spread_far(x, idx):
-    got = [lax.ppermute(x, "ctx", [(0, 4 * z)]) for z in (2, 4, 6)]
+    got = [lax.ppermute(x, "ctx", [(0, even_index(chip))]) for chip in FIRST]
     at = call(first_kernel, "first", jax.ShapeDtypeStruct(x.shape, x.dtype), (idx, x, *got), smem=1)
-    return at, [lax.ppermute(at, "ctx", [(e, e + d) for e in (0, 8, 16, 24)]) for d in (4, 6, 2)]
+    return at, [
+        lax.ppermute(at, "ctx", [(even_index(a), even_index(b)) for a, b in step.items()]) for step in SECOND
+    ]
 
 
 def held(*arrays):
@@ -344,19 +359,20 @@
     sine = jnp.sin(angles) * jnp.where(jnp.arange(HEAD) < HALF, -1.0, 1.0)[None, :]
     lengths = seg_lengths.reshape(-1, 1)
 
-    xu, xl = call(
-        prepare_kernel, "prepare", [shape(TAILED, 2048, bf16)] * 2, (mine, theirs, gain, hidden), stay=(3,),
+    xu, xl, power = call(
+        prepare_kernel, "prepare", [shape(TAILED, 2048, bf16)] * 2 + [shape(8, ROWS, f32)], (mine, theirs, gain, hidden), stay=(3,),
         scratch=held(hidden), flops=ROWS * 2048 * 3,
     )
     x1l = rel(xl, "tc", 4, 1)
     x3u = rel(xu, "tc", 4, 3)
+    h2u = rel(h1u, "tc", 4, 1)
+    h2l = rel(h3l, "tc", 4, 3)
+    p2 = rel(power, "tc", 4, 2)
+    own_u, _, _ = lax.optimization_barrier((xu, h1u, h3l))
     kv0, q0, send0 = call(
         own_kernel, "own", [shape(ROWS, 2 * HEAD, f32), shape(ROWS, QW, f32), shape(ROWS, 7 * HEAD, bf16)],
-        (wq, wk, wv, xu, xl), stay=(0, 1, 2), scratch=held(wq, wk, wv), flops=2 * ROWS * 2048 * 768,
-    )
-    x1l, x3u, send0 = lax.optimization_barrier((x1l, x3u, send0))
-    x2l = rel(x1l, "tc", 4, 1)
-    x2u = rel(x3u, "tc", 4, 3)
+        (wq, wk, wv, own_u, xl), stay=(0, 1, 2), scratch=held(wq, wk, wv), flops=2 * ROWS * 2048 * 768,
+    )
     got0 = rel(send0, "tr", 2, 1)
     x13, kv13, send13 = call(
         near_kernel, "near",
@@ -367,12 +383,11 @@
     x2, kv2, send2 = call(
         far_kernel, "far",
         [shape(ROWS, 2048, bf16), shape(ROWS, 2 * HEAD, f32), shape(ROWS, 3 * HEAD, bf16)],
-        (wk, wv, x2u, x2l), stay=(0, 1), scratch=held(wk, wv), flops=2 * ROWS * 2048 * 256,
+        (wk, wv, gain, p2, h2u, h2l), stay=(0, 1), scratch=held(wk, wv), flops=2 * ROWS * 2048 * 256,
     )
     got2 = rel(send2, "tr", 2, 1)
     q1, send_q = call(
-        q_kernel, "q", [shape(3 * ROWS, QW, f32), shape(3 * ROWS, QW, bf16)], (x13, x2, wq),
-        stay=(2,), scratch=held(wq), flops=6 * ROWS * 2048 * QW,
+        q_kernel, "q", [shape(3 * ROWS, QW, f32), shape(3 * ROWS, QW, bf16)], (x13, x2, wq), flops=6 * ROWS * 2048 * QW,
     )
     got_q = rel(send_q, "tr", 2, 1)
     got2, send_q = lax.optimization_barrier((got2, send_q))

time: 97.3 us -> 91.9 us (0.945)
  starting transfers between devices: 35.9 us -> 33.8 us
  waiting for transfers between devices: 34.7 us -> 32.9 us
  Pallas kernels: 23.2 us -> 21.6 us
    ppermute x17 -> x18, starting transfers between devices: 24.9 us -> 22 us  [rel(): return lax.ppermute(x, axis, [((i + distance) % n, i) for i in range(n)])]
    pallas_call x14, Pallas kernels: 23.2 us -> 21.6 us  [call(): pl.pallas_call(kernel, out_shape=out_shape, in_specs=[spec(w) for w in wh...]
    ppermute x17 -> x18, waiting for transfers between devices: 21.9 us -> 20.8 us  [rel(): return lax.ppermute(x, axis, [((i + distance) % n, i) for i in range(n)])]
    ppermute x1, starting transfers between devices: 5.41 us -> 6.44 us  [per_device(): lax.ppermute(kv, 'ctx', [(i, i + 1) for i in range(lax.axis_size('ctx') -...]
  transfers between devices with their start and end apart: 25 -> 26, of which waited for: 10 -> 11; matrix products, arithmetic and copies ran while one was open for 2% -> 2% of each run, Pallas kernels for 18% -> 17%
where the time goes in v4:
time: 91.9 us; the launch traced here: 91.4 us
  starting transfers between devices  33.8 us (37%)
  waiting for transfers between devices  32.9 us (36%)
  Pallas kernels  21.6 us (24%)
  other arithmetic  2.01 us (2%)
    ppermute x18, starting transfers between devices, rel(): return lax.ppermute(x, axis, [((i + distance) % n, i) for i in range(n)])  22 us
    pallas_call x14, Pallas kernels, call(): pl.pallas_call(kernel, out_shape=out_shape, in_specs=[spec(w) for w in wh...  21.6 us
    ppermute x18, waiting for transfers between devices, rel(): return lax.ppermute(x, axis, [((i + distance) % n, i) for i in range(n)])  20.8 us
    ppermute x1, waiting for transfers between devices, per_device(): lax.ppermute(at, 'ctx', [(2 * i, 2 * i + 1) for i in range(lax.axis_size(...  6.68 us
    ppermute x1, starting transfers between devices, per_device(): lax.ppermute(kv, 'ctx', [(i, i + 1) for i in range(lax.axis_size('ctx') -...  6.44 us
    ppermute x1, waiting for transfers between devices, per_device(): lax.ppermute(kv, 'ctx', [(i, i + 1) for i in range(lax.axis_size('ctx') -...  5.44 us
    ppermute x3, starting transfers between devices, spread_far(): got = [lax.ppermute(x, 'ctx', [(0, even_index(chip))]) for chip in FIRST]  2.03 us
    ppermute x3, starting transfers between devices, spread_far(): lax.ppermute(at, 'ctx', [(even_index(a), even_index(b)) for a, b in step....  2.03 us
  transfers between devices with their start and end apart: 26, of which 11 were waited for; matrix products, arithmetic and copies ran while one was open for 2% of the time, Pallas kernels for 17%

profile of v4, /device:TPU:1, one launch (start us, length us, event | category | flops | bytes accessed | tf_op | source)
XLA Modules:
  0.0 91.4 jit_solution(1293346372509415418)
XLA Ops:
  1.3 3.8 %collective-permute-start = (f32[8,128]{1,0:T(8,128)S(1)}, f32[8,128]{1,0:T(8,128)S(1)}, u32[]{:S(2)}, u32[]{:S(2)}) collective-permute-start(f32[8,128]{1,0:T(8,128)S(1)} %get-tuple-element.41.mine_ref), channel_id=1, source_target_pairs={{4,0},{0,4},{5,1},{1,5},{6,2},{2,6},{7,3},{3,7},{12,8},{8,12},{13,... | collective-permute-start | bytes 12296 | tf_op jit(solution)/shard_map/ppermute | solution.py:34
  5.1 2.5 %collective-permute-start.1 = (bf16[64,2048]{1,0:T(8,128)(2,1)S(1)}, bf16[64,2048]{1,0:T(8,128)(2,1)S(1)}, u32[]{:S(2)}, u32[]{:S(2)}) collective-permute-start(bf16[64,2048]{1,0:T(8,128)(2,1)S(1)} %get-tuple-element.43), channel_id=1, source_target_pairs={{1,0},{2,1},{3,2},{0,3},{5,4},{6,5},{7,6},{4,7},{9,8},{10,9},{11,1... | collective-permute-start | bytes 786440 | tf_op jit(solution)/shard_map/ppermute | solution.py:34
  10.2 2.8 %collective-permute-start.4 = (bf16[80,2048]{1,0:T(8,128)(2,1)S(1)}, bf16[80,2048]{1,0:T(8,128)(2,1)S(1)}, u32[]{:S(2)}, u32[]{:S(2)}) collective-permute-start(bf16[80,2048]{1,0:T(8,128)(2,1)S(1)} %get-tuple-element.46.lower_ref), channel_id=1, source_target_pairs={{1,0},{2,1},{3,2},{0,3},{5,4},{6,5},{7,6},{4,7},{9,8},{10,9},{11,1... | collective-permute-start | bytes 983048 | tf_op jit(solution)/shard_map/ppermute | solution.py:34
  13.0 2.7 %collective-permute-start.8 = (bf16[64,2048]{1,0:T(8,128)(2,1)S(1)}, bf16[64,2048]{1,0:T(8,128)(2,1)S(1)}, u32[]{:S(2)}, u32[]{:S(2)}) collective-permute-start(bf16[64,2048]{1,0:T(8,128)(2,1)S(1)} %collective-permute-done.1.h1u_ref), channel_id=1, source_target_pairs={{1,0},{2,1},{3,2},{0,3},{5,4},{6,5},{7,6},{4,7},{9,8},{10,9},{11,1... | collective-permute-start | bytes 786440 | tf_op jit(solution)/shard_map/ppermute | solution.py:34
  17.0 2.4 %own.1 = (f32[128,256]{1,0:T(8,128)S(1)}, f32[128,512]{1,0:T(8,128)S(1)}, bf16[128,896]{1,0:T(8,128)(2,1)S(1)}) custom-call(bf16[2048,512]{1,0:T(8,128)(2,1)} %wq_ref.3, bf16[2048,128]{1,0:T(8,128)(2,1)} %wk_ref.5, bf16[2048,128]{1,0:T(8,128)(2,1)} %wv_ref.5, bf16[80,2048]{1,0:T(8,128)(2,1)S(1)} %get-tuple-element.45.upper_ref, ...), custom_call_target="tpu_custom_call" | custom-call | flops 402653184 | bytes 4194304 | tf_op jit(solution)/shard_map/own/pallas_call | solution.py:41
  20.2 1.9 %collective-permute-done.5.x3u_ref = bf16[80,2048]{1,0:T(8,128)(2,1)S(1)} collective-permute-done((bf16[80,2048]{1,0:T(8,128)(2,1)S(1)}, bf16[80,2048]{1,0:T(8,128)(2,1)S(1)}, u32[]{:S(2)}, u32[]{:S(2)}) %collective-permute-start.5) | collective-permute-done | bytes 327712 | tf_op jit(solution)/shard_map/ppermute | solution.py:34
  22.1 1.9 %near.1 = (bf16[256,2048]{1,0:T(8,128)(2,1)S(1)}, f32[256,256]{1,0:T(8,128)S(1)}, bf16[256,384]{1,0:T(8,128)(2,1)S(1)}) custom-call(bf16[2048,128]{1,0:T(8,128)(2,1)} %wk_ref.5, bf16[2048,128]{1,0:T(8,128)(2,1)} %wv_ref.5, f32[1,2048]{1,0:T(1,128)S(1)} %bitcast.7, bf16[64,2048]{1,0:T(8,128)(2,1)S(1)} %collective-permute-done.1.h1u_ref, ...), custom_call_target="tpu_custom_call" | custom-call | flops 268435456 | bytes 4194304 | tf_op jit(solution)/shard_map/near/pallas_call | solution.py:41
  24.5 3.0 %collective-permute-done.7.power_ref = f32[8,128]{1,0:T(8,128)S(1)} collective-permute-done((f32[8,128]{1,0:T(8,128)S(1)}, f32[8,128]{1,0:T(8,128)S(1)}, u32[]{:S(2)}, u32[]{:S(2)}) %collective-permute-start.7) | collective-permute-done | bytes 4128 | tf_op jit(solution)/shard_map/ppermute | solution.py:34
  27.7 1.7 %far.1 = (bf16[128,2048]{1,0:T(8,128)(2,1)S(1)}, f32[128,256]{1,0:T(8,128)S(1)}, bf16[128,384]{1,0:T(8,128)(2,1)S(1)}) custom-call(bf16[2048,128]{1,0:T(8,128)(2,1)} %wk_ref.5, bf16[2048,128]{1,0:T(8,128)(2,1)} %wv_ref.5, f32[1,2048]{1,0:T(1,128)S(1)} %bitcast.8, f32[8,128]{1,0:T(8,128)S(1)} %collective-permute-done.7.power_ref, ...), custom_call_target="tpu_custom_call" | custom-call | flops 134217728 | bytes 4194304 | tf_op jit(solution)/shard_map/far/pallas_call | solution.py:41
  30.5 1.8 %q.1 = (f32[384,512]{1,0:T(8,128)S(1)}, bf16[384,512]{1,0:T(8,128)(2,1)}) custom-call(bf16[256,2048]{1,0:T(8,128)(2,1)S(1)} %get-tuple-element.54.xa_ref, bf16[128,2048]{1,0:T(8,128)(2,1)S(1)} %get-tuple-element.55.xb_ref, bf16[2048,512]{1,0:T(8,128)(2,1)S(1)} %copy-done.1), custom_call_target="tpu_custom_call" | custom-call | flops 805306368 | bytes 4194304 | tf_op jit(solution)/shard_map/q/pallas_call | solution.py:41
  32.3 3.5 %collective-permute-done.10.gotb_ref = bf16[128,384]{1,0:T(8,128)(2,1)S(1)} collective-permute-done((bf16[128,384]{1,0:T(8,128)(2,1)S(1)}, bf16[128,384]{1,0:T(8,128)(2,1)S(1)}, u32[]{:S(2)}, u32[]{:S(2)}) %collective-permute-start.10) | collective-permute-done | bytes 98336 | tf_op jit(solution)/shard_map/ppermute | solution.py:34
  38.3 6.4 %collective-permute-start.18 = (bf16[512,256]{1,0:T(8,128)(2,1)S(1)}, bf16[512,256]{1,0:T(8,128)(2,1)}, u32[]{:S(2)}, u32[]{:S(2)}) collective-permute-start(bf16[512,256]{1,0:T(8,128)(2,1)S(1)} %rotary_kv.1.x_ref.own_ref), channel_id=1, source_target_pairs={{0,8},{8,16},{16,24},{24,32},{32,40},{40,48},{48,56},{56,64},{64,7... | collective-permute-start | bytes 786440 | tf_op jit(solution)/shard_map/ppermute | solution.py:398
  47.9 5.4 %collective-permute-done.18.prev_ref = bf16[512,256]{1,0:T(8,128)(2,1)} collective-permute-done((bf16[512,256]{1,0:T(8,128)(2,1)S(1)}, bf16[512,256]{1,0:T(8,128)(2,1)}, u32[]{:S(2)}, u32[]{:S(2)}) %collective-permute-start.18) | collective-permute-done | bytes 262176 | tf_op jit(solution)/shard_map/ppermute | solution.py:398
  53.4 3.8 %local.1 = (f32[4,512,128]{2,1,0:T(8,128)S(1)}, f32[4,512,128]{2,1,0:T(8,128)S(1)}, f32[4,512,128]{2,1,0:T(8,128)S(1)}) custom-call(s32[2]{0:T(128)S(1)} %pad_add_fusion.idx_ref, s32[64,1]{1,0:T(8,128)S(1)} %copy.10.len_ref, bf16[512,512]{1,0:T(8,128)(2,1)S(1)} %rotary_q.1.q_ref, bf16[512,256]{1,0:T(8,128)(2,1)S(1)} %rotary_kv.1.x_ref.own_ref, ...), custom_call_target="tpu_custom_call" | custom-call | flops 671088640 | bytes 4194304 | tf_op jit(solution)/shard_map/local/pallas_call | solution.py:41
  58.5 6.7 %collective-permute-done.19.other_ref = bf16[512,256]{1,0:T(8,128)(2,1)S(1)} collective-permute-done((bf16[512,256]{1,0:T(8,128)(2,1)S(1)}, bf16[512,256]{1,0:T(8,128)(2,1)S(1)}, u32[]{:S(2)}, u32[]{:S(2)}) %collective-permute-start.19) | collective-permute-done | bytes 262176 | tf_op jit(solution)/shard_map/ppermute | solution.py:407
  65.2 3.6 %prefix.3 = (bf16[128,1024]{1,0:T(8,128)(2,1)S(1)}, bf16[128,1024]{1,0:T(8,128)(2,1)S(1)}, f32[128,1024]{1,0:T(8,128)S(1)}, bf16[128,1024]{1,0:T(8,128)(2,1)S(1)...) custom-call(s32[2]{0:T(128)S(1)} %pad_add_fusion.idx_ref, s32[64,1]{1,0:T(8,128)S(1)} %copy.10.len_ref, ...), custom_call_target="tpu_custom_call" | custom-call | flops 1207959552 | bytes 4194304 | tf_op jit(solution)/shard_map/prefix/pallas_call | solution.py:41
  68.8 1.7 %collective-permute-start.24 = (bf16[128,1024]{1,0:T(8,128)(2,1)S(1)}, bf16[128,1024]{1,0:T(8,128)(2,1)S(1)}, u32[]{:S(2)}, u32[]{:S(2)}) collective-permute-start(bf16[128,1024]{1,0:T(8,128)(2,1)S(1)} %get-tuple-element.76), channel_id=1, source_target_pairs={{1,0},{2,1},{3,2},{0,3},{5,4},{6,5},{7,6},{4,7},{9,8},{10,9},{11,1... | collective-permute-start | bytes 786440 | tf_op jit(solution)/shard_map/ppermute | solution.py:34
  70.5 2.7 %collective-permute-start.22 = (bf16[128,1024]{1,0:T(8,128)(2,1)S(1)}, bf16[128,1024]{1,0:T(8,128)(2,1)S(1)}, u32[]{:S(2)}, u32[]{:S(2)}) collective-permute-start(bf16[128,1024]{1,0:T(8,128)(2,1)S(1)} %get-tuple-element.72), channel_id=1, source_target_pairs={{1,0},{2,1},{3,2},{0,3},{5,4},{6,5},{7,6},{4,7},{9,8},{10,9},{11,1... | collective-permute-start | bytes 786440 | tf_op jit(solution)/shard_map/ppermute | solution.py:34
  73.2 3.5 %collective-permute-done.24 = bf16[128,1024]{1,0:T(8,128)(2,1)S(1)} collective-permute-done((bf16[128,1024]{1,0:T(8,128)(2,1)S(1)}, bf16[128,1024]{1,0:T(8,128)(2,1)S(1)}, u32[]{:S(2)}, u32[]{:S(2)}) %collective-permute-start.24) | collective-permute-done | bytes 262176 | tf_op jit(solution)/shard_map/ppermute | solution.py:34
  76.7 2.9 %collective-permute-start.25 = (bf16[128,1024]{1,0:T(8,128)(2,1)S(1)}, bf16[128,1024]{1,0:T(8,128)(2,1)S(1)}, u32[]{:S(2)}, u32[]{:S(2)}) collective-permute-start(bf16[128,1024]{1,0:T(8,128)(2,1)S(1)} %add_convert_fusion), channel_id=1, source_target_pairs={{1,0},{2,1},{3,2},{0,3},{5,4},{6,5},{7,6},{4,7},{9,8},{10,9},{11,1... | collective-permute-start | bytes 786440 | tf_op jit(solution)/shard_map/ppermute | solution.py:34
  79.8 1.9 %prefix.2 = (f32[128,1024]{1,0:T(8,128)S(1)}, f32[128,1024]{1,0:T(8,128)S(1)}) custom-call(s32[2]{0:T(128)S(1)} %pad_add_fusion.idx_ref, s32[64,1]{1,0:T(8,128)S(1)} %copy.10.len_ref, f32[4,512,128]{2,1,0:T(8,128)S(1)} %get-tuple-element.63.acc_ref, f32[4,512,128]{2,1,0:T(8,128)S(1)} %get-tuple-element.64.max_ref, ...), custom_call_target="tpu_custom_call" | custom-call | flops 402653184 | bytes 4194304 | tf_op jit(solution)/shard_map/prefix/pallas_call | solution.py:41
  82.2 2.5 %collective-permute-done.23.refs_4_ = bf16[128,1024]{1,0:T(8,128)(2,1)S(1)} collective-permute-done((bf16[128,1024]{1,0:T(8,128)(2,1)S(1)}, bf16[128,1024]{1,0:T(8,128)(2,1)S(1)}, u32[]{:S(2)}, u32[]{:S(2)}) %collective-permute-start.23) | collective-permute-done | bytes 262176 | tf_op jit(solution)/shard_map/ppermute | solution.py:34
  84.8 3.1 %collective-permute-done.25.refs_5_ = bf16[128,1024]{1,0:T(8,128)(2,1)S(1)} collective-permute-done((bf16[128,1024]{1,0:T(8,128)(2,1)S(1)}, bf16[128,1024]{1,0:T(8,128)(2,1)S(1)}, u32[]{:S(2)}, u32[]{:S(2)}) %collective-permute-start.25) | collective-permute-done | bytes 262176 | tf_op jit(solution)/shard_map/ppermute | solution.py:34
  87.9 2.5 %collective-permute-done.21.refs_1_ = bf16[128,1024]{1,0:T(8,128)(2,1)S(1)} collective-permute-done((bf16[128,1024]{1,0:T(8,128)(2,1)S(1)}, bf16[128,1024]{1,0:T(8,128)(2,1)S(1)}, u32[]{:S(2)}, u32[]{:S(2)}) %collective-permute-start.21) | collective-permute-done | bytes 262176 | tf_op jit(solution)/shard_map/ppermute | solution.py:34
  (63 shorter events, 16.6 us)
Async XLA Ops:
  5.1 7.9 %collective-permute-start.1 = (bf16[64,2048]{1,0:T(8,128)(2,1)S(1)}, bf16[64,2048]{1,0:T(8,128)(2,1)S(1)}, u32[]{:S(2)}, u32[]{:S(2)}) collective-permute-start(bf16[64,2048]{1,0:T(8,128)(2,1)S(1)} %get-tuple-element.43), channel_id=1, source_target_pairs={{1,0},{2,1},{3,2},{0,3},{5,4},{6,5},{7,6},{4,7},{9,8},{10,9},{11,1... | collective-permute-start | bytes 786440 | tf_op jit(solution)/shard_map/ppermute | solution.py:34
  7.6 8.1 %collective-permute-start.2 = (bf16[64,2048]{1,0:T(8,128)(2,1)S(1)}, bf16[64,2048]{1,0:T(8,128)(2,1)S(1)}, u32[]{:S(2)}, u32[]{:S(2)}) collective-permute-start(bf16[64,2048]{1,0:T(8,128)(2,1)S(1)} %get-tuple-element.44), channel_id=1, source_target_pairs={{3,0},{0,1},{1,2},{2,3},{7,4},{4,5},{5,6},{6,7},{11,8},{8,9},{9,10... | collective-permute-start | bytes 786440 | tf_op jit(solution)/shard_map/ppermute | solution.py:34
  10.2 9.3 %collective-permute-start.4 = (bf16[80,2048]{1,0:T(8,128)(2,1)S(1)}, bf16[80,2048]{1,0:T(8,128)(2,1)S(1)}, u32[]{:S(2)}, u32[]{:S(2)}) collective-permute-start(bf16[80,2048]{1,0:T(8,128)(2,1)S(1)} %get-tuple-element.46.lower_ref), channel_id=1, source_target_pairs={{1,0},{2,1},{3,2},{0,3},{5,4},{6,5},{7,6},{4,7},{9,8},{10,9},{11,1... | collective-permute-start | bytes 983048 | tf_op jit(solution)/shard_map/ppermute | solution.py:34
  12.9 9.2 %collective-permute-start.5 = (bf16[80,2048]{1,0:T(8,128)(2,1)S(1)}, bf16[80,2048]{1,0:T(8,128)(2,1)S(1)}, u32[]{:S(2)}, u32[]{:S(2)}) collective-permute-start(bf16[80,2048]{1,0:T(8,128)(2,1)S(1)} %get-tuple-element.45.upper_ref), channel_id=1, source_target_pairs={{3,0},{0,1},{1,2},{2,3},{7,4},{4,5},{5,6},{6,7},{11,8},{8,9},{9,10... | collective-permute-start | bytes 983048 | tf_op jit(solution)/shard_map/ppermute | solution.py:34
  13.0 14.6 %collective-permute-start.8 = (bf16[64,2048]{1,0:T(8,128)(2,1)S(1)}, bf16[64,2048]{1,0:T(8,128)(2,1)S(1)}, u32[]{:S(2)}, u32[]{:S(2)}) collective-permute-start(bf16[64,2048]{1,0:T(8,128)(2,1)S(1)} %collective-permute-done.1.h1u_ref), channel_id=1, source_target_pairs={{1,0},{2,1},{3,2},{0,3},{5,4},{6,5},{7,6},{4,7},{9,8},{10,9},{11,1... | collective-permute-start | bytes 786440 | tf_op jit(solution)/shard_map/ppermute | solution.py:34
  15.7 12.0 %collective-permute-start.9 = (bf16[64,2048]{1,0:T(8,128)(2,1)S(1)}, bf16[64,2048]{1,0:T(8,128)(2,1)S(1)}, u32[]{:S(2)}, u32[]{:S(2)}) collective-permute-start(bf16[64,2048]{1,0:T(8,128)(2,1)S(1)} %collective-permute-done.2.h3l_ref), channel_id=1, source_target_pairs={{3,0},{0,1},{1,2},{2,3},{7,4},{4,5},{5,6},{6,7},{11,8},{8,9},{9,10... | collective-permute-start | bytes 786440 | tf_op jit(solution)/shard_map/ppermute | solution.py:34
  15.8 11.8 %collective-permute-start.7 = (f32[8,128]{1,0:T(8,128)S(1)}, f32[8,128]{1,0:T(8,128)S(1)}, u32[]{:S(2)}, u32[]{:S(2)}) collective-permute-start(f32[8,128]{1,0:T(8,128)S(1)} %get-tuple-element.51), channel_id=1, source_target_pairs={{2,0},{3,1},{0,2},{1,3},{6,4},{7,5},{4,6},{5,7},{10,8},{11,9},{8,1... | collective-permute-start | bytes 12296 | tf_op jit(solution)/shard_map/ppermute | solution.py:34
  19.5 16.3 %collective-permute-start.3 = (bf16[128,896]{1,0:T(8,128)(2,1)S(1)}, bf16[128,896]{1,0:T(8,128)(2,1)S(1)}, u32[]{:S(2)}, u32[]{:S(2)}) collective-permute-start(bf16[128,896]{1,0:T(8,128)(2,1)S(1)} %get-tuple-element.48), channel_id=1, source_target_pairs={{4,0},{0,4},{5,1},{1,5},{6,2},{2,6},{7,3},{3,7},{12,8},{8,12},{13,... | collective-permute-start | bytes 688136 | tf_op jit(solution)/shard_map/ppermute | solution.py:34
  24.0 11.8 %collective-permute-start.6 = (bf16[256,384]{1,0:T(8,128)(2,1)S(1)}, bf16[256,384]{1,0:T(8,128)(2,1)S(1)}, u32[]{:S(2)}, u32[]{:S(2)}) collective-permute-start(bf16[256,384]{1,0:T(8,128)(2,1)S(1)} %get-tuple-element.50), channel_id=1, source_target_pairs={{4,0},{0,4},{5,1},{1,5},{6,2},{2,6},{7,3},{3,7},{12,8},{8,12},{13,... | collective-permute-start | bytes 589832 | tf_op jit(solution)/shard_map/ppermute | solution.py:34
  35.9 8.9 %collective-permute-start.11 = (bf16[512,256]{1,0:T(8,128)(2,1)S(1)}, bf16[512,256]{1,0:T(8,128)(2,1)S(1)}, u32[]{:S(2)}, u32[]{:S(2)}) collective-permute-start(bf16[512,256]{1,0:T(8,128)(2,1)S(1)} %rotary_kv.1.x_ref.own_ref), channel_id=1, source_target_pairs={{0,32},{1,33},{2,34},{3,35},{4,36},{5,37},{6,38},{7,39}} | collective-permute-start | bytes 786440 | tf_op jit(solution)/shard_map/ppermute | solution.py:328
  36.6 8.2 %collective-permute-start.12 = (bf16[512,256]{1,0:T(8,128)(2,1)S(1)}, bf16[512,256]{1,0:T(8,128)(2,1)S(1)}, u32[]{:S(2)}, u32[]{:S(2)}) collective-permute-start(bf16[512,256]{1,0:T(8,128)(2,1)S(1)} %rotary_kv.1.x_ref.own_ref), channel_id=1, source_target_pairs={{0,224},{1,225},{2,226},{3,227},{4,228},{5,229},{6,230},{7,231}} | collective-permute-start | bytes 786440 | tf_op jit(solution)/shard_map/ppermute | solution.py:328
  37.3 7.5 %collective-permute-start.13 = (bf16[512,256]{1,0:T(8,128)(2,1)S(1)}, bf16[512,256]{1,0:T(8,128)(2,1)S(1)}, u32[]{:S(2)}, u32[]{:S(2)}) collective-permute-start(bf16[512,256]{1,0:T(8,128)(2,1)S(1)} %rotary_kv.1.x_ref.own_ref), channel_id=1, source_target_pairs={{0,128},{1,129},{2,130},{3,131},{4,132},{5,133},{6,134},{7,135}} | collective-permute-start | bytes 786440 | tf_op jit(solution)/shard_map/ppermute | solution.py:328
  38.0 9.6 %collective-permute-start.17 = (bf16[384,512]{1,0:T(8,128)(2,1)}, bf16[384,512]{1,0:T(8,128)(2,1)S(1)}, u32[]{:S(2)}, u32[]{:S(2)}) collective-permute-start(bf16[384,512]{1,0:T(8,128)(2,1)} %get-tuple-element.56), channel_id=1, source_target_pairs={{4,0},{0,4},{5,1},{1,5},{6,2},{2,6},{7,3},{3,7},{12,8},{8,12},{13,... | collective-permute-start | bytes 1179656 | tf_op jit(solution)/shard_map/ppermute | solution.py:34
  38.3 15.1 %collective-permute-start.18 = (bf16[512,256]{1,0:T(8,128)(2,1)S(1)}, bf16[512,256]{1,0:T(8,128)(2,1)}, u32[]{:S(2)}, u32[]{:S(2)}) collective-permute-start(bf16[512,256]{1,0:T(8,128)(2,1)S(1)} %rotary_kv.1.x_ref.own_ref), channel_id=1, source_target_pairs={{0,8},{8,16},{16,24},{24,32},{32,40},{40,48},{48,56},{56,64},{64,7... | collective-permute-start | bytes 786440 | tf_op jit(solution)/shard_map/ppermute | solution.py:398
  45.4 11.7 %collective-permute-start.14 = (bf16[512,256]{1,0:T(8,128)(2,1)S(1)}, bf16[512,256]{1,0:T(8,128)(2,1)S(1)}, u32[]{:S(2)}, u32[]{:S(2)}) collective-permute-start(bf16[512,256]{1,0:T(8,128)(2,1)S(1)} %first.1.x_ref), channel_id=1, source_target_pairs={{32,64},{224,192},{128,96},{0,176},{33,65},{225,193},{129,97},{1,1... | collective-permute-start | bytes 786440 | tf_op jit(solution)/shard_map/ppermute | solution.py:331
  46.1 11.1 %collective-permute-start.15 = (bf16[512,256]{1,0:T(8,128)(2,1)S(1)}, bf16[512,256]{1,0:T(8,128)(2,1)S(1)}, u32[]{:S(2)}, u32[]{:S(2)}) collective-permute-start(bf16[512,256]{1,0:T(8,128)(2,1)S(1)} %first.1.x_ref), channel_id=1, source_target_pairs={{32,80},{224,208},{128,160},{0,112},{33,81},{225,209},{129,161},{1... | collective-permute-start | bytes 786440 | tf_op jit(solution)/shard_map/ppermute | solution.py:331
  46.8 10.4 %collective-permute-start.16 = (bf16[512,256]{1,0:T(8,128)(2,1)S(1)}, bf16[512,256]{1,0:T(8,128)(2,1)S(1)}, u32[]{:S(2)}, u32[]{:S(2)}) collective-permute-start(bf16[512,256]{1,0:T(8,128)(2,1)S(1)} %first.1.x_ref), channel_id=1, source_target_pairs={{32,48},{224,240},{128,144},{0,16},{33,49},{225,241},{129,145},{1,... | collective-permute-start | bytes 786440 | tf_op jit(solution)/shard_map/ppermute | solution.py:331
  57.2 8.0 %collective-permute-start.19 = (bf16[512,256]{1,0:T(8,128)(2,1)S(1)}, bf16[512,256]{1,0:T(8,128)(2,1)S(1)}, u32[]{:S(2)}, u32[]{:S(2)}) collective-permute-start(bf16[512,256]{1,0:T(8,128)(2,1)S(1)} %second.1.pre_ref), channel_id=1, source_target_pairs={{0,8},{16,24},{32,40},{48,56},{64,72},{80,88},{96,104},{112,120},{... | collective-permute-start | bytes 786440 | tf_op jit(solution)/shard_map/ppermute | solution.py:407
  68.8 7.8 %collective-permute-start.24 = (bf16[128,1024]{1,0:T(8,128)(2,1)S(1)}, bf16[128,1024]{1,0:T(8,128)(2,1)S(1)}, u32[]{:S(2)}, u32[]{:S(2)}) collective-permute-start(bf16[128,1024]{1,0:T(8,128)(2,1)S(1)} %get-tuple-element.76), channel_id=1, source_target_pairs={{1,0},{2,1},{3,2},{0,3},{5,4},{6,5},{7,6},{4,7},{9,8},{10,9},{11,1... | collective-permute-start | bytes 786440 | tf_op jit(solution)/shard_map/ppermute | solution.py:34
  70.5 9.1 %collective-permute-start.20 = (bf16[128,1024]{1,0:T(8,128)(2,1)S(1)}, bf16[128,1024]{1,0:T(8,128)(2,1)S(1)}, u32[]{:S(2)}, u32[]{:S(2)}) collective-permute-start(bf16[128,1024]{1,0:T(8,128)(2,1)S(1)} %get-tuple-element.71), channel_id=1, source_target_pairs={{3,0},{0,1},{1,2},{2,3},{7,4},{4,5},{5,6},{6,7},{11,8},{8,9},{9,10... | collective-permute-start | bytes 786440 | tf_op jit(solution)/shard_map/ppermute | solution.py:34
  70.5 11.8 %collective-permute-start.22 = (bf16[128,1024]{1,0:T(8,128)(2,1)S(1)}, bf16[128,1024]{1,0:T(8,128)(2,1)S(1)}, u32[]{:S(2)}, u32[]{:S(2)}) collective-permute-start(bf16[128,1024]{1,0:T(8,128)(2,1)S(1)} %get-tuple-element.72), channel_id=1, source_target_pairs={{1,0},{2,1},{3,2},{0,3},{5,4},{6,5},{7,6},{4,7},{9,8},{10,9},{11,1... | collective-permute-start | bytes 786440 | tf_op jit(solution)/shard_map/ppermute | solution.py:34
  73.2 11.6 %collective-permute-start.23 = (bf16[128,1024]{1,0:T(8,128)(2,1)S(1)}, bf16[128,1024]{1,0:T(8,128)(2,1)S(1)}, u32[]{:S(2)}, u32[]{:S(2)}) collective-permute-start(bf16[128,1024]{1,0:T(8,128)(2,1)S(1)} %get-tuple-element.74), channel_id=1, source_target_pairs={{3,0},{0,1},{1,2},{2,3},{7,4},{4,5},{5,6},{6,7},{11,8},{8,9},{9,10... | collective-permute-start | bytes 786440 | tf_op jit(solution)/shard_map/ppermute | solution.py:34
  76.7 11.2 %collective-permute-start.25 = (bf16[128,1024]{1,0:T(8,128)(2,1)S(1)}, bf16[128,1024]{1,0:T(8,128)(2,1)S(1)}, u32[]{:S(2)}, u32[]{:S(2)}) collective-permute-start(bf16[128,1024]{1,0:T(8,128)(2,1)S(1)} %add_convert_fusion), channel_id=1, source_target_pairs={{1,0},{2,1},{3,2},{0,3},{5,4},{6,5},{7,6},{4,7},{9,8},{10,9},{11,1... | collective-permute-start | bytes 786440 | tf_op jit(solution)/shard_map/ppermute | solution.py:34
  79.7 10.7 %collective-permute-start.21 = (bf16[128,1024]{1,0:T(8,128)(2,1)S(1)}, bf16[128,1024]{1,0:T(8,128)(2,1)S(1)}, u32[]{:S(2)}, u32[]{:S(2)}) collective-permute-start(bf16[128,1024]{1,0:T(8,128)(2,1)S(1)} %add_convert_fusion.1), channel_id=1, source_target_pairs={{3,0},{0,1},{1,2},{2,3},{7,4},{4,5},{5,6},{6,7},{11,8},{8,9},{9,10... | collective-permute-start | bytes 786440 | tf_op jit(solution)/shard_map/ppermute | solution.py:34
  (8 other events, 81.4 us)

commit v5 on v4

--- a/solution.py
+++ b/solution.py
@@ -406,8 +406,9 @@
     at = call(second_kernel, "second", shape(BLOCK, 2 * HEAD, bf16), (at, *got))
     pre = (at, lax.ppermute(at, "ctx", [(2 * i, 2 * i + 1) for i in range(lax.axis_size("ctx") // 2)]))
     args = (idx, lengths, state, q, pre, wo)
-    left2, right2, left1, right1, left3, right3 = finish((2, 1, 3), *args, (bf16, bf16, f32, bf16, bf16, f32))
+    left2, right2 = finish((2,), *args, (bf16, bf16))
     left2, right2 = rel(left2, "tc", 4, -1), rel(right2, "tc", 4, 1)
+    left1, right1, left3, right3 = finish((1, 3), *args, (f32, bf16, bf16, f32))
     right1, left3 = rel(right1, "tc", 4, -1), rel(left3, "tc", 4, 1)
     left1 = rel((left1 + left2.astype(f32)).astype(bf16), "tc", 4, -1)
     right3 = rel((right3 + right2.astype(f32)).astype(bf16), "tc", 4, 1)

time: 91.9 us -> 89.8 us (0.977)
  waiting for transfers between devices: 32.9 us -> 29.8 us
  Pallas kernels: 21.6 us -> 22.6 us
    ppermute x18, waiting for transfers between devices: 20.8 us -> 17.6 us  [rel(): return lax.ppermute(x, axis, [((i + distance) % n, i) for i in range(n)])]
    pallas_call x14 -> x15, Pallas kernels: 21.6 us -> 22.6 us  [call(): pl.pallas_call(kernel, out_shape=out_shape, in_specs=[spec(w) for w in wh...]
  transfers between devices with their start and end apart: 26 -> 26, of which waited for: 11 -> 11; matrix products, arithmetic and copies ran while one was open for 2% -> 2% of each run, Pallas kernels for 17% -> 20%
where the time goes in v5:
time: 89.8 us; the launch traced here: 89.4 us
  starting transfers between devices  33.9 us (38%)
  waiting for transfers between devices  29.8 us (33%)
  Pallas kernels  22.6 us (25%)
  other arithmetic  2.01 us (2%)
    pallas_call x15, Pallas kernels, call(): pl.pallas_call(kernel, out_shape=out_shape, in_specs=[spec(w) for w in wh...  22.6 us
    ppermute x18, starting transfers between devices, rel(): return lax.ppermute(x, axis, [((i + distance) % n, i) for i in range(n)])  22.1 us
    ppermute x18, waiting for transfers between devices, rel(): return lax.ppermute(x, axis, [((i + distance) % n, i) for i in range(n)])  17.6 us
    ppermute x1, waiting for transfers between devices, per_device(): lax.ppermute(at, 'ctx', [(2 * i, 2 * i + 1) for i in range(lax.axis_size(...  6.67 us
    ppermute x1, starting transfers between devices, per_device(): lax.ppermute(kv, 'ctx', [(i, i + 1) for i in range(lax.axis_size('ctx') -...  6.44 us
    ppermute x1, waiting for transfers between devices, per_device(): lax.ppermute(kv, 'ctx', [(i, i + 1) for i in range(lax.axis_size('ctx') -...  5.44 us
    ppermute x3, starting transfers between devices, spread_far(): lax.ppermute(at, 'ctx', [(even_index(a), even_index(b)) for a, b in step....  2.03 us
    ppermute x3, starting transfers between devices, spread_far(): got = [lax.ppermute(x, 'ctx', [(0, even_index(chip))]) for chip in FIRST]  2.03 us
  transfers between devices with their start and end apart: 26, of which 11 were waited for; matrix products, arithmetic and copies ran while one was open for 2% of the time, Pallas kernels for 20%

profile of v5, /device:TPU:1, one launch (start us, length us, event | category | flops | bytes accessed | tf_op | source)
XLA Modules:
  0.0 89.4 jit_solution(3702625252445352011)
XLA Ops:
  1.3 3.8 %collective-permute-start = (f32[8,128]{1,0:T(8,128)S(1)}, f32[8,128]{1,0:T(8,128)S(1)}, u32[]{:S(2)}, u32[]{:S(2)}) collective-permute-start(f32[8,128]{1,0:T(8,128)S(1)} %get-tuple-element.41.mine_ref), channel_id=1, source_target_pairs={{4,0},{0,4},{5,1},{1,5},{6,2},{2,6},{7,3},{3,7},{12,8},{8,12},{13,... | collective-permute-start | bytes 12296 | tf_op jit(solution)/shard_map/ppermute | solution.py:34
  5.1 2.5 %collective-permute-start.1 = (bf16[64,2048]{1,0:T(8,128)(2,1)S(1)}, bf16[64,2048]{1,0:T(8,128)(2,1)S(1)}, u32[]{:S(2)}, u32[]{:S(2)}) collective-permute-start(bf16[64,2048]{1,0:T(8,128)(2,1)S(1)} %get-tuple-element.43), channel_id=1, source_target_pairs={{1,0},{2,1},{3,2},{0,3},{5,4},{6,5},{7,6},{4,7},{9,8},{10,9},{11,1... | collective-permute-start | bytes 786440 | tf_op jit(solution)/shard_map/ppermute | solution.py:34
  10.2 2.8 %collective-permute-start.4 = (bf16[80,2048]{1,0:T(8,128)(2,1)S(1)}, bf16[80,2048]{1,0:T(8,128)(2,1)S(1)}, u32[]{:S(2)}, u32[]{:S(2)}) collective-permute-start(bf16[80,2048]{1,0:T(8,128)(2,1)S(1)} %get-tuple-element.46.lower_ref), channel_id=1, source_target_pairs={{1,0},{2,1},{3,2},{0,3},{5,4},{6,5},{7,6},{4,7},{9,8},{10,9},{11,1... | collective-permute-start | bytes 983048 | tf_op jit(solution)/shard_map/ppermute | solution.py:34
  13.0 2.7 %collective-permute-start.8 = (bf16[64,2048]{1,0:T(8,128)(2,1)S(1)}, bf16[64,2048]{1,0:T(8,128)(2,1)S(1)}, u32[]{:S(2)}, u32[]{:S(2)}) collective-permute-start(bf16[64,2048]{1,0:T(8,128)(2,1)S(1)} %collective-permute-done.1.h1u_ref), channel_id=1, source_target_pairs={{1,0},{2,1},{3,2},{0,3},{5,4},{6,5},{7,6},{4,7},{9,8},{10,9},{11,1... | collective-permute-start | bytes 786440 | tf_op jit(solution)/shard_map/ppermute | solution.py:34
  17.0 2.4 %own.1 = (f32[128,256]{1,0:T(8,128)S(1)}, f32[128,512]{1,0:T(8,128)S(1)}, bf16[128,896]{1,0:T(8,128)(2,1)S(1)}) custom-call(bf16[2048,512]{1,0:T(8,128)(2,1)} %wq_ref.3, bf16[2048,128]{1,0:T(8,128)(2,1)} %wk_ref.5, bf16[2048,128]{1,0:T(8,128)(2,1)} %wv_ref.5, bf16[80,2048]{1,0:T(8,128)(2,1)S(1)} %get-tuple-element.45.upper_ref, ...), custom_call_target="tpu_custom_call" | custom-call | flops 402653184 | bytes 4194304 | tf_op jit(solution)/shard_map/own/pallas_call | solution.py:41
  20.2 1.9 %collective-permute-done.5.x3u_ref = bf16[80,2048]{1,0:T(8,128)(2,1)S(1)} collective-permute-done((bf16[80,2048]{1,0:T(8,128)(2,1)S(1)}, bf16[80,2048]{1,0:T(8,128)(2,1)S(1)}, u32[]{:S(2)}, u32[]{:S(2)}) %collective-permute-start.5) | collective-permute-done | bytes 327712 | tf_op jit(solution)/shard_map/ppermute | solution.py:34
  22.1 1.9 %near.1 = (bf16[256,2048]{1,0:T(8,128)(2,1)S(1)}, f32[256,256]{1,0:T(8,128)S(1)}, bf16[256,384]{1,0:T(8,128)(2,1)S(1)}) custom-call(bf16[2048,128]{1,0:T(8,128)(2,1)} %wk_ref.5, bf16[2048,128]{1,0:T(8,128)(2,1)} %wv_ref.5, f32[1,2048]{1,0:T(1,128)S(1)} %bitcast.7, bf16[64,2048]{1,0:T(8,128)(2,1)S(1)} %collective-permute-done.1.h1u_ref, ...), custom_call_target="tpu_custom_call" | custom-call | flops 268435456 | bytes 4194304 | tf_op jit(solution)/shard_map/near/pallas_call | solution.py:41
  24.5 3.0 %collective-permute-done.7.power_ref = f32[8,128]{1,0:T(8,128)S(1)} collective-permute-done((f32[8,128]{1,0:T(8,128)S(1)}, f32[8,128]{1,0:T(8,128)S(1)}, u32[]{:S(2)}, u32[]{:S(2)}) %collective-permute-start.7) | collective-permute-done | bytes 4128 | tf_op jit(solution)/shard_map/ppermute | solution.py:34
  27.7 1.7 %far.1 = (bf16[128,2048]{1,0:T(8,128)(2,1)S(1)}, f32[128,256]{1,0:T(8,128)S(1)}, bf16[128,384]{1,0:T(8,128)(2,1)S(1)}) custom-call(bf16[2048,128]{1,0:T(8,128)(2,1)} %wk_ref.5, bf16[2048,128]{1,0:T(8,128)(2,1)} %wv_ref.5, f32[1,2048]{1,0:T(1,128)S(1)} %bitcast.8, f32[8,128]{1,0:T(8,128)S(1)} %collective-permute-done.7.power_ref, ...), custom_call_target="tpu_custom_call" | custom-call | flops 134217728 | bytes 4194304 | tf_op jit(solution)/shard_map/far/pallas_call | solution.py:41
  30.5 1.8 %q.1 = (f32[384,512]{1,0:T(8,128)S(1)}, bf16[384,512]{1,0:T(8,128)(2,1)}) custom-call(bf16[256,2048]{1,0:T(8,128)(2,1)S(1)} %get-tuple-element.54.xa_ref, bf16[128,2048]{1,0:T(8,128)(2,1)S(1)} %get-tuple-element.55.xb_ref, bf16[2048,512]{1,0:T(8,128)(2,1)S(1)} %copy-done.1), custom_call_target="tpu_custom_call" | custom-call | flops 805306368 | bytes 4194304 | tf_op jit(solution)/shard_map/q/pallas_call | solution.py:41
  32.3 3.5 %collective-permute-done.10.gotb_ref = bf16[128,384]{1,0:T(8,128)(2,1)S(1)} collective-permute-done((bf16[128,384]{1,0:T(8,128)(2,1)S(1)}, bf16[128,384]{1,0:T(8,128)(2,1)S(1)}, u32[]{:S(2)}, u32[]{:S(2)}) %collective-permute-start.10) | collective-permute-done | bytes 98336 | tf_op jit(solution)/shard_map/ppermute | solution.py:34
  38.3 6.4 %collective-permute-start.18 = (bf16[512,256]{1,0:T(8,128)(2,1)S(1)}, bf16[512,256]{1,0:T(8,128)(2,1)}, u32[]{:S(2)}, u32[]{:S(2)}) collective-permute-start(bf16[512,256]{1,0:T(8,128)(2,1)S(1)} %rotary_kv.1.x_ref.own_ref), channel_id=1, source_target_pairs={{0,8},{8,16},{16,24},{24,32},{32,40},{40,48},{48,56},{56,64},{64,7... | collective-permute-start | bytes 786440 | tf_op jit(solution)/shard_map/ppermute | solution.py:398
  47.9 5.4 %collective-permute-done.18.prev_ref = bf16[512,256]{1,0:T(8,128)(2,1)} collective-permute-done((bf16[512,256]{1,0:T(8,128)(2,1)S(1)}, bf16[512,256]{1,0:T(8,128)(2,1)}, u32[]{:S(2)}, u32[]{:S(2)}) %collective-permute-start.18) | collective-permute-done | bytes 262176 | tf_op jit(solution)/shard_map/ppermute | solution.py:398
  53.4 3.7 %local.1 = (f32[4,512,128]{2,1,0:T(8,128)S(1)}, f32[4,512,128]{2,1,0:T(8,128)S(1)}, f32[4,512,128]{2,1,0:T(8,128)S(1)}) custom-call(s32[2]{0:T(128)S(1)} %pad_add_fusion.idx_ref, s32[64,1]{1,0:T(8,128)S(1)} %copy.10.len_ref, bf16[512,512]{1,0:T(8,128)(2,1)S(1)} %rotary_q.1.q_ref, bf16[512,256]{1,0:T(8,128)(2,1)S(1)} %rotary_kv.1.x_ref.own_ref, ...), custom_call_target="tpu_custom_call" | custom-call | flops 671088640 | bytes 4194304 | tf_op jit(solution)/shard_map/local/pallas_call | solution.py:41
  58.5 6.7 %collective-permute-done.19.other_ref = bf16[512,256]{1,0:T(8,128)(2,1)S(1)} collective-permute-done((bf16[512,256]{1,0:T(8,128)(2,1)S(1)}, bf16[512,256]{1,0:T(8,128)(2,1)S(1)}, u32[]{:S(2)}, u32[]{:S(2)}) %collective-permute-start.19) | collective-permute-done | bytes 262176 | tf_op jit(solution)/shard_map/ppermute | solution.py:407
  65.2 1.9 %prefix.5 = (bf16[128,1024]{1,0:T(8,128)(2,1)S(1)}, bf16[128,1024]{1,0:T(8,128)(2,1)S(1)}) custom-call(s32[2]{0:T(128)S(1)} %pad_add_fusion.idx_ref, s32[64,1]{1,0:T(8,128)S(1)} %copy.10.len_ref, f32[4,512,128]{2,1,0:T(8,128)S(1)} %get-tuple-element.63.acc_ref, f32[4,512,128]{2,1,0:T(8,128)S(1)} %get-tuple-element.64.max_ref, ...), custom_call_target="tpu_custom_call" | custom-call | flops 402653184 | bytes 4194304 | tf_op jit(solution)/shard_map/prefix/pallas_call | solution.py:41
  67.1 1.7 %collective-permute-start.24 = (bf16[128,1024]{1,0:T(8,128)(2,1)S(1)}, bf16[128,1024]{1,0:T(8,128)(2,1)S(1)}, u32[]{:S(2)}, u32[]{:S(2)}) collective-permute-start(bf16[128,1024]{1,0:T(8,128)(2,1)S(1)} %get-tuple-element.76), channel_id=1, source_target_pairs={{1,0},{2,1},{3,2},{0,3},{5,4},{6,5},{7,6},{4,7},{9,8},{10,9},{11,1... | collective-permute-start | bytes 786440 | tf_op jit(solution)/shard_map/ppermute | solution.py:34
  68.8 2.6 %prefix.4 = (f32[128,1024]{1,0:T(8,128)S(1)}, bf16[128,1024]{1,0:T(8,128)(2,1)S(1)}, bf16[128,1024]{1,0:T(8,128)(2,1)S(1)}, f32[128,1024]{1,0:T(8,128)S(1)}) custom-call(s32[2]{0:T(128)S(1)} %pad_add_fusion.idx_ref, s32[64,1]{1,0:T(8,128)S(1)} %copy.10.len_ref, f32[4,512,128]{2,1,0:T(8,128)S(1)} %get-tuple-element.63.acc_ref, ...), custom_call_target="tpu_custom_call" | custom-call | flops 805306368 | bytes 4194304 | tf_op jit(solution)/shard_map/prefix/pallas_call | solution.py:41
  71.4 2.8 %collective-permute-start.22 = (bf16[128,1024]{1,0:T(8,128)(2,1)S(1)}, bf16[128,1024]{1,0:T(8,128)(2,1)S(1)}, u32[]{:S(2)}, u32[]{:S(2)}) collective-permute-start(bf16[128,1024]{1,0:T(8,128)(2,1)S(1)} %get-tuple-element.72), channel_id=1, source_target_pairs={{1,0},{2,1},{3,2},{0,3},{5,4},{6,5},{7,6},{4,7},{9,8},{10,9},{11,1... | collective-permute-start | bytes 786440 | tf_op jit(solution)/shard_map/ppermute | solution.py:34
  75.0 2.9 %collective-permute-start.25 = (bf16[128,1024]{1,0:T(8,128)(2,1)S(1)}, bf16[128,1024]{1,0:T(8,128)(2,1)S(1)}, u32[]{:S(2)}, u32[]{:S(2)}) collective-permute-start(bf16[128,1024]{1,0:T(8,128)(2,1)S(1)} %add_convert_fusion), channel_id=1, source_target_pairs={{1,0},{2,1},{3,2},{0,3},{5,4},{6,5},{7,6},{4,7},{9,8},{10,9},{11,1... | collective-permute-start | bytes 786440 | tf_op jit(solution)/shard_map/ppermute | solution.py:34
  78.1 1.9 %prefix.3 = (f32[128,1024]{1,0:T(8,128)S(1)}, f32[128,1024]{1,0:T(8,128)S(1)}) custom-call(s32[2]{0:T(128)S(1)} %pad_add_fusion.idx_ref, s32[64,1]{1,0:T(8,128)S(1)} %copy.10.len_ref, f32[4,512,128]{2,1,0:T(8,128)S(1)} %get-tuple-element.63.acc_ref, f32[4,512,128]{2,1,0:T(8,128)S(1)} %get-tuple-element.64.max_ref, ...), custom_call_target="tpu_custom_call" | custom-call | flops 402653184 | bytes 4194304 | tf_op jit(solution)/shard_map/prefix/pallas_call | solution.py:41
  80.6 2.2 %collective-permute-done.23.refs_4_ = bf16[128,1024]{1,0:T(8,128)(2,1)S(1)} collective-permute-done((bf16[128,1024]{1,0:T(8,128)(2,1)S(1)}, bf16[128,1024]{1,0:T(8,128)(2,1)S(1)}, u32[]{:S(2)}, u32[]{:S(2)}) %collective-permute-start.23) | collective-permute-done | bytes 262176 | tf_op jit(solution)/shard_map/ppermute | solution.py:34
  82.7 3.5 %collective-permute-done.25.refs_5_ = bf16[128,1024]{1,0:T(8,128)(2,1)S(1)} collective-permute-done((bf16[128,1024]{1,0:T(8,128)(2,1)S(1)}, bf16[128,1024]{1,0:T(8,128)(2,1)S(1)}, u32[]{:S(2)}, u32[]{:S(2)}) %collective-permute-start.25) | collective-permute-done | bytes 262176 | tf_op jit(solution)/shard_map/ppermute | solution.py:34
  86.2 2.2 %collective-permute-done.21.refs_1_ = bf16[128,1024]{1,0:T(8,128)(2,1)S(1)} collective-permute-done((bf16[128,1024]{1,0:T(8,128)(2,1)S(1)}, bf16[128,1024]{1,0:T(8,128)(2,1)S(1)}, u32[]{:S(2)}, u32[]{:S(2)}) %collective-permute-start.21) | collective-permute-done | bytes 262176 | tf_op jit(solution)/shard_map/ppermute | solution.py:34
  (64 shorter events, 17.3 us)
Async XLA Ops:
  5.1 7.9 %collective-permute-start.1 = (bf16[64,2048]{1,0:T(8,128)(2,1)S(1)}, bf16[64,2048]{1,0:T(8,128)(2,1)S(1)}, u32[]{:S(2)}, u32[]{:S(2)}) collective-permute-start(bf16[64,2048]{1,0:T(8,128)(2,1)S(1)} %get-tuple-element.43), channel_id=1, source_target_pairs={{1,0},{2,1},{3,2},{0,3},{5,4},{6,5},{7,6},{4,7},{9,8},{10,9},{11,1... | collective-permute-start | bytes 786440 | tf_op jit(solution)/shard_map/ppermute | solution.py:34
  7.6 8.1 %collective-permute-start.2 = (bf16[64,2048]{1,0:T(8,128)(2,1)S(1)}, bf16[64,2048]{1,0:T(8,128)(2,1)S(1)}, u32[]{:S(2)}, u32[]{:S(2)}) collective-permute-start(bf16[64,2048]{1,0:T(8,128)(2,1)S(1)} %get-tuple-element.44), channel_id=1, source_target_pairs={{3,0},{0,1},{1,2},{2,3},{7,4},{4,5},{5,6},{6,7},{11,8},{8,9},{9,10... | collective-permute-start | bytes 786440 | tf_op jit(solution)/shard_map/ppermute | solution.py:34
  10.2 9.3 %collective-permute-start.4 = (bf16[80,2048]{1,0:T(8,128)(2,1)S(1)}, bf16[80,2048]{1,0:T(8,128)(2,1)S(1)}, u32[]{:S(2)}, u32[]{:S(2)}) collective-permute-start(bf16[80,2048]{1,0:T(8,128)(2,1)S(1)} %get-tuple-element.46.lower_ref), channel_id=1, source_target_pairs={{1,0},{2,1},{3,2},{0,3},{5,4},{6,5},{7,6},{4,7},{9,8},{10,9},{11,1... | collective-permute-start | bytes 983048 | tf_op jit(solution)/shard_map/ppermute | solution.py:34
  12.9 9.2 %collective-permute-start.5 = (bf16[80,2048]{1,0:T(8,128)(2,1)S(1)}, bf16[80,2048]{1,0:T(8,128)(2,1)S(1)}, u32[]{:S(2)}, u32[]{:S(2)}) collective-permute-start(bf16[80,2048]{1,0:T(8,128)(2,1)S(1)} %get-tuple-element.45.upper_ref), channel_id=1, source_target_pairs={{3,0},{0,1},{1,2},{2,3},{7,4},{4,5},{5,6},{6,7},{11,8},{8,9},{9,10... | collective-permute-start | bytes 983048 | tf_op jit(solution)/shard_map/ppermute | solution.py:34
  13.0 14.6 %collective-permute-start.8 = (bf16[64,2048]{1,0:T(8,128)(2,1)S(1)}, bf16[64,2048]{1,0:T(8,128)(2,1)S(1)}, u32[]{:S(2)}, u32[]{:S(2)}) collective-permute-start(bf16[64,2048]{1,0:T(8,128)(2,1)S(1)} %collective-permute-done.1.h1u_ref), channel_id=1, source_target_pairs={{1,0},{2,1},{3,2},{0,3},{5,4},{6,5},{7,6},{4,7},{9,8},{10,9},{11,1... | collective-permute-start | bytes 786440 | tf_op jit(solution)/shard_map/ppermute | solution.py:34
  15.7 12.0 %collective-permute-start.9 = (bf16[64,2048]{1,0:T(8,128)(2,1)S(1)}, bf16[64,2048]{1,0:T(8,128)(2,1)S(1)}, u32[]{:S(2)}, u32[]{:S(2)}) collective-permute-start(bf16[64,2048]{1,0:T(8,128)(2,1)S(1)} %collective-permute-done.2.h3l_ref), channel_id=1, source_target_pairs={{3,0},{0,1},{1,2},{2,3},{7,4},{4,5},{5,6},{6,7},{11,8},{8,9},{9,10... | collective-permute-start | bytes 786440 | tf_op jit(solution)/shard_map/ppermute | solution.py:34
  15.8 11.8 %collective-permute-start.7 = (f32[8,128]{1,0:T(8,128)S(1)}, f32[8,128]{1,0:T(8,128)S(1)}, u32[]{:S(2)}, u32[]{:S(2)}) collective-permute-start(f32[8,128]{1,0:T(8,128)S(1)} %get-tuple-element.51), channel_id=1, source_target_pairs={{2,0},{3,1},{0,2},{1,3},{6,4},{7,5},{4,6},{5,7},{10,8},{11,9},{8,1... | collective-permute-start | bytes 12296 | tf_op jit(solution)/shard_map/ppermute | solution.py:34
  19.5 16.3 %collective-permute-start.3 = (bf16[128,896]{1,0:T(8,128)(2,1)S(1)}, bf16[128,896]{1,0:T(8,128)(2,1)S(1)}, u32[]{:S(2)}, u32[]{:S(2)}) collective-permute-start(bf16[128,896]{1,0:T(8,128)(2,1)S(1)} %get-tuple-element.48), channel_id=1, source_target_pairs={{4,0},{0,4},{5,1},{1,5},{6,2},{2,6},{7,3},{3,7},{12,8},{8,12},{13,... | collective-permute-start | bytes 688136 | tf_op jit(solution)/shard_map/ppermute | solution.py:34
  24.0 11.8 %collective-permute-start.6 = (bf16[256,384]{1,0:T(8,128)(2,1)S(1)}, bf16[256,384]{1,0:T(8,128)(2,1)S(1)}, u32[]{:S(2)}, u32[]{:S(2)}) collective-permute-start(bf16[256,384]{1,0:T(8,128)(2,1)S(1)} %get-tuple-element.50), channel_id=1, source_target_pairs={{4,0},{0,4},{5,1},{1,5},{6,2},{2,6},{7,3},{3,7},{12,8},{8,12},{13,... | collective-permute-start | bytes 589832 | tf_op jit(solution)/shard_map/ppermute | solution.py:34
  35.9 8.9 %collective-permute-start.11 = (bf16[512,256]{1,0:T(8,128)(2,1)S(1)}, bf16[512,256]{1,0:T(8,128)(2,1)S(1)}, u32[]{:S(2)}, u32[]{:S(2)}) collective-permute-start(bf16[512,256]{1,0:T(8,128)(2,1)S(1)} %rotary_kv.1.x_ref.own_ref), channel_id=1, source_target_pairs={{0,32},{1,33},{2,34},{3,35},{4,36},{5,37},{6,38},{7,39}} | collective-permute-start | bytes 786440 | tf_op jit(solution)/shard_map/ppermute | solution.py:328
  36.6 8.2 %collective-permute-start.12 = (bf16[512,256]{1,0:T(8,128)(2,1)S(1)}, bf16[512,256]{1,0:T(8,128)(2,1)S(1)}, u32[]{:S(2)}, u32[]{:S(2)}) collective-permute-start(bf16[512,256]{1,0:T(8,128)(2,1)S(1)} %rotary_kv.1.x_ref.own_ref), channel_id=1, source_target_pairs={{0,224},{1,225},{2,226},{3,227},{4,228},{5,229},{6,230},{7,231}} | collective-permute-start | bytes 786440 | tf_op jit(solution)/shard_map/ppermute | solution.py:328
  37.3 7.5 %collective-permute-start.13 = (bf16[512,256]{1,0:T(8,128)(2,1)S(1)}, bf16[512,256]{1,0:T(8,128)(2,1)S(1)}, u32[]{:S(2)}, u32[]{:S(2)}) collective-permute-start(bf16[512,256]{1,0:T(8,128)(2,1)S(1)} %rotary_kv.1.x_ref.own_ref), channel_id=1, source_target_pairs={{0,128},{1,129},{2,130},{3,131},{4,132},{5,133},{6,134},{7,135}} | collective-permute-start | bytes 786440 | tf_op jit(solution)/shard_map/ppermute | solution.py:328
  38.0 9.6 %collective-permute-start.17 = (bf16[384,512]{1,0:T(8,128)(2,1)}, bf16[384,512]{1,0:T(8,128)(2,1)S(1)}, u32[]{:S(2)}, u32[]{:S(2)}) collective-permute-start(bf16[384,512]{1,0:T(8,128)(2,1)} %get-tuple-element.56), channel_id=1, source_target_pairs={{4,0},{0,4},{5,1},{1,5},{6,2},{2,6},{7,3},{3,7},{12,8},{8,12},{13,... | collective-permute-start | bytes 1179656 | tf_op jit(solution)/shard_map/ppermute | solution.py:34
  38.3 15.1 %collective-permute-start.18 = (bf16[512,256]{1,0:T(8,128)(2,1)S(1)}, bf16[512,256]{1,0:T(8,128)(2,1)}, u32[]{:S(2)}, u32[]{:S(2)}) collective-permute-start(bf16[512,256]{1,0:T(8,128)(2,1)S(1)} %rotary_kv.1.x_ref.own_ref), channel_id=1, source_target_pairs={{0,8},{8,16},{16,24},{24,32},{32,40},{40,48},{48,56},{56,64},{64,7... | collective-permute-start | bytes 786440 | tf_op jit(solution)/shard_map/ppermute | solution.py:398
  45.4 11.7 %collective-permute-start.14 = (bf16[512,256]{1,0:T(8,128)(2,1)S(1)}, bf16[512,256]{1,0:T(8,128)(2,1)S(1)}, u32[]{:S(2)}, u32[]{:S(2)}) collective-permute-start(bf16[512,256]{1,0:T(8,128)(2,1)S(1)} %first.1.x_ref), channel_id=1, source_target_pairs={{32,64},{224,192},{128,96},{0,176},{33,65},{225,193},{129,97},{1,1... | collective-permute-start | bytes 786440 | tf_op jit(solution)/shard_map/ppermute | solution.py:331
  46.1 11.0 %collective-permute-start.15 = (bf16[512,256]{1,0:T(8,128)(2,1)S(1)}, bf16[512,256]{1,0:T(8,128)(2,1)S(1)}, u32[]{:S(2)}, u32[]{:S(2)}) collective-permute-start(bf16[512,256]{1,0:T(8,128)(2,1)S(1)} %first.1.x_ref), channel_id=1, source_target_pairs={{32,80},{224,208},{128,160},{0,112},{33,81},{225,209},{129,161},{1... | collective-permute-start | bytes 786440 | tf_op jit(solution)/shard_map/ppermute | solution.py:331
  46.8 10.4 %collective-permute-start.16 = (bf16[512,256]{1,0:T(8,128)(2,1)S(1)}, bf16[512,256]{1,0:T(8,128)(2,1)S(1)}, u32[]{:S(2)}, u32[]{:S(2)}) collective-permute-start(bf16[512,256]{1,0:T(8,128)(2,1)S(1)} %first.1.x_ref), channel_id=1, source_target_pairs={{32,48},{224,240},{128,144},{0,16},{33,49},{225,241},{129,145},{1,... | collective-permute-start | bytes 786440 | tf_op jit(solution)/shard_map/ppermute | solution.py:331
  57.2 8.0 %collective-permute-start.19 = (bf16[512,256]{1,0:T(8,128)(2,1)S(1)}, bf16[512,256]{1,0:T(8,128)(2,1)S(1)}, u32[]{:S(2)}, u32[]{:S(2)}) collective-permute-start(bf16[512,256]{1,0:T(8,128)(2,1)S(1)} %second.1.pre_ref), channel_id=1, source_target_pairs={{0,8},{16,24},{32,40},{48,56},{64,72},{80,88},{96,104},{112,120},{... | collective-permute-start | bytes 786440 | tf_op jit(solution)/shard_map/ppermute | solution.py:407
  67.1 7.8 %collective-permute-start.24 = (bf16[128,1024]{1,0:T(8,128)(2,1)S(1)}, bf16[128,1024]{1,0:T(8,128)(2,1)S(1)}, u32[]{:S(2)}, u32[]{:S(2)}) collective-permute-start(bf16[128,1024]{1,0:T(8,128)(2,1)S(1)} %get-tuple-element.76), channel_id=1, source_target_pairs={{1,0},{2,1},{3,2},{0,3},{5,4},{6,5},{7,6},{4,7},{9,8},{10,9},{11,1... | collective-permute-start | bytes 786440 | tf_op jit(solution)/shard_map/ppermute | solution.py:34
  68.8 9.1 %collective-permute-start.20 = (bf16[128,1024]{1,0:T(8,128)(2,1)S(1)}, bf16[128,1024]{1,0:T(8,128)(2,1)S(1)}, u32[]{:S(2)}, u32[]{:S(2)}) collective-permute-start(bf16[128,1024]{1,0:T(8,128)(2,1)S(1)} %get-tuple-element.71), channel_id=1, source_target_pairs={{3,0},{0,1},{1,2},{2,3},{7,4},{4,5},{5,6},{6,7},{11,8},{8,9},{9,10... | collective-permute-start | bytes 786440 | tf_op jit(solution)/shard_map/ppermute | solution.py:34
  71.4 9.1 %collective-permute-start.22 = (bf16[128,1024]{1,0:T(8,128)(2,1)S(1)}, bf16[128,1024]{1,0:T(8,128)(2,1)S(1)}, u32[]{:S(2)}, u32[]{:S(2)}) collective-permute-start(bf16[128,1024]{1,0:T(8,128)(2,1)S(1)} %get-tuple-element.72), channel_id=1, source_target_pairs={{1,0},{2,1},{3,2},{0,3},{5,4},{6,5},{7,6},{4,7},{9,8},{10,9},{11,1... | collective-permute-start | bytes 786440 | tf_op jit(solution)/shard_map/ppermute | solution.py:34
  74.2 8.5 %collective-permute-start.23 = (bf16[128,1024]{1,0:T(8,128)(2,1)S(1)}, bf16[128,1024]{1,0:T(8,128)(2,1)S(1)}, u32[]{:S(2)}, u32[]{:S(2)}) collective-permute-start(bf16[128,1024]{1,0:T(8,128)(2,1)S(1)} %get-tuple-element.74), channel_id=1, source_target_pairs={{3,0},{0,1},{1,2},{2,3},{7,4},{4,5},{5,6},{6,7},{11,8},{8,9},{9,10... | collective-permute-start | bytes 786440 | tf_op jit(solution)/shard_map/ppermute | solution.py:34
  75.0 11.2 %collective-permute-start.25 = (bf16[128,1024]{1,0:T(8,128)(2,1)S(1)}, bf16[128,1024]{1,0:T(8,128)(2,1)S(1)}, u32[]{:S(2)}, u32[]{:S(2)}) collective-permute-start(bf16[128,1024]{1,0:T(8,128)(2,1)S(1)} %add_convert_fusion), channel_id=1, source_target_pairs={{1,0},{2,1},{3,2},{0,3},{5,4},{6,5},{7,6},{4,7},{9,8},{10,9},{11,1... | collective-permute-start | bytes 786440 | tf_op jit(solution)/shard_map/ppermute | solution.py:34
  78.0 10.3 %collective-permute-start.21 = (bf16[128,1024]{1,0:T(8,128)(2,1)S(1)}, bf16[128,1024]{1,0:T(8,128)(2,1)S(1)}, u32[]{:S(2)}, u32[]{:S(2)}) collective-permute-start(bf16[128,1024]{1,0:T(8,128)(2,1)S(1)} %add_convert_fusion.1), channel_id=1, source_target_pairs={{3,0},{0,1},{1,2},{2,3},{7,4},{4,5},{5,6},{6,7},{11,8},{8,9},{9,10... | collective-permute-start | bytes 786440 | tf_op jit(solution)/shard_map/ppermute | solution.py:34
  (8 other events, 81.0 us)

commit v6 on v5

--- a/solution.py
+++ b/solution.py
@@ -75,8 +75,10 @@
     return (h.astype(f32) * lax.rsqrt(power / D + EPS) * gain).astype(bf16)
 
 
-def put_kv(x, wk_ref, wv_ref, keep_ref, send_ref):
+def put_kv(x, wk_ref, wv_ref, keep_ref, send_ref, pending):
+    pending[0].wait()
     k = jnp.dot(x, wk_ref[...], preferred_element_type=f32)
+    pending[1].wait()
     v = jnp.dot(x, wv_ref[...], preferred_element_type=f32)
     high = k.astype(bf16)
     keep_ref[:, :HEAD] = v
@@ -124,9 +126,7 @@
 def own_kernel(wq_ref, wk_ref, wv_ref, upper_ref, lower_ref, kv_ref, q_ref, send_ref, wq, wk, wv, sems):
     pending = fetch(sems, (wk_ref, wk), (wv_ref, wv), (wq_ref, wq))
     x = jnp.concatenate([upper_ref[:HALF, :], lower_ref[:HALF, :]], axis=0)
-    pending[0].wait()
-    pending[1].wait()
-    put_kv(x, wk, wv, kv_ref, send_ref)
+    put_kv(x, wk, wv, kv_ref, send_ref, pending)
     pending[2].wait()
     put_q(x, wq, q_ref, send_ref, 3 * HEAD)
 
@@ -137,9 +137,7 @@
     x_ref[HALF : 2 * HALF, :] = x1l_ref[:HALF, :]
     x_ref[2 * HALF : 3 * HALF, :] = x3u_ref[:HALF, :]
     x_ref[3 * HALF :, :] = normed(h3l_ref[...], power_of(x3u_ref[HALF:, :]), gain_ref[...])
-    for copy in pending:
-        copy.wait()
-    put_kv(x_ref[...], wk, wv, kv_ref, send_ref)
+    put_kv(x_ref[...], wk, wv, kv_ref, send_ref, pending)
 
 
 def far_kernel(wk_ref, wv_ref, gain_ref, power_ref, h2u_ref, h2l_ref, x_ref, kv_ref, send_ref, wk, wv, sems):
@@ -147,9 +145,7 @@
     column = jnp.sum(jnp.where(square_column(ROWS), power_ref[:1, :], 0.0), axis=1, keepdims=True)
     h = jnp.concatenate([h2u_ref[...], h2l_ref[...]], axis=0)
     x_ref[...] = normed(h, column, gain_ref[...])
-    for copy in pending:
-        copy.wait()
-    put_kv(x_ref[...], wk, wv, kv_ref, send_ref)
+    put_kv(x_ref[...], wk, wv, kv_ref, send_ref, pending)
 
 
 def q_kernel(xa_ref, xb_ref, wq_ref, keep_ref, send_ref):
@@ -276,7 +272,7 @@
         factor = jnp.exp2((before - largest) * EXPONENT)
         total = jnp.sum(p, axis=1, keepdims=True) + factor * sum_ref[r][:, :1]
         mixed = jnp.dot(p.astype(bf16), values, preferred_element_type=f32) + factor * acc_ref[r]
-        mixed = (mixed / total).astype(bf16)
+        mixed = (mixed * (1.0 / total)).astype(bf16)
         for h in range(HEADS):
             attended_ref[n * ROWS : (n + 1) * ROWS, h * HEAD : (h + 1) * HEAD] = mixed[h * ROWS : (h + 1) * ROWS]
     for side, columns in ((0, slice(0, SIDE)), (1, slice(SIDE, 2 * SIDE))):

time: 89.8 us -> 89.8 us (level)
  no operation moved by 1% of the time
where the time goes in v6:
time: 89.8 us; the launch traced here: 89.4 us
  starting transfers between devices  33.9 us (38%)
  waiting for transfers between devices  29.8 us (33%)
  Pallas kernels  22.6 us (25%)
  other arithmetic  2.01 us (2%)
    pallas_call x15, Pallas kernels, call(): pl.pallas_call(kernel, out_shape=out_shape, in_specs=[spec(w) for w in wh...  22.6 us
    ppermute x18, starting transfers between devices, rel(): return lax.ppermute(x, axis, [((i + distance) % n, i) for i in range(n)])  21.9 us
    ppermute x18, waiting for transfers between devices, rel(): return lax.ppermute(x, axis, [((i + distance) % n, i) for i in range(n)])  17.6 us
    ppermute x1, waiting for transfers between devices, per_device(): lax.ppermute(at, 'ctx', [(2 * i, 2 * i + 1) for i in range(lax.axis_size(...  6.67 us
    ppermute x1, starting transfers between devices, per_device(): lax.ppermute(kv, 'ctx', [(i, i + 1) for i in range(lax.axis_size('ctx') -...  6.45 us
    ppermute x1, waiting for transfers between devices, per_device(): lax.ppermute(kv, 'ctx', [(i, i + 1) for i in range(lax.axis_size('ctx') -...  5.44 us
    ppermute x3, starting transfers between devices, spread_far(): got = [lax.ppermute(x, 'ctx', [(0, even_index(chip))]) for chip in FIRST]  2.21 us
    ppermute x3, starting transfers between devices, spread_far(): lax.ppermute(at, 'ctx', [(even_index(a), even_index(b)) for a, b in step....  2.03 us
  transfers between devices with their start and end apart: 26, of which 11 were waited for; matrix products, arithmetic and copies ran while one was open for 2% of the time, Pallas kernels for 20%

profile of v6, /device:TPU:1, one launch (start us, length us, event | category | flops | bytes accessed | tf_op | source)
XLA Modules:
  0.0 89.4 jit_solution(7248300937692900797)
XLA Ops:
  1.3 3.8 %collective-permute-start = (f32[8,128]{1,0:T(8,128)S(1)}, f32[8,128]{1,0:T(8,128)S(1)}, u32[]{:S(2)}, u32[]{:S(2)}) collective-permute-start(f32[8,128]{1,0:T(8,128)S(1)} %get-tuple-element.41.mine_ref), channel_id=1, source_target_pairs={{4,0},{0,4},{5,1},{1,5},{6,2},{2,6},{7,3},{3,7},{12,8},{8,12},{13,... | collective-permute-start | bytes 12296 | tf_op jit(solution)/shard_map/ppermute | solution.py:34
  5.1 2.5 %collective-permute-start.1 = (bf16[64,2048]{1,0:T(8,128)(2,1)S(1)}, bf16[64,2048]{1,0:T(8,128)(2,1)S(1)}, u32[]{:S(2)}, u32[]{:S(2)}) collective-permute-start(bf16[64,2048]{1,0:T(8,128)(2,1)S(1)} %get-tuple-element.43), channel_id=1, source_target_pairs={{1,0},{2,1},{3,2},{0,3},{5,4},{6,5},{7,6},{4,7},{9,8},{10,9},{11,1... | collective-permute-start | bytes 786440 | tf_op jit(solution)/shard_map/ppermute | solution.py:34
  10.2 2.8 %collective-permute-start.4 = (bf16[80,2048]{1,0:T(8,128)(2,1)S(1)}, bf16[80,2048]{1,0:T(8,128)(2,1)S(1)}, u32[]{:S(2)}, u32[]{:S(2)}) collective-permute-start(bf16[80,2048]{1,0:T(8,128)(2,1)S(1)} %get-tuple-element.46.lower_ref), channel_id=1, source_target_pairs={{1,0},{2,1},{3,2},{0,3},{5,4},{6,5},{7,6},{4,7},{9,8},{10,9},{11,1... | collective-permute-start | bytes 983048 | tf_op jit(solution)/shard_map/ppermute | solution.py:34
  13.0 2.7 %collective-permute-start.8 = (bf16[64,2048]{1,0:T(8,128)(2,1)S(1)}, bf16[64,2048]{1,0:T(8,128)(2,1)S(1)}, u32[]{:S(2)}, u32[]{:S(2)}) collective-permute-start(bf16[64,2048]{1,0:T(8,128)(2,1)S(1)} %collective-permute-done.1.h1u_ref), channel_id=1, source_target_pairs={{1,0},{2,1},{3,2},{0,3},{5,4},{6,5},{7,6},{4,7},{9,8},{10,9},{11,1... | collective-permute-start | bytes 786440 | tf_op jit(solution)/shard_map/ppermute | solution.py:34
  17.0 2.4 %own.1 = (f32[128,256]{1,0:T(8,128)S(1)}, f32[128,512]{1,0:T(8,128)S(1)}, bf16[128,896]{1,0:T(8,128)(2,1)S(1)}) custom-call(bf16[2048,512]{1,0:T(8,128)(2,1)} %wq_ref.3, bf16[2048,128]{1,0:T(8,128)(2,1)} %wk_ref.5, bf16[2048,128]{1,0:T(8,128)(2,1)} %wv_ref.5, bf16[80,2048]{1,0:T(8,128)(2,1)S(1)} %get-tuple-element.45.upper_ref, ...), custom_call_target="tpu_custom_call" | custom-call | flops 402653184 | bytes 4194304 | tf_op jit(solution)/shard_map/own/pallas_call | solution.py:41
  20.1 1.9 %collective-permute-done.5.x3u_ref = bf16[80,2048]{1,0:T(8,128)(2,1)S(1)} collective-permute-done((bf16[80,2048]{1,0:T(8,128)(2,1)S(1)}, bf16[80,2048]{1,0:T(8,128)(2,1)S(1)}, u32[]{:S(2)}, u32[]{:S(2)}) %collective-permute-start.5) | collective-permute-done | bytes 327712 | tf_op jit(solution)/shard_map/ppermute | solution.py:34
  22.1 1.9 %near.1 = (bf16[256,2048]{1,0:T(8,128)(2,1)S(1)}, f32[256,256]{1,0:T(8,128)S(1)}, bf16[256,384]{1,0:T(8,128)(2,1)S(1)}) custom-call(bf16[2048,128]{1,0:T(8,128)(2,1)} %wk_ref.5, bf16[2048,128]{1,0:T(8,128)(2,1)} %wv_ref.5, f32[1,2048]{1,0:T(1,128)S(1)} %bitcast.7, bf16[64,2048]{1,0:T(8,128)(2,1)S(1)} %collective-permute-done.1.h1u_ref, ...), custom_call_target="tpu_custom_call" | custom-call | flops 268435456 | bytes 4194304 | tf_op jit(solution)/shard_map/near/pallas_call | solution.py:41
  24.6 3.0 %collective-permute-done.7.power_ref = f32[8,128]{1,0:T(8,128)S(1)} collective-permute-done((f32[8,128]{1,0:T(8,128)S(1)}, f32[8,128]{1,0:T(8,128)S(1)}, u32[]{:S(2)}, u32[]{:S(2)}) %collective-permute-start.7) | collective-permute-done | bytes 4128 | tf_op jit(solution)/shard_map/ppermute | solution.py:34
  27.7 1.7 %far.1 = (bf16[128,2048]{1,0:T(8,128)(2,1)S(1)}, f32[128,256]{1,0:T(8,128)S(1)}, bf16[128,384]{1,0:T(8,128)(2,1)S(1)}) custom-call(bf16[2048,128]{1,0:T(8,128)(2,1)} %wk_ref.5, bf16[2048,128]{1,0:T(8,128)(2,1)} %wv_ref.5, f32[1,2048]{1,0:T(1,128)S(1)} %bitcast.8, f32[8,128]{1,0:T(8,128)S(1)} %collective-permute-done.7.power_ref, ...), custom_call_target="tpu_custom_call" | custom-call | flops 134217728 | bytes 4194304 | tf_op jit(solution)/shard_map/far/pallas_call | solution.py:41
  30.5 1.8 %q.1 = (f32[384,512]{1,0:T(8,128)S(1)}, bf16[384,512]{1,0:T(8,128)(2,1)}) custom-call(bf16[256,2048]{1,0:T(8,128)(2,1)S(1)} %get-tuple-element.54.xa_ref, bf16[128,2048]{1,0:T(8,128)(2,1)S(1)} %get-tuple-element.55.xb_ref, bf16[2048,512]{1,0:T(8,128)(2,1)S(1)} %copy-done.1), custom_call_target="tpu_custom_call" | custom-call | flops 805306368 | bytes 4194304 | tf_op jit(solution)/shard_map/q/pallas_call | solution.py:41
  32.3 3.5 %collective-permute-done.10.gotb_ref = bf16[128,384]{1,0:T(8,128)(2,1)S(1)} collective-permute-done((bf16[128,384]{1,0:T(8,128)(2,1)S(1)}, bf16[128,384]{1,0:T(8,128)(2,1)S(1)}, u32[]{:S(2)}, u32[]{:S(2)}) %collective-permute-start.10) | collective-permute-done | bytes 98336 | tf_op jit(solution)/shard_map/ppermute | solution.py:34
  38.2 6.5 %collective-permute-start.18 = (bf16[512,256]{1,0:T(8,128)(2,1)S(1)}, bf16[512,256]{1,0:T(8,128)(2,1)}, u32[]{:S(2)}, u32[]{:S(2)}) collective-permute-start(bf16[512,256]{1,0:T(8,128)(2,1)S(1)} %rotary_kv.1.x_ref.own_ref), channel_id=1, source_target_pairs={{0,8},{8,16},{16,24},{24,32},{32,40},{40,48},{48,56},{56,64},{64,7... | collective-permute-start | bytes 786440 | tf_op jit(solution)/shard_map/ppermute | solution.py:394
  47.9 5.4 %collective-permute-done.18.prev_ref = bf16[512,256]{1,0:T(8,128)(2,1)} collective-permute-done((bf16[512,256]{1,0:T(8,128)(2,1)S(1)}, bf16[512,256]{1,0:T(8,128)(2,1)}, u32[]{:S(2)}, u32[]{:S(2)}) %collective-permute-start.18) | collective-permute-done | bytes 262176 | tf_op jit(solution)/shard_map/ppermute | solution.py:394
  53.4 3.7 %local.1 = (f32[4,512,128]{2,1,0:T(8,128)S(1)}, f32[4,512,128]{2,1,0:T(8,128)S(1)}, f32[4,512,128]{2,1,0:T(8,128)S(1)}) custom-call(s32[2]{0:T(128)S(1)} %pad_add_fusion.idx_ref, s32[64,1]{1,0:T(8,128)S(1)} %copy.10.len_ref, bf16[512,512]{1,0:T(8,128)(2,1)S(1)} %rotary_q.1.q_ref, bf16[512,256]{1,0:T(8,128)(2,1)S(1)} %rotary_kv.1.x_ref.own_ref, ...), custom_call_target="tpu_custom_call" | custom-call | flops 671088640 | bytes 4194304 | tf_op jit(solution)/shard_map/local/pallas_call | solution.py:41
  58.5 6.7 %collective-permute-done.19.other_ref = bf16[512,256]{1,0:T(8,128)(2,1)S(1)} collective-permute-done((bf16[512,256]{1,0:T(8,128)(2,1)S(1)}, bf16[512,256]{1,0:T(8,128)(2,1)S(1)}, u32[]{:S(2)}, u32[]{:S(2)}) %collective-permute-start.19) | collective-permute-done | bytes 262176 | tf_op jit(solution)/shard_map/ppermute | solution.py:403
  65.2 1.9 %prefix.5 = (bf16[128,1024]{1,0:T(8,128)(2,1)S(1)}, bf16[128,1024]{1,0:T(8,128)(2,1)S(1)}) custom-call(s32[2]{0:T(128)S(1)} %pad_add_fusion.idx_ref, s32[64,1]{1,0:T(8,128)S(1)} %copy.10.len_ref, f32[4,512,128]{2,1,0:T(8,128)S(1)} %get-tuple-element.63.acc_ref, f32[4,512,128]{2,1,0:T(8,128)S(1)} %get-tuple-element.64.max_ref, ...), custom_call_target="tpu_custom_call" | custom-call | flops 402653184 | bytes 4194304 | tf_op jit(solution)/shard_map/prefix/pallas_call | solution.py:41
  67.1 1.7 %collective-permute-start.24 = (bf16[128,1024]{1,0:T(8,128)(2,1)S(1)}, bf16[128,1024]{1,0:T(8,128)(2,1)S(1)}, u32[]{:S(2)}, u32[]{:S(2)}) collective-permute-start(bf16[128,1024]{1,0:T(8,128)(2,1)S(1)} %get-tuple-element.76), channel_id=1, source_target_pairs={{1,0},{2,1},{3,2},{0,3},{5,4},{6,5},{7,6},{4,7},{9,8},{10,9},{11,1... | collective-permute-start | bytes 786440 | tf_op jit(solution)/shard_map/ppermute | solution.py:34
  68.8 2.6 %prefix.4 = (f32[128,1024]{1,0:T(8,128)S(1)}, bf16[128,1024]{1,0:T(8,128)(2,1)S(1)}, bf16[128,1024]{1,0:T(8,128)(2,1)S(1)}, f32[128,1024]{1,0:T(8,128)S(1)}) custom-call(s32[2]{0:T(128)S(1)} %pad_add_fusion.idx_ref, s32[64,1]{1,0:T(8,128)S(1)} %copy.10.len_ref, f32[4,512,128]{2,1,0:T(8,128)S(1)} %get-tuple-element.63.acc_ref, ...), custom_call_target="tpu_custom_call" | custom-call | flops 805306368 | bytes 4194304 | tf_op jit(solution)/shard_map/prefix/pallas_call | solution.py:41
  71.4 2.8 %collective-permute-start.22 = (bf16[128,1024]{1,0:T(8,128)(2,1)S(1)}, bf16[128,1024]{1,0:T(8,128)(2,1)S(1)}, u32[]{:S(2)}, u32[]{:S(2)}) collective-permute-start(bf16[128,1024]{1,0:T(8,128)(2,1)S(1)} %get-tuple-element.72), channel_id=1, source_target_pairs={{1,0},{2,1},{3,2},{0,3},{5,4},{6,5},{7,6},{4,7},{9,8},{10,9},{11,1... | collective-permute-start | bytes 786440 | tf_op jit(solution)/shard_map/ppermute | solution.py:34
  75.0 2.9 %collective-permute-start.25 = (bf16[128,1024]{1,0:T(8,128)(2,1)S(1)}, bf16[128,1024]{1,0:T(8,128)(2,1)S(1)}, u32[]{:S(2)}, u32[]{:S(2)}) collective-permute-start(bf16[128,1024]{1,0:T(8,128)(2,1)S(1)} %add_convert_fusion), channel_id=1, source_target_pairs={{1,0},{2,1},{3,2},{0,3},{5,4},{6,5},{7,6},{4,7},{9,8},{10,9},{11,1... | collective-permute-start | bytes 786440 | tf_op jit(solution)/shard_map/ppermute | solution.py:34
  78.1 1.9 %prefix.3 = (f32[128,1024]{1,0:T(8,128)S(1)}, f32[128,1024]{1,0:T(8,128)S(1)}) custom-call(s32[2]{0:T(128)S(1)} %pad_add_fusion.idx_ref, s32[64,1]{1,0:T(8,128)S(1)} %copy.10.len_ref, f32[4,512,128]{2,1,0:T(8,128)S(1)} %get-tuple-element.63.acc_ref, f32[4,512,128]{2,1,0:T(8,128)S(1)} %get-tuple-element.64.max_ref, ...), custom_call_target="tpu_custom_call" | custom-call | flops 402653184 | bytes 4194304 | tf_op jit(solution)/shard_map/prefix/pallas_call | solution.py:41
  80.6 2.1 %collective-permute-done.23.refs_4_ = bf16[128,1024]{1,0:T(8,128)(2,1)S(1)} collective-permute-done((bf16[128,1024]{1,0:T(8,128)(2,1)S(1)}, bf16[128,1024]{1,0:T(8,128)(2,1)S(1)}, u32[]{:S(2)}, u32[]{:S(2)}) %collective-permute-start.23) | collective-permute-done | bytes 262176 | tf_op jit(solution)/shard_map/ppermute | solution.py:34
  82.7 3.5 %collective-permute-done.25.refs_5_ = bf16[128,1024]{1,0:T(8,128)(2,1)S(1)} collective-permute-done((bf16[128,1024]{1,0:T(8,128)(2,1)S(1)}, bf16[128,1024]{1,0:T(8,128)(2,1)S(1)}, u32[]{:S(2)}, u32[]{:S(2)}) %collective-permute-start.25) | collective-permute-done | bytes 262176 | tf_op jit(solution)/shard_map/ppermute | solution.py:34
  86.2 2.1 %collective-permute-done.21.refs_1_ = bf16[128,1024]{1,0:T(8,128)(2,1)S(1)} collective-permute-done((bf16[128,1024]{1,0:T(8,128)(2,1)S(1)}, bf16[128,1024]{1,0:T(8,128)(2,1)S(1)}, u32[]{:S(2)}, u32[]{:S(2)}) %collective-permute-start.21) | collective-permute-done | bytes 262176 | tf_op jit(solution)/shard_map/ppermute | solution.py:34
  (64 shorter events, 17.3 us)
Async XLA Ops:
  5.1 7.9 %collective-permute-start.1 = (bf16[64,2048]{1,0:T(8,128)(2,1)S(1)}, bf16[64,2048]{1,0:T(8,128)(2,1)S(1)}, u32[]{:S(2)}, u32[]{:S(2)}) collective-permute-start(bf16[64,2048]{1,0:T(8,128)(2,1)S(1)} %get-tuple-element.43), channel_id=1, source_target_pairs={{1,0},{2,1},{3,2},{0,3},{5,4},{6,5},{7,6},{4,7},{9,8},{10,9},{11,1... | collective-permute-start | bytes 786440 | tf_op jit(solution)/shard_map/ppermute | solution.py:34
  7.6 8.1 %collective-permute-start.2 = (bf16[64,2048]{1,0:T(8,128)(2,1)S(1)}, bf16[64,2048]{1,0:T(8,128)(2,1)S(1)}, u32[]{:S(2)}, u32[]{:S(2)}) collective-permute-start(bf16[64,2048]{1,0:T(8,128)(2,1)S(1)} %get-tuple-element.44), channel_id=1, source_target_pairs={{3,0},{0,1},{1,2},{2,3},{7,4},{4,5},{5,6},{6,7},{11,8},{8,9},{9,10... | collective-permute-start | bytes 786440 | tf_op jit(solution)/shard_map/ppermute | solution.py:34
  10.2 9.3 %collective-permute-start.4 = (bf16[80,2048]{1,0:T(8,128)(2,1)S(1)}, bf16[80,2048]{1,0:T(8,128)(2,1)S(1)}, u32[]{:S(2)}, u32[]{:S(2)}) collective-permute-start(bf16[80,2048]{1,0:T(8,128)(2,1)S(1)} %get-tuple-element.46.lower_ref), channel_id=1, source_target_pairs={{1,0},{2,1},{3,2},{0,3},{5,4},{6,5},{7,6},{4,7},{9,8},{10,9},{11,1... | collective-permute-start | bytes 983048 | tf_op jit(solution)/shard_map/ppermute | solution.py:34
  12.9 9.2 %collective-permute-start.5 = (bf16[80,2048]{1,0:T(8,128)(2,1)S(1)}, bf16[80,2048]{1,0:T(8,128)(2,1)S(1)}, u32[]{:S(2)}, u32[]{:S(2)}) collective-permute-start(bf16[80,2048]{1,0:T(8,128)(2,1)S(1)} %get-tuple-element.45.upper_ref), channel_id=1, source_target_pairs={{3,0},{0,1},{1,2},{2,3},{7,4},{4,5},{5,6},{6,7},{11,8},{8,9},{9,10... | collective-permute-start | bytes 983048 | tf_op jit(solution)/shard_map/ppermute | solution.py:34
  13.0 14.6 %collective-permute-start.8 = (bf16[64,2048]{1,0:T(8,128)(2,1)S(1)}, bf16[64,2048]{1,0:T(8,128)(2,1)S(1)}, u32[]{:S(2)}, u32[]{:S(2)}) collective-permute-start(bf16[64,2048]{1,0:T(8,128)(2,1)S(1)} %collective-permute-done.1.h1u_ref), channel_id=1, source_target_pairs={{1,0},{2,1},{3,2},{0,3},{5,4},{6,5},{7,6},{4,7},{9,8},{10,9},{11,1... | collective-permute-start | bytes 786440 | tf_op jit(solution)/shard_map/ppermute | solution.py:34
  15.7 12.0 %collective-permute-start.9 = (bf16[64,2048]{1,0:T(8,128)(2,1)S(1)}, bf16[64,2048]{1,0:T(8,128)(2,1)S(1)}, u32[]{:S(2)}, u32[]{:S(2)}) collective-permute-start(bf16[64,2048]{1,0:T(8,128)(2,1)S(1)} %collective-permute-done.2.h3l_ref), channel_id=1, source_target_pairs={{3,0},{0,1},{1,2},{2,3},{7,4},{4,5},{5,6},{6,7},{11,8},{8,9},{9,10... | collective-permute-start | bytes 786440 | tf_op jit(solution)/shard_map/ppermute | solution.py:34
  15.8 11.8 %collective-permute-start.7 = (f32[8,128]{1,0:T(8,128)S(1)}, f32[8,128]{1,0:T(8,128)S(1)}, u32[]{:S(2)}, u32[]{:S(2)}) collective-permute-start(f32[8,128]{1,0:T(8,128)S(1)} %get-tuple-element.51), channel_id=1, source_target_pairs={{2,0},{3,1},{0,2},{1,3},{6,4},{7,5},{4,6},{5,7},{10,8},{11,9},{8,1... | collective-permute-start | bytes 12296 | tf_op jit(solution)/shard_map/ppermute | solution.py:34
  19.5 16.3 %collective-permute-start.3 = (bf16[128,896]{1,0:T(8,128)(2,1)S(1)}, bf16[128,896]{1,0:T(8,128)(2,1)S(1)}, u32[]{:S(2)}, u32[]{:S(2)}) collective-permute-start(bf16[128,896]{1,0:T(8,128)(2,1)S(1)} %get-tuple-element.48), channel_id=1, source_target_pairs={{4,0},{0,4},{5,1},{1,5},{6,2},{2,6},{7,3},{3,7},{12,8},{8,12},{13,... | collective-permute-start | bytes 688136 | tf_op jit(solution)/shard_map/ppermute | solution.py:34
  24.0 11.7 %collective-permute-start.6 = (bf16[256,384]{1,0:T(8,128)(2,1)S(1)}, bf16[256,384]{1,0:T(8,128)(2,1)S(1)}, u32[]{:S(2)}, u32[]{:S(2)}) collective-permute-start(bf16[256,384]{1,0:T(8,128)(2,1)S(1)} %get-tuple-element.50), channel_id=1, source_target_pairs={{4,0},{0,4},{5,1},{1,5},{6,2},{2,6},{7,3},{3,7},{12,8},{8,12},{13,... | collective-permute-start | bytes 589832 | tf_op jit(solution)/shard_map/ppermute | solution.py:34
  35.9 8.9 %collective-permute-start.11 = (bf16[512,256]{1,0:T(8,128)(2,1)S(1)}, bf16[512,256]{1,0:T(8,128)(2,1)S(1)}, u32[]{:S(2)}, u32[]{:S(2)}) collective-permute-start(bf16[512,256]{1,0:T(8,128)(2,1)S(1)} %rotary_kv.1.x_ref.own_ref), channel_id=1, source_target_pairs={{0,32},{1,33},{2,34},{3,35},{4,36},{5,37},{6,38},{7,39}} | collective-permute-start | bytes 786440 | tf_op jit(solution)/shard_map/ppermute | solution.py:324
  36.8 8.0 %collective-permute-start.12 = (bf16[512,256]{1,0:T(8,128)(2,1)S(1)}, bf16[512,256]{1,0:T(8,128)(2,1)S(1)}, u32[]{:S(2)}, u32[]{:S(2)}) collective-permute-start(bf16[512,256]{1,0:T(8,128)(2,1)S(1)} %rotary_kv.1.x_ref.own_ref), channel_id=1, source_target_pairs={{0,224},{1,225},{2,226},{3,227},{4,228},{5,229},{6,230},{7,231}} | collective-permute-start | bytes 786440 | tf_op jit(solution)/shard_map/ppermute | solution.py:324
  37.4 7.3 %collective-permute-start.13 = (bf16[512,256]{1,0:T(8,128)(2,1)S(1)}, bf16[512,256]{1,0:T(8,128)(2,1)S(1)}, u32[]{:S(2)}, u32[]{:S(2)}) collective-permute-start(bf16[512,256]{1,0:T(8,128)(2,1)S(1)} %rotary_kv.1.x_ref.own_ref), channel_id=1, source_target_pairs={{0,128},{1,129},{2,130},{3,131},{4,132},{5,133},{6,134},{7,135}} | collective-permute-start | bytes 786440 | tf_op jit(solution)/shard_map/ppermute | solution.py:324
  38.1 9.4 %collective-permute-start.17 = (bf16[384,512]{1,0:T(8,128)(2,1)}, bf16[384,512]{1,0:T(8,128)(2,1)S(1)}, u32[]{:S(2)}, u32[]{:S(2)}) collective-permute-start(bf16[384,512]{1,0:T(8,128)(2,1)} %get-tuple-element.56), channel_id=1, source_target_pairs={{4,0},{0,4},{5,1},{1,5},{6,2},{2,6},{7,3},{3,7},{12,8},{8,12},{13,... | collective-permute-start | bytes 1179656 | tf_op jit(solution)/shard_map/ppermute | solution.py:34
  38.2 15.1 %collective-permute-start.18 = (bf16[512,256]{1,0:T(8,128)(2,1)S(1)}, bf16[512,256]{1,0:T(8,128)(2,1)}, u32[]{:S(2)}, u32[]{:S(2)}) collective-permute-start(bf16[512,256]{1,0:T(8,128)(2,1)S(1)} %rotary_kv.1.x_ref.own_ref), channel_id=1, source_target_pairs={{0,8},{8,16},{16,24},{24,32},{32,40},{40,48},{48,56},{56,64},{64,7... | collective-permute-start | bytes 786440 | tf_op jit(solution)/shard_map/ppermute | solution.py:394
  45.4 11.7 %collective-permute-start.14 = (bf16[512,256]{1,0:T(8,128)(2,1)S(1)}, bf16[512,256]{1,0:T(8,128)(2,1)S(1)}, u32[]{:S(2)}, u32[]{:S(2)}) collective-permute-start(bf16[512,256]{1,0:T(8,128)(2,1)S(1)} %first.1.x_ref), channel_id=1, source_target_pairs={{32,64},{224,192},{128,96},{0,176},{33,65},{225,193},{129,97},{1,1... | collective-permute-start | bytes 786440 | tf_op jit(solution)/shard_map/ppermute | solution.py:327
  46.1 11.0 %collective-permute-start.15 = (bf16[512,256]{1,0:T(8,128)(2,1)S(1)}, bf16[512,256]{1,0:T(8,128)(2,1)S(1)}, u32[]{:S(2)}, u32[]{:S(2)}) collective-permute-start(bf16[512,256]{1,0:T(8,128)(2,1)S(1)} %first.1.x_ref), channel_id=1, source_target_pairs={{32,80},{224,208},{128,160},{0,112},{33,81},{225,209},{129,161},{1... | collective-permute-start | bytes 786440 | tf_op jit(solution)/shard_map/ppermute | solution.py:327
  46.8 10.4 %collective-permute-start.16 = (bf16[512,256]{1,0:T(8,128)(2,1)S(1)}, bf16[512,256]{1,0:T(8,128)(2,1)S(1)}, u32[]{:S(2)}, u32[]{:S(2)}) collective-permute-start(bf16[512,256]{1,0:T(8,128)(2,1)S(1)} %first.1.x_ref), channel_id=1, source_target_pairs={{32,48},{224,240},{128,144},{0,16},{33,49},{225,241},{129,145},{1,... | collective-permute-start | bytes 786440 | tf_op jit(solution)/shard_map/ppermute | solution.py:327
  57.2 8.0 %collective-permute-start.19 = (bf16[512,256]{1,0:T(8,128)(2,1)S(1)}, bf16[512,256]{1,0:T(8,128)(2,1)S(1)}, u32[]{:S(2)}, u32[]{:S(2)}) collective-permute-start(bf16[512,256]{1,0:T(8,128)(2,1)S(1)} %second.1.pre_ref), channel_id=1, source_target_pairs={{0,8},{16,24},{32,40},{48,56},{64,72},{80,88},{96,104},{112,120},{... | collective-permute-start | bytes 786440 | tf_op jit(solution)/shard_map/ppermute | solution.py:403
  67.1 7.8 %collective-permute-start.24 = (bf16[128,1024]{1,0:T(8,128)(2,1)S(1)}, bf16[128,1024]{1,0:T(8,128)(2,1)S(1)}, u32[]{:S(2)}, u32[]{:S(2)}) collective-permute-start(bf16[128,1024]{1,0:T(8,128)(2,1)S(1)} %get-tuple-element.76), channel_id=1, source_target_pairs={{1,0},{2,1},{3,2},{0,3},{5,4},{6,5},{7,6},{4,7},{9,8},{10,9},{11,1... | collective-permute-start | bytes 786440 | tf_op jit(solution)/shard_map/ppermute | solution.py:34
  68.8 9.1 %collective-permute-start.20 = (bf16[128,1024]{1,0:T(8,128)(2,1)S(1)}, bf16[128,1024]{1,0:T(8,128)(2,1)S(1)}, u32[]{:S(2)}, u32[]{:S(2)}) collective-permute-start(bf16[128,1024]{1,0:T(8,128)(2,1)S(1)} %get-tuple-element.71), channel_id=1, source_target_pairs={{3,0},{0,1},{1,2},{2,3},{7,4},{4,5},{5,6},{6,7},{11,8},{8,9},{9,10... | collective-permute-start | bytes 786440 | tf_op jit(solution)/shard_map/ppermute | solution.py:34
  71.4 9.1 %collective-permute-start.22 = (bf16[128,1024]{1,0:T(8,128)(2,1)S(1)}, bf16[128,1024]{1,0:T(8,128)(2,1)S(1)}, u32[]{:S(2)}, u32[]{:S(2)}) collective-permute-start(bf16[128,1024]{1,0:T(8,128)(2,1)S(1)} %get-tuple-element.72), channel_id=1, source_target_pairs={{1,0},{2,1},{3,2},{0,3},{5,4},{6,5},{7,6},{4,7},{9,8},{10,9},{11,1... | collective-permute-start | bytes 786440 | tf_op jit(solution)/shard_map/ppermute | solution.py:34
  74.2 8.5 %collective-permute-start.23 = (bf16[128,1024]{1,0:T(8,128)(2,1)S(1)}, bf16[128,1024]{1,0:T(8,128)(2,1)S(1)}, u32[]{:S(2)}, u32[]{:S(2)}) collective-permute-start(bf16[128,1024]{1,0:T(8,128)(2,1)S(1)} %get-tuple-element.74), channel_id=1, source_target_pairs={{3,0},{0,1},{1,2},{2,3},{7,4},{4,5},{5,6},{6,7},{11,8},{8,9},{9,10... | collective-permute-start | bytes 786440 | tf_op jit(solution)/shard_map/ppermute | solution.py:34
  75.0 11.2 %collective-permute-start.25 = (bf16[128,1024]{1,0:T(8,128)(2,1)S(1)}, bf16[128,1024]{1,0:T(8,128)(2,1)S(1)}, u32[]{:S(2)}, u32[]{:S(2)}) collective-permute-start(bf16[128,1024]{1,0:T(8,128)(2,1)S(1)} %add_convert_fusion), channel_id=1, source_target_pairs={{1,0},{2,1},{3,2},{0,3},{5,4},{6,5},{7,6},{4,7},{9,8},{10,9},{11,1... | collective-permute-start | bytes 786440 | tf_op jit(solution)/shard_map/ppermute | solution.py:34
  78.0 10.3 %collective-permute-start.21 = (bf16[128,1024]{1,0:T(8,128)(2,1)S(1)}, bf16[128,1024]{1,0:T(8,128)(2,1)S(1)}, u32[]{:S(2)}, u32[]{:S(2)}) collective-permute-start(bf16[128,1024]{1,0:T(8,128)(2,1)S(1)} %add_convert_fusion.1), channel_id=1, source_target_pairs={{3,0},{0,1},{1,2},{2,3},{7,4},{4,5},{5,6},{6,7},{11,8},{8,9},{9,10... | collective-permute-start | bytes 786440 | tf_op jit(solution)/shard_map/ppermute | solution.py:34
  (8 other events, 80.9 us)
